TPU v7x, 128 devices: a whole 4x4x4 slice. The times are simulated.
128 devices in a mesh: dp: 16 (over x, z), tensor: 8 (over y, core).
Axes of the slice: x: 4, y: 4, z: 4, core: 2. Of those that a mesh axis runs over, the one named last changes fastest.
Arguments:
- activations: bfloat16 [4, 16384, 4096], P(None, 'dp', 'tensor'), may hold values from -6 to 6
- out_grads: bfloat16 [4, 16384, 14336], P(None, 'dp', 'tensor'), may hold values from -6 to 6
- proj_input: bfloat16 [4, 64, 4096], P(None, None, 'tensor'), may hold values from -0.09375 to 0.09375
- proj_output: bfloat16 [4, 64, 14336], P(None, None, 'tensor'), may hold values from -0.046875 to 0.046875
- query_feats: bfloat16 [4, 512, 4096], P(None, 'tensor', 'dp'), may hold values from -6 to 6
Outputs:
- scores: float32 [16384, 512], P('dp', 'tensor')
All inputs are finite; a program needn't handle non-finite values.
Results may differ from a plain program's by a relative error of at most 0.0029.
Values may be sent and summed in bfloat16 or wider, within the bound.
No kernel may reach another device: no remote copies, remote signals or barrier semaphores. Data moves between devices by JAX's collectives and lax.ppermute only.
A program may use at most 192 MiB of HBM per device.

v0:
```python
import jax
import jax.numpy as jnp
from jax import lax
from jax.sharding import PartitionSpec as P


def project(acts, grads, p_in, p_out):
    in_part = jnp.einsum("td,rd->tr", acts, p_in, preferred_element_type=jnp.float32)
    out_part = jnp.einsum("tf,rf->tr", grads, p_out, preferred_element_type=jnp.float32)
    return (in_part, out_part)


def kron_rows(in_proj, out_proj):
    rows = in_proj.shape[-2]
    width = in_proj.shape[-1]
    lead = in_proj.shape[:-2]
    outer = in_proj[..., :, :, None] * out_proj[..., :, None, :]
    return outer.reshape(lead + (rows, width * width)).astype(jnp.bfloat16)


def local(activations, out_grads, proj_input, proj_output, query_feats):
    layers = activations.shape[0]
    tok_rows = activations.shape[1]
    width = proj_input.shape[1]
    scale = (layers * width * width) ** (-0.5)
    feat_list = []
    for layer in range(layers):
        in_part, out_part = project(
            activations[layer], out_grads[layer], proj_input[layer], proj_output[layer]
        )
        summed_in, summed_out = lax.psum((in_part, out_part), "tensor")
        feat_list.append(kron_rows(summed_in, summed_out))
    start = jnp.zeros((tok_rows, query_feats.shape[1]), jnp.float32)
    total = start
    for layer in range(layers):
        feats = feat_list[layer]

        def score_one(carry, piece, first, feats=feats):
            return carry + jnp.einsum("tk,qk->tq", feats, piece, preferred_element_type=jnp.float32)

        total = score_one(
            total, lax.all_gather(query_feats[layer], "dp", axis=1, tiled=True), jnp.int32(0)
        )
    return total * scale


def solution(mesh):
    in_specs = (
        P(None, "dp", "tensor"),
        P(None, "dp", "tensor"),
        P(None, None, "tensor"),
        P(None, None, "tensor"),
        P(None, "tensor", "dp"),
    )
    out_specs = P("dp", "tensor")
    return jax.shard_map(local, mesh=mesh, in_specs=in_specs, out_specs=out_specs, check_vma=False)
```

profile of v0, /device:TPU:24, one launch (start us, length us, event | category | flops | bytes accessed | tf_op | source)
XLA Modules:
  0.0 156.2 jit_solution(13924424514426243147)
XLA Ops:
  6.5 0.0 all-reduce.3.cloned.1.call-start
  6.5 2.5 %fusion.13 = f32[1024,64]{0,1:T(8,128)} fusion(bf16[4,1024,512]{2,1,0:T(8,128)(2,1)} %param.5, bf16[4,64,512]{2,1,0:T(8,128)(2,1)} %param.7), kind=kOutput, calls=%fused_computation.20 | convolution fusion | flops 67108864 | bytes 1376256 | tf_op jit(solution)/shard_map/td,rd->tr/dot_general | solution.py:8
  9.1 3.1 %fusion.15 = f32[1024,64]{0,1:T(8,128)} fusion(bf16[4,1024,512]{2,1,0:T(8,128)(2,1)} %param.5, bf16[4,64,512]{2,1,0:T(8,128)(2,1)} %param.7), kind=kOutput, calls=%fused_computation.22 | convolution fusion | flops 67108864 | bytes 1376256 | tf_op jit(solution)/shard_map/td,rd->tr/dot_general | solution.py:8
  12.2 2.4 %fusion.17 = f32[1024,64]{0,1:T(8,128)} fusion(bf16[4,1024,512]{2,1,0:T(8,128)(2,1)} %param.5, bf16[4,64,512]{2,1,0:T(8,128)(2,1)} %param.7), kind=kOutput, calls=%fused_computation.24 | convolution fusion | flops 67108864 | bytes 1376256 | tf_op jit(solution)/shard_map/td,rd->tr/dot_general | solution.py:8
  14.6 2.4 %fusion.19 = f32[1024,64]{0,1:T(8,128)} fusion(bf16[4,1024,512]{2,1,0:T(8,128)(2,1)} %param.5, bf16[4,64,512]{2,1,0:T(8,128)(2,1)} %param.7), kind=kOutput, calls=%fused_computation.26 | convolution fusion | flops 67108864 | bytes 1376256 | tf_op jit(solution)/shard_map/td,rd->tr/dot_general | solution.py:8
  16.9 4.0 %fusion = f32[1024,64]{0,1:T(8,128)} fusion(bf16[4,1024,1792]{2,1,0:T(8,128)(2,1)} %param.6, bf16[4,64,1792]{2,1,0:T(8,128)(2,1)} %param.8), kind=kOutput, calls=%fused_computation.4 | convolution fusion | flops 234881024 | bytes 4161536 | tf_op jit(solution)/shard_map/tf,rf->tr/dot_general | solution.py:9
  21.0 0.0 copy-done.6
  21.0 2.9 %fusion.2 = f32[1024,64]{0,1:T(8,128)} fusion(bf16[4,1024,1792]{2,1,0:T(8,128)(2,1)S(1)} %copy-done.6, bf16[4,64,1792]{2,1,0:T(8,128)(2,1)} %param.8), kind=kOutput, calls=%fused_computation.6 | convolution fusion | flops 234881024 | bytes 4161536 | tf_op jit(solution)/shard_map/tf,rf->tr/dot_general | solution.py:9
  23.9 0.0 copy-done.7
  23.9 1.9 %fusion.4 = f32[1024,64]{0,1:T(8,128)} fusion(bf16[4,1024,1792]{2,1,0:T(8,128)(2,1)S(1)} %copy-done.6, bf16[4,64,1792]{2,1,0:T(8,128)(2,1)S(1)} %copy-done.7), kind=kOutput, calls=%fused_computation.8 | convolution fusion | flops 234881024 | bytes 4161536 | tf_op jit(solution)/shard_map/tf,rf->tr/dot_general | solution.py:9
  25.8 1.9 %fusion.6 = f32[1024,64]{0,1:T(8,128)} fusion(bf16[4,1024,1792]{2,1,0:T(8,128)(2,1)S(1)} %copy-done.6, bf16[4,64,1792]{2,1,0:T(8,128)(2,1)S(1)} %copy-done.7), kind=kOutput, calls=%fused_computation.10 | convolution fusion | flops 234881024 | bytes 4161536 | tf_op jit(solution)/shard_map/tf,rf->tr/dot_general | solution.py:9
  27.7 0.0 all-reduce.3.cloned.1.call-update
  27.8 0.0 copy-done.5
  27.8 26.1 %all-gather = bf16[1,64,4096]{2,1,0:T(8,128)(2,1)S(1)} all-gather(bf16[1,64,256]{2,1,0:T(8,128)(2,1)S(1)} %get-tuple-element.15), channel_id=2, replica_groups=mesh['dp'=16,'tensor'=8] {'dp'}, dimensions={2}, use_global_device_ids=true | all-gather | bytes 557056 | tf_op jit(solution)/shard_map/all_gather | solution.py:42
  53.9 23.7 %all-gather.1 = bf16[1,64,4096]{2,1,0:T(8,128)(2,1)S(1)} all-gather(bf16[1,64,256]{2,1,0:T(8,128)(2,1)S(1)} %get-tuple-element.14), channel_id=3, replica_groups=mesh['dp'=16,'tensor'=8] {'dp'}, dimensions={2}, use_global_device_ids=true | all-gather | bytes 557056 | tf_op jit(solution)/shard_map/all_gather | solution.py:42
  77.7 23.2 %all-gather.2 = bf16[1,64,4096]{2,1,0:T(8,128)(2,1)S(1)} all-gather(bf16[1,64,256]{2,1,0:T(8,128)(2,1)S(1)} %get-tuple-element.16), channel_id=4, replica_groups=mesh['dp'=16,'tensor'=8] {'dp'}, dimensions={2}, use_global_device_ids=true | all-gather | bytes 557056 | tf_op jit(solution)/shard_map/all_gather | solution.py:42
  100.9 23.7 %all-gather.3 = bf16[1,64,4096]{2,1,0:T(8,128)(2,1)S(1)} all-gather(bf16[1,64,256]{2,1,0:T(8,128)(2,1)S(1)} %get-tuple-element.13), channel_id=5, replica_groups=mesh['dp'=16,'tensor'=8] {'dp'}, dimensions={2}, use_global_device_ids=true | all-gather | bytes 557056 | tf_op jit(solution)/shard_map/all_gather | solution.py:42
  124.6 3.9 %multiply_convert_fusion.3 = bf16[1024,64,64]{0,2,1:T(8,128)(2,1)S(1)} fusion(f32[1024,64]{0,1:T(8,128)} %get-tuple-element.5, f32[1024,64]{0,1:T(8,128)} %get-tuple-element.6), kind=kLoop, calls=%fused_computation.3 | loop fusion | flops 8388608 | bytes 8912896 | tf_op jit(solution)/shard_map/convert_element_type | solution.py:18
  128.5 0.0 copy-start.3
  128.5 0.0 copy-start.4
  128.5 1.6 %fusion.28 = f32[1024,64]{0,1:T(8,128)S(1)} fusion(bf16[1024,4096]{0,1:T(8,128)(2,1)S(1)} %bitcast.73, bf16[1,64,4096]{2,1,0:T(8,128)(2,1)S(1)} %all-gather), kind=kOutput, calls=%fused_computation.35 | convolution fusion | flops 536870912 | bytes 9175040 | tf_op jit(solution)/shard_map/tk,qk->tq/dot_general | solution.py:39
  130.1 0.0 copy-start.2
  130.2 2.9 %multiply_convert_fusion.2 = bf16[1024,64,64]{0,2,1:T(8,128)(2,1)S(1)} fusion(f32[1024,64]{0,1:T(8,128)S(1)} %copy-done.3, f32[1024,64]{0,1:T(8,128)S(1)} %copy-done.4), kind=kLoop, calls=%fused_computation.2 | loop fusion | flops 8388608 | bytes 8912896 | tf_op jit(solution)/shard_map/convert_element_type | solution.py:18
  133.1 0.0 copy-done.2
  133.1 3.8 %multiply_convert_fusion.1 = bf16[1024,64,64]{0,2,1:T(8,128)(2,1)S(1)} fusion(f32[1024,64]{0,1:T(8,128)S(1)} %copy-done.2, f32[1024,64]{0,1:T(8,128)} %get-tuple-element.10), kind=kLoop, calls=%fused_computation.1 | loop fusion | flops 8388608 | bytes 8912896 | tf_op jit(solution)/shard_map/convert_element_type | solution.py:18
  137.0 6.2 %multiply_convert_fusion = bf16[1024,64,64]{0,2,1:T(8,128)(2,1)} fusion(f32[1024,64]{0,1:T(8,128)S(1)} %copy-done, f32[1024,64]{0,1:T(8,128)S(1)} %copy-done.1), kind=kLoop, calls=%fused_computation | loop fusion | flops 8388608 | bytes 8912896 | tf_op jit(solution)/shard_map/convert_element_type | solution.py:18
  143.2 1.6 %convolution_add_fusion.2 = f32[1024,64]{0,1:T(8,128)S(1)} fusion(f32[1024,64]{0,1:T(8,128)S(1)} %fusion.28, bf16[1024,4096]{0,1:T(8,128)(2,1)S(1)} %bitcast.68, bf16[1,64,4096]{2,1,0:T(8,128)(2,1)S(1)} %all-gather.1), kind=kOutput, calls=%fused_computation.19 | convolution fusion | flops 536936448 | bytes 9437184 | tf_op jit(solution)/shard_map/tk,qk->tq/dot_general | solution.py:39
  144.8 0.0 slice-start.1
  144.8 1.6 %convolution_add_fusion.1 = f32[1024,64]{0,1:T(8,128)S(1)} fusion(f32[1024,64]{0,1:T(8,128)S(1)} %convolution_add_fusion.2, bf16[1024,4096]{0,1:T(8,128)(2,1)S(1)} %bitcast.69, bf16[1,64,4096]{2,1,0:T(8,128)(2,1)S(1)} %all-gather.2), kind=kOutput, calls=%fused_computation.18 | convolution fusion | flops 536936448 | bytes 9437184 | tf_op jit(solution)/shard_map/tk,qk->tq/dot_general | solution.py:39
  146.4 0.0 slice-done
  146.4 0.7 slice-done.1
  147.1 2.3 %fusion.12 = f32[1024,64]{0,1:T(8,128)} fusion(f32[1024,64]{0,1:T(8,128)S(1)} %convolution_add_fusion.1, bf16[1024,4096]{0,1:T(8,128)(2,1)S(1)} %bitcast.72, bf16[1,64,4096]{2,1,0:T(8,128)(2,1)S(1)} %all-gather.3), kind=kOutput, calls=%fused_computation.17 | convolution fusion | flops 537001984 | bytes 9437184 | tf_op jit(solution)/shard_map/tk,qk->tq/dot_general | solution.py:39
  (13 shorter events, 0.0 us)
Async XLA Ops:
  6.5 118.0 %all-reduce.3.cloned.1.call-start = ((), (), s32[]{:S(2)}) async-start(), calls=%async_computation | async-start | bytes 4194304 | tf_op jit(solution)/shard_map/psum | solution.py:31
  6.5 14.5 %copy-start.6 = (bf16[4,1024,1792]{2,1,0:T(8,128)(2,1)S(1)}, bf16[4,1024,1792]{2,1,0:T(8,128)(2,1)}, u32[]{:S(2)}) copy-start(bf16[4,1024,1792]{2,1,0:T(8,128)(2,1)} %param.6) | copy-start | bytes 44040196
  16.9 6.9 %copy-start.7 = (bf16[4,64,1792]{2,1,0:T(8,128)(2,1)S(1)}, bf16[4,64,1792]{2,1,0:T(8,128)(2,1)}, u32[]{:S(2)}) copy-start(bf16[4,64,1792]{2,1,0:T(8,128)(2,1)} %param.8) | copy-start | bytes 2752516
  23.9 3.9 %copy-start.5 = (bf16[4,64,256]{2,1,0:T(8,128)(2,1)S(1)}, bf16[4,64,256]{2,1,0:T(8,128)(2,1)}, u32[]{:S(2)}) copy-start(bf16[4,64,256]{2,1,0:T(8,128)(2,1)} %param.9) | copy-start | bytes 393220
  128.5 1.6 %copy-start.3 = (f32[1024,64]{0,1:T(8,128)S(1)}, f32[1024,64]{0,1:T(8,128)}, u32[]{:S(2)}) copy-start(f32[1024,64]{0,1:T(8,128)} %get-tuple-element.7) | copy-start | bytes 786436
  128.5 1.6 %copy-start.4 = (f32[1024,64]{0,1:T(8,128)S(1)}, f32[1024,64]{0,1:T(8,128)}, u32[]{:S(2)}) copy-start(f32[1024,64]{0,1:T(8,128)} %get-tuple-element.8) | copy-start | bytes 786436
  130.1 3.0 %copy-start.2 = (f32[1024,64]{0,1:T(8,128)S(1)}, f32[1024,64]{0,1:T(8,128)}, u32[]{:S(2)}) copy-start(f32[1024,64]{0,1:T(8,128)} %get-tuple-element.9) | copy-start | bytes 786436
  130.2 6.8 %copy-start = (f32[1024,64]{0,1:T(8,128)S(1)}, f32[1024,64]{0,1:T(8,128)}, u32[]{:S(2)}) copy-start(f32[1024,64]{0,1:T(8,128)} %get-tuple-element.11) | copy-start | bytes 786436
  130.2 6.8 %copy-start.1 = (f32[1024,64]{0,1:T(8,128)S(1)}, f32[1024,64]{0,1:T(8,128)}, u32[]{:S(2)}) copy-start(f32[1024,64]{0,1:T(8,128)} %get-tuple-element.12) | copy-start | bytes 786436
  143.2 3.2 %slice-start = ((s8[8388608]{0:T(1024)(128)(4,1)}), s8[4194304]{0:T(1024)(128)(4,1)S(1)}, s32[]{:S(2)}) async-start(s8[8388608]{0:T(1024)(128)(4,1)} %bitcast.70), calls=%async_computation.1 | async-start | bytes 8388608
  144.8 2.3 %slice-start.1 = ((s8[8388608]{0:T(1024)(128)(4,1)}), s8[4194304]{0:T(1024)(128)(4,1)S(1)}, s32[]{:S(2)}) async-start(s8[8388608]{0:T(1024)(128)(4,1)} %bitcast.70), calls=%async_computation.2 | async-start | bytes 8388608
Sparse Core Ops, SparseCore 0:
  27.9 65.9 all-reduce.2
where the time goes:
time: 157 us; the launch traced here: 156 us
  blocking collectives  96.8 us (62%)
  matrix products  28.2 us (18%)
  other arithmetic  16.9 us (11%)
  between operations  13.6 us (9%)
    all_gather x4, blocking collectives, local(): lax.all_gather(query_feats[layer], 'dp', axis=1, tiled=True)  96.8 us
    convert_element_type x4, other arithmetic, kron_rows(): return outer.reshape(lead + (rows, width * width)).astype(jnp.bfloat16)  16.9 us
    dot_general x4, matrix products, project(): jnp.einsum('tf,rf->tr', grads, p_out, preferred_element_type=jnp.float32)  10.8 us
    dot_general x4, matrix products, project(): jnp.einsum('td,rd->tr', acts, p_in, preferred_element_type=jnp.float32)  10.4 us
    dot_general x4, matrix products, score_one(): jnp.einsum('tk,qk->tq', feats, piece, preferred_element_type=jnp.float32)  7.05 us
  transfers between devices with their start and end apart: 1, of which 0 were waited for; matrix products, arithmetic and copies ran while one was open for 0% of the time, Pallas kernels for 0%

commit v1 on v0

v1 whole, which is shorter than its diff:
```python
import functools

import jax
import jax.numpy as jnp
from jax import lax
from jax.experimental import pallas as pl
from jax.experimental.pallas import tpu as pltpu
from jax.sharding import PartitionSpec as P

NT = (((1,), (1,)), ((), ()))
PROJECT_VMEM = 61 * 2**20
SCORE_VMEM = 24 * 2**20
RING = 4
WIDTH = 64
QTOK = 256
QUART = 4
ROWS = 2 * WIDTH + 8
TINY = 1e-30
TOP = 15.0


def swap_perm():
    return [(y * 2 + c, y * 2 + 1 - c) for y in range(RING) for c in range(2)]


def y_perm(d):
    return [(y * 2 + c, ((y + d) % RING) * 2 + c) for y in range(RING) for c in range(2)]


def xz_perm(d, flip):
    pairs = []
    for x in range(RING):
        for z in range(RING):
            for t in range(2 * RING):
                along_x = (t % 2 == 0) != flip
                sx, sz = ((x + d) % RING, z) if along_x else (x, (z + d) % RING)
                pairs.append(((sx * RING + sz) * 2 * RING + t, (x * RING + z) * 2 * RING + t))
    return pairs


def add_powers(per, out, j, s):
    for k in range(per):
        for h in range(2):
            most = jnp.max(jnp.abs(out[s * per + k, j, h * WIDTH : (h + 1) * WIDTH, :]), axis=0, keepdims=True)
            power = jnp.ceil(jnp.log2(jnp.maximum(most, TINY)))
            out[s * per + k, j, 2 * WIDTH + 4 * h : 2 * WIDTH + 4 * h + 4, :] = jnp.broadcast_to(power, (4, QTOK))


def project_kernel(chunk, slots, acts, grads, p_in, p_out, keep, give, av, gv, piv, pov, sem_a, sem_g, sem_p):
    t = lax.axis_index("tensor")
    y, core = t // 2, t % 2
    per = chunk // QTOK
    weights, steps = [], []
    order = ((give, 2 * (1 - core), 0), (give, 2 * (1 - core), 1), (keep, 2 * core, 0), (keep, 2 * core, 1))
    for w, (out, first, j) in enumerate(order):
        layer = first + j
        weights.append(
            (
                pltpu.make_async_copy(p_in.at[layer], piv.at[w], sem_p.at[2 * w]),
                pltpu.make_async_copy(p_out.at[layer], pov.at[w], sem_p.at[2 * w + 1]),
            )
        )
        for s in range(QUART // per):
            slot = len(steps) % slots
            group = []
            for k in range(per):
                rows = pl.ds(pl.multiple_of(lax.rem(y + s * per + k, QUART) * QTOK, QTOK), QTOK)
                place = pl.ds(k * QTOK, QTOK)
                group.append(pltpu.make_async_copy(acts.at[layer, rows, :], av.at[slot, place, :], sem_a.at[slot, k]))
                group.append(pltpu.make_async_copy(grads.at[layer, rows, :], gv.at[slot, place, :], sem_g.at[slot, k]))
            steps.append((out, j, s, w, slot, group))
    for n in range(slots):
        if n == 0:
            for c in weights[0]:
                c.start()
        for c in steps[n][5]:
            c.start()
        if n == 0:
            for pair in weights[1:]:
                for c in pair:
                    c.start()
    for n, (out, j, s, w, slot, group) in enumerate(steps):
        if s == 0:
            for c in weights[w]:
                c.wait()
        for c in group:
            c.wait()
        parts = (
            lax.dot_general(piv[w], av[slot], NT, preferred_element_type=jnp.float32),
            lax.dot_general(pov[w], gv[slot], NT, preferred_element_type=jnp.float32),
        )
        if n > 0:
            add_powers(per, *steps[n - 1][:3])
        for h, part in enumerate(parts):
            for k in range(per):
                out[s * per + k, j, h * WIDTH : (h + 1) * WIDTH, :] = part[:, k * QTOK : (k + 1) * QTOK]
        if n + slots < len(steps):
            for c in steps[n + slots][5]:
                c.start()
    add_powers(per, *steps[-1][:3])


def project(acts, grads, p_in, p_out, chunk, slots):
    layers, tokens, d_in, d_out = acts.shape[0], acts.shape[1], acts.shape[2], grads.shape[2]
    in_any = pl.BlockSpec(memory_space=pl.ANY)
    return pl.pallas_call(
        functools.partial(project_kernel, chunk, slots),
        in_specs=[in_any] * 4,
        out_specs=[pl.BlockSpec(memory_space=pltpu.VMEM)] * 2,
        out_shape=[jax.ShapeDtypeStruct((QUART, 2, ROWS, QTOK), jnp.float32)] * 2,
        scratch_shapes=[
            pltpu.VMEM((slots, chunk, d_in), jnp.bfloat16),
            pltpu.VMEM((slots, chunk, d_out), jnp.bfloat16),
            pltpu.VMEM((layers, WIDTH, d_in), jnp.bfloat16),
            pltpu.VMEM((layers, WIDTH, d_out), jnp.bfloat16),
            pltpu.SemaphoreType.DMA((slots, chunk // QTOK)),
            pltpu.SemaphoreType.DMA((slots, chunk // QTOK)),
            pltpu.SemaphoreType.DMA((2 * layers,)),
        ],
        compiler_params=pltpu.CompilerParams(vmem_limit_bytes=PROJECT_VMEM),
        cost_estimate=pl.CostEstimate(
            flops=2 * layers * tokens * (d_in + d_out) * WIDTH,
            bytes_accessed=2 * layers * tokens * (d_in + d_out),
            transcendentals=0,
        ),
        name="project",
    )(acts, grads, p_in, p_out)


def score_kernel(scale, s0, s1, s2, s3, q0, q1, q2a, q2b, q3, keep, give):
    t = lax.axis_index("tensor")
    chip = lax.axis_index("dp")
    y, core = t // 2, t % 2
    x, z = chip // RING, chip % RING
    sums = (s0, s1, s2, s3)

    def query(a, b, j):
        if a == 2:
            return (q2a if b < 2 else q2b)[b % 2, j]
        return (q0, q1, None, q3)[a][b, j]

    for d in range(QUART):
        acc = None
        for j in range(2):
            outs = sums[d][j, WIDTH : 2 * WIDTH, :]
            for a in range(RING):
                for b in range(RING):
                    cx = lax.rem(x + jnp.where(core == 0, b, a), RING)
                    cz = lax.rem(z + jnp.where(core == 0, a, b), RING)
                    base = (cx * RING + cz) * 4
                    feats = jnp.concatenate(
                        [
                            (sums[d][j, pl.ds(base + i, 1), :] * outs).astype(jnp.bfloat16)
                            for i in range(4)
                        ],
                        0,
                    )
                    part = jnp.dot(query(a, b, j), feats, preferred_element_type=jnp.float32)
                    acc = part if acc is None else acc + part
        acc = acc * scale
        place = pl.ds(pl.multiple_of(lax.rem(y + d, QUART) * QTOK, QTOK), QTOK)
        keep[:, place] = acc[0:WIDTH]
        give[:, place] = acc[WIDTH : 2 * WIDTH]


def score(sums, quers, scale):
    vm = pl.BlockSpec(memory_space=pltpu.VMEM)
    shape = jax.ShapeDtypeStruct((WIDTH, QUART * QTOK), jnp.float32)
    return pl.pallas_call(
        functools.partial(score_kernel, scale),
        in_specs=[vm] * 9,
        out_specs=[vm] * 2,
        out_shape=[shape] * 2,
        compiler_params=pltpu.CompilerParams(vmem_limit_bytes=SCORE_VMEM),
        cost_estimate=pl.CostEstimate(
            flops=2 * 2 * 1024 * 4096 * 128, bytes_accessed=4 * 2**20, transcendentals=0
        ),
        name="score",
    )(*sums, *quers)


def row_index():
    return lax.broadcasted_iota(jnp.int32, (1, ROWS, 1), 1)


def powers(message):
    row = row_index()
    first = message[:, 2 * WIDTH : 2 * WIDTH + 1].astype(jnp.float32)
    second = message[:, 2 * WIDTH + 4 : 2 * WIDTH + 5].astype(jnp.float32)
    return jnp.where((row < WIDTH) | ((row >= 2 * WIDTH) & (row < 2 * WIDTH + 4)), first, second)


def pack(values, power):
    scaled = values * jnp.exp2(TOP - power)
    return jnp.where(row_index() < 2 * WIDTH, scaled, power).astype(jnp.float16)


def unpack(message):
    return message.astype(jnp.float32) * jnp.exp2(powers(message) - TOP)


def local(activations, out_grads, proj_input, proj_output, query_feats):
    layers = activations.shape[0]
    width = proj_input.shape[1]
    scale = (layers * width * width) ** (-0.5)
    core = lax.axis_index("tensor") % 2
    both = ("dp", "tensor")

    theirs = lax.ppermute(query_feats, "tensor", swap_perm())
    mine = lax.dynamic_slice_in_dim(query_feats, 2 * core, 2, 0)
    got = lax.dynamic_slice_in_dim(theirs, 2 * core, 2, 0)
    line0 = jnp.concatenate([mine, got], axis=1)
    lines = [line0] + [lax.ppermute(line0, both, xz_perm(d, False)) for d in range(1, RING)]
    keep, give = project(activations, out_grads, proj_input, proj_output, 512, 3)
    give, lines = lax.optimization_barrier((give, lines))
    plane0 = jnp.stack(lines)
    taken = lax.ppermute(give, "tensor", swap_perm())
    part = [keep[d] + taken[d] for d in range(QUART)]
    power = [jnp.maximum(powers(keep[d]), powers(taken[d])) + 1.0 for d in range(QUART)]
    packed = [pack(part[d], power[d]) for d in range(1, QUART)]
    sent = [lax.ppermute(packed[d - 1], "tensor", y_perm(d)) for d in range(1, QUART)]
    plane1 = lax.ppermute(plane0, both, xz_perm(1, True))
    plane3 = lax.ppermute(plane0, both, xz_perm(3, True))
    total = part[0] + sum(unpack(m) for m in sent)
    top = power[0]
    for m in sent:
        top = jnp.maximum(top, powers(m))
    message = pack(total, top + 2.0)
    message, plane1, plane3 = lax.optimization_barrier((message, plane1, plane3))
    plane2 = (
        lax.ppermute(plane1[:2], both, xz_perm(1, True)),
        lax.ppermute(plane3[2:], both, xz_perm(3, True)),
    )
    quers = [plane0, plane1, *plane2, plane3]
    sums = [total[:, : 2 * WIDTH]]
    for d in range(1, QUART):
        sums.append(unpack(lax.ppermute(message, "tensor", y_perm(-d)))[:, : 2 * WIDTH])

    keep_s, give_s = score(sums, quers, scale)
    return (keep_s + lax.ppermute(give_s, "tensor", swap_perm())).T


def solution(mesh):
    in_specs = (
        P(None, "dp", "tensor"),
        P(None, "dp", "tensor"),
        P(None, None, "tensor"),
        P(None, None, "tensor"),
        P(None, "tensor", "dp"),
    )
    out_specs = P("dp", "tensor")
    return jax.shard_map(local, mesh=mesh, in_specs=in_specs, out_specs=out_specs, check_vma=False)
```

time: 157 us -> 55.7 us (0.35)
  the two profiles are of different devices: /device:TPU:24 before, /device:TPU:1 now
where the time goes in v1:
time: 55.7 us; the launch traced here: 55.5 us
  starting transfers between devices  24.5 us (44%)
  waiting for transfers between devices  14 us (25%)
  Pallas kernels  12.1 us (22%)
  local copies, waits for them, and re-layouts  2.39 us (4%)
  other arithmetic  2.09 us (4%)
    pallas_call x1, Pallas kernels, project(): pl.pallas_call(functools.partial(project_kernel, chunk, slots), in_specs=...  9.73 us
    ppermute x3, waiting for transfers between devices, local(): lax.ppermute(packed[d - 1], 'tensor', y_perm(d))  6.46 us
    ppermute x3, starting transfers between devices, local(): lax.ppermute(line0, both, xz_perm(d, False))  4.61 us
    ppermute x1, starting transfers between devices, local(): lax.ppermute(plane1[:2], both, xz_perm(1, True))  4.46 us
    ppermute x1, starting transfers between devices, local(): return (keep_s + lax.ppermute(give_s, 'tensor', swap_perm())).T  4.31 us
    ppermute x3, starting transfers between devices, local(): lax.ppermute(packed[d - 1], 'tensor', y_perm(d))  3.92 us
    ppermute x1, waiting for transfers between devices, local(): lax.ppermute(plane3[2:], both, xz_perm(3, True))  3.39 us
    ppermute x3, starting transfers between devices, local(): lax.ppermute(message, 'tensor', y_perm(-d))  2.83 us
  transfers between devices with their start and end apart: 16, of which 7 were waited for; matrix products, arithmetic and copies ran while one was open for 7% of the time, Pallas kernels for 18%

profile of v1, /device:TPU:1, one launch (start us, length us, event | category | flops | bytes accessed | tf_op | source)
XLA Modules:
  0.0 55.5 jit_solution(12163576214005494599)
XLA Ops:
  0.0 1.4 %collective-permute-start = (bf16[4,64,256]{2,1,0:T(8,128)(2,1)}, bf16[4,64,256]{2,1,0:T(8,128)(2,1)S(1)}, u32[]{:S(2)}, u32[]{:S(2)}) collective-permute-start(bf16[4,64,256]{2,1,0:T(8,128)(2,1)} %param.9), channel_id=1, source_target_pairs={{0,1},{1,0},{2,3},{3,2},{4,5},{5,4},{6,7},{7,6},{8,9},{9,8},{10,11... | collective-permute-start | bytes 393224 | tf_op jit(solution)/shard_map/ppermute | solution.py:209
  1.4 0.8 %constant_dynamic-slice_fusion.1 = bf16[2,64,256]{2,1,0:T(8,128)(2,1)S(1)} fusion(bf16[4,64,256]{2,1,0:T(8,128)(2,1)} %param.9, s32[]{:T(128)S(6)} %select_n.71), kind=kLoop, calls=%fused_computation.84 | loop fusion | bytes 131076 | tf_op jit(solution)/shard_map/dynamic_slice | solution.py:210
  2.3 0.4 collective-permute-done
  2.6 3.9 %collective-permute-start.1 = (bf16[2,128,256]{2,1,0:T(8,128)(2,1)S(1)}, bf16[2,128,256]{2,1,0:T(8,128)(2,1)S(1)}, u32[]{:S(2)}, u32[]{:S(2)}) collective-permute-start(bf16[2,128,256]{2,1,0:T(8,128)(2,1)S(1)} %pad_maximum_fusion.1), channel_id=1, source_target_pairs={{32,0},{9,1},{34,2},{11,3},{36,4},{13,5},{38,6},{15,7},{40,8},{17,... | collective-permute-start | bytes 393224 | tf_op jit(solution)/shard_map/ppermute | solution.py:213
  6.6 0.7 %collective-permute-start.3 = (bf16[2,128,256]{2,1,0:T(8,128)(2,1)S(1)}, bf16[2,128,256]{2,1,0:T(8,128)(2,1)S(1)}, u32[]{:S(2)}, u32[]{:S(2)}) collective-permute-start(bf16[2,128,256]{2,1,0:T(8,128)(2,1)S(1)} %pad_maximum_fusion.1), channel_id=1, source_target_pairs={{96,0},{25,1},{98,2},{27,3},{100,4},{29,5},{102,6},{31,7},{104,8},... | collective-permute-start | bytes 393224 | tf_op jit(solution)/shard_map/ppermute | solution.py:213
  7.2 9.7 %project.1 = (f32[4,2,136,256]{3,2,1,0:T(8,128)}, f32[4,2,136,256]{3,2,1,0:T(8,128)}) custom-call(bf16[4,1024,512]{2,1,0:T(8,128)(2,1)} %acts.1, bf16[4,1024,1792]{2,1,0:T(8,128)(2,1)} %grads.1, bf16[4,64,512]{2,1,0:T(8,128)(2,1)} %p_in.1, bf16[4,64,1792]{2,1,0:T(8,128)(2,1)} %p_out.1), custom_call_target="tpu_custom_call" | custom-call | flops 1207959552 | bytes 18874368 | tf_op jit(solution)/shard_map/project/pallas_call | solution.py:106
  17.0 0.4 collective-permute-start.4
  17.4 1.3 %slice_bitcast_fusion.6 = (f32[2,136,256]{2,1,0:T(8,128)S(1)}, f32[2,136,256]{2,1,0:T(8,128)S(1)}, f32[2,136,256]{2,1,0:T(8,128)S(1)}, f32[2,136,256]{2,1,0:T(8,128)S(1)}) fusion(f32[4,2,136,256]{3,2,1,0:T(8,128)} %get-tuple-element.17), kind=kLoop, calls=%fused_computation.30 | loop fusion | bytes 2228224 | tf_op jit(solution)/shard_map/squeeze | solution.py:218
  18.9 0.1 pad_maximum_fusion.q0
  19.0 2.2 %collective-permute-start.8 = (bf16[4,2,128,256]{3,2,1,0:T(8,128)(2,1)S(1)}, bf16[4,2,128,256]{3,2,1,0:T(8,128)(2,1)S(1)}, u32[]{:S(2)}, u32[]{:S(2)}) collective-permute-start(bf16[4,2,128,256]{3,2,1,0:T(8,128)(2,1)S(1)} %pad_maximum_fusion.q0), channel_id=1, source_target_pairs={{8,0},{33,1},{10,2},{35,3},{12,4},{37,5},{14,6},{39,7},{16,8},{41,... | collective-permute-start | bytes 1572872 | tf_op jit(solution)/shard_map/ppermute | solution.py:222
  21.2 0.1 slice_bitcast_fusion.2
  21.4 0.3 select_convert_fusion.3
  21.7 2.8 %collective-permute-start.7 = (f16[2,136,256]{2,1,0:T(8,128)(2,1)S(1)}, f16[2,136,256]{2,1,0:T(8,128)(2,1)S(1)}, u32[]{:S(2)}, u32[]{:S(2)}) collective-permute-start(f16[2,136,256]{2,1,0:T(8,128)(2,1)S(1)} %get-tuple-element.32), channel_id=1, source_target_pairs={{0,6},{1,7},{2,0},{3,1},{4,2},{5,3},{6,4},{7,5},{8,14},{9,15},{10,... | collective-permute-start | bytes 417800 | tf_op jit(solution)/shard_map/ppermute | solution.py:221
  24.5 0.2 select_convert_fusion.2
  24.7 0.4 collective-permute-start.6
  25.1 0.7 %collective-permute-start.5 = (f16[2,136,256]{2,1,0:T(8,128)(2,1)S(1)}, f16[2,136,256]{2,1,0:T(8,128)(2,1)S(1)}, u32[]{:S(2)}, u32[]{:S(2)}) collective-permute-start(f16[2,136,256]{2,1,0:T(8,128)(2,1)S(1)} %get-tuple-element.31), channel_id=1, source_target_pairs={{0,2},{1,3},{2,4},{3,5},{4,6},{5,7},{6,0},{7,1},{8,10},{9,11},{10,... | collective-permute-start | bytes 417800 | tf_op jit(solution)/shard_map/ppermute | solution.py:221
  25.8 1.0 %collective-permute-done.7 = f16[2,136,256]{2,1,0:T(8,128)(2,1)S(1)} collective-permute-done((f16[2,136,256]{2,1,0:T(8,128)(2,1)S(1)}, f16[2,136,256]{2,1,0:T(8,128)(2,1)S(1)}, u32[]{:S(2)}, u32[]{:S(2)}) %collective-permute-start.7) | collective-permute-done | bytes 139296 | tf_op jit(solution)/shard_map/ppermute | solution.py:221
  26.8 3.5 %collective-permute-done.6 = f16[2,136,256]{2,1,0:T(8,128)(2,1)S(1)} collective-permute-done((f16[2,136,256]{2,1,0:T(8,128)(2,1)S(1)}, f16[2,136,256]{2,1,0:T(8,128)(2,1)S(1)}, u32[]{:S(2)}, u32[]{:S(2)}) %collective-permute-start.6) | collective-permute-done | bytes 139296 | tf_op jit(solution)/shard_map/ppermute | solution.py:221
  30.3 2.0 %collective-permute-done.5 = f16[2,136,256]{2,1,0:T(8,128)(2,1)S(1)} collective-permute-done((f16[2,136,256]{2,1,0:T(8,128)(2,1)S(1)}, f16[2,136,256]{2,1,0:T(8,128)(2,1)S(1)}, u32[]{:S(2)}, u32[]{:S(2)}) %collective-permute-start.5) | collective-permute-done | bytes 139296 | tf_op jit(solution)/shard_map/ppermute | solution.py:221
  32.4 0.5 select_convert_fusion
  32.9 0.1 collective-permute-start.12
  32.9 1.7 %collective-permute-start.11 = (f16[2,136,256]{2,1,0:T(8,128)(2,1)S(1)}, f16[2,136,256]{2,1,0:T(8,128)(2,1)S(1)}, u32[]{:S(2)}, u32[]{:S(2)}) collective-permute-start(f16[2,136,256]{2,1,0:T(8,128)(2,1)S(1)} %get-tuple-element.24), channel_id=1, source_target_pairs={{0,4},{1,5},{2,6},{3,7},{4,0},{5,1},{6,2},{7,3},{8,12},{9,13},{10,... | collective-permute-start | bytes 417800 | tf_op jit(solution)/shard_map/ppermute | solution.py:237
  34.6 1.1 %collective-permute-start.10 = (f16[2,136,256]{2,1,0:T(8,128)(2,1)S(1)}, f16[2,136,256]{2,1,0:T(8,128)(2,1)S(1)}, u32[]{:S(2)}, u32[]{:S(2)}) collective-permute-start(f16[2,136,256]{2,1,0:T(8,128)(2,1)S(1)} %get-tuple-element.24), channel_id=1, source_target_pairs={{0,6},{1,7},{2,0},{3,1},{4,2},{5,3},{6,4},{7,5},{8,14},{9,15},{10,... | collective-permute-start | bytes 417800 | tf_op jit(solution)/shard_map/ppermute | solution.py:237
  35.8 4.5 %collective-permute-start.13 = (bf16[2,2,128,256]{3,2,1,0:T(8,128)(2,1)S(1)}, bf16[2,2,128,256]{3,2,1,0:T(8,128)(2,1)S(1)}, u32[]{:S(2)}, u32[]{:S(2)}) collective-permute-start(bf16[2,2,128,256]{3,2,1,0:T(8,128)(2,1)S(1)} %slice.180), channel_id=1, source_target_pairs={{8,0},{33,1},{10,2},{35,3},{12,4},{37,5},{14,6},{39,7},{16,8},{41,... | collective-permute-start | bytes 786440 | tf_op jit(solution)/shard_map/ppermute | solution.py:231
  40.2 0.3 collective-permute-start.14
  40.6 0.3 exponential_multiply_fusion
  40.9 2.6 %collective-permute-done.13.q2a = bf16[2,2,128,256]{3,2,1,0:T(8,128)(2,1)S(1)} collective-permute-done((bf16[2,2,128,256]{3,2,1,0:T(8,128)(2,1)S(1)}, bf16[2,2,128,256]{3,2,1,0:T(8,128)(2,1)S(1)}, u32[]{:S(2)}, u32[]{:S(2)}) %collective-permute-start.13) | collective-permute-done | bytes 262176 | tf_op jit(solution)/shard_map/ppermute | solution.py:231
  43.5 3.4 %collective-permute-done.14.q2b = bf16[2,2,128,256]{3,2,1,0:T(8,128)(2,1)S(1)} collective-permute-done((bf16[2,2,128,256]{3,2,1,0:T(8,128)(2,1)S(1)}, bf16[2,2,128,256]{3,2,1,0:T(8,128)(2,1)S(1)}, u32[]{:S(2)}, u32[]{:S(2)}) %collective-permute-start.14) | collective-permute-done | bytes 262176 | tf_op jit(solution)/shard_map/ppermute | solution.py:232
  46.9 2.4 %score.1 = (f32[64,1024]{1,0:T(8,128)S(1)}, f32[64,1024]{1,0:T(8,128)S(1)}) custom-call(f32[2,128,256]{2,1,0:T(8,128)S(1)} %slice.204.s0, f32[2,128,256]{2,1,0:T(8,128)S(1)} %get-tuple-element.71.s1, f32[2,128,256]{2,1,0:T(8,128)S(1)} %get-tuple-element.70.s2, f32[2,128,256]{2,1,0:T(8,128)S(1)} %get-tuple-element.69.s3, ...), custom_call_target="tpu_custom_call" | custom-call | flops 2147483648 | bytes 4194304 | tf_op jit(solution)/shard_map/score/pallas_call | solution.py:169
  49.3 4.3 %collective-permute-start.15 = (f32[64,1024]{1,0:T(8,128)S(1)}, f32[64,1024]{1,0:T(8,128)S(1)}, u32[]{:S(2)}, u32[]{:S(2)}) collective-permute-start(f32[64,1024]{1,0:T(8,128)S(1)} %get-tuple-element.28), channel_id=1, source_target_pairs={{0,1},{1,0},{2,3},{3,2},{4,5},{5,4},{6,7},{7,6},{8,9},{9,8},{10,11... | collective-permute-start | bytes 786440 | tf_op jit(solution)/shard_map/ppermute | solution.py:240
  53.6 1.2 %collective-permute-done.15 = f32[64,1024]{1,0:T(8,128)S(1)} collective-permute-done((f32[64,1024]{1,0:T(8,128)S(1)}, f32[64,1024]{1,0:T(8,128)S(1)}, u32[]{:S(2)}, u32[]{:S(2)}) %collective-permute-start.15) | collective-permute-done | bytes 262176 | tf_op jit(solution)/shard_map/ppermute | solution.py:240
  54.8 0.7 %add_bitcast_fusion = f32[1024,64]{0,1:T(8,128)} fusion(f32[64,1024]{1,0:T(8,128)S(1)} %get-tuple-element.27, f32[64,1024]{1,0:T(8,128)S(1)} %collective-permute-done.15), kind=kLoop, calls=%fused_computation.32 | loop fusion | flops 65536 | bytes 786432 | tf_op jit(solution)/shard_map/transpose | solution.py:240
  (57 shorter events, 0.2 us)
Async XLA Ops:
  0.0 2.6 %collective-permute-start = (bf16[4,64,256]{2,1,0:T(8,128)(2,1)}, bf16[4,64,256]{2,1,0:T(8,128)(2,1)S(1)}, u32[]{:S(2)}, u32[]{:S(2)}) collective-permute-start(bf16[4,64,256]{2,1,0:T(8,128)(2,1)} %param.9), channel_id=1, source_target_pairs={{0,1},{1,0},{2,3},{3,2},{4,5},{5,4},{6,7},{7,6},{8,9},{9,8},{10,11... | collective-permute-start | bytes 393224 | tf_op jit(solution)/shard_map/ppermute | solution.py:209
  2.6 14.3 %collective-permute-start.1 = (bf16[2,128,256]{2,1,0:T(8,128)(2,1)S(1)}, bf16[2,128,256]{2,1,0:T(8,128)(2,1)S(1)}, u32[]{:S(2)}, u32[]{:S(2)}) collective-permute-start(bf16[2,128,256]{2,1,0:T(8,128)(2,1)S(1)} %pad_maximum_fusion.1), channel_id=1, source_target_pairs={{32,0},{9,1},{34,2},{11,3},{36,4},{13,5},{38,6},{15,7},{40,8},{17,... | collective-permute-start | bytes 393224 | tf_op jit(solution)/shard_map/ppermute | solution.py:213
  6.5 10.4 %collective-permute-start.2 = (bf16[2,128,256]{2,1,0:T(8,128)(2,1)S(1)}, bf16[2,128,256]{2,1,0:T(8,128)(2,1)S(1)}, u32[]{:S(2)}, u32[]{:S(2)}) collective-permute-start(bf16[2,128,256]{2,1,0:T(8,128)(2,1)S(1)} %pad_maximum_fusion.1), channel_id=1, source_target_pairs={{64,0},{17,1},{66,2},{19,3},{68,4},{21,5},{70,6},{23,7},{72,8},{25... | collective-permute-start | bytes 393224 | tf_op jit(solution)/shard_map/ppermute | solution.py:213
  6.6 10.5 %collective-permute-start.3 = (bf16[2,128,256]{2,1,0:T(8,128)(2,1)S(1)}, bf16[2,128,256]{2,1,0:T(8,128)(2,1)S(1)}, u32[]{:S(2)}, u32[]{:S(2)}) collective-permute-start(bf16[2,128,256]{2,1,0:T(8,128)(2,1)S(1)} %pad_maximum_fusion.1), channel_id=1, source_target_pairs={{96,0},{25,1},{98,2},{27,3},{100,4},{29,5},{102,6},{31,7},{104,8},... | collective-permute-start | bytes 393224 | tf_op jit(solution)/shard_map/ppermute | solution.py:213
  17.0 4.2 %collective-permute-start.4 = (f32[4,2,136,256]{3,2,1,0:T(8,128)}, f32[4,2,136,256]{3,2,1,0:T(8,128)S(1)}, u32[]{:S(2)}, u32[]{:S(2)}) collective-permute-start(f32[4,2,136,256]{3,2,1,0:T(8,128)} %get-tuple-element.19), channel_id=1, source_target_pairs={{0,1},{1,0},{2,3},{3,2},{4,5},{5,4},{6,7},{7,6},{8,9},{9,8},{10,11... | collective-permute-start | bytes 3342344 | tf_op jit(solution)/shard_map/ppermute | solution.py:217
  18.9 2.4 %copy-start = (f32[4,2,136,256]{3,2,1,0:T(8,128)S(1)}, f32[4,2,136,256]{3,2,1,0:T(8,128)}, u32[]{:S(2)}) copy-start(f32[4,2,136,256]{3,2,1,0:T(8,128)} %get-tuple-element.17) | copy-start | bytes 3342340
  19.0 13.9 %collective-permute-start.8 = (bf16[4,2,128,256]{3,2,1,0:T(8,128)(2,1)S(1)}, bf16[4,2,128,256]{3,2,1,0:T(8,128)(2,1)S(1)}, u32[]{:S(2)}, u32[]{:S(2)}) collective-permute-start(bf16[4,2,128,256]{3,2,1,0:T(8,128)(2,1)S(1)} %pad_maximum_fusion.q0), channel_id=1, source_target_pairs={{8,0},{33,1},{10,2},{35,3},{12,4},{37,5},{14,6},{39,7},{16,8},{41,... | collective-permute-start | bytes 1572872 | tf_op jit(solution)/shard_map/ppermute | solution.py:222
  21.2 11.7 %collective-permute-start.9 = (bf16[4,2,128,256]{3,2,1,0:T(8,128)(2,1)S(1)}, bf16[4,2,128,256]{3,2,1,0:T(8,128)(2,1)S(1)}, u32[]{:S(2)}, u32[]{:S(2)}) collective-permute-start(bf16[4,2,128,256]{3,2,1,0:T(8,128)(2,1)S(1)} %pad_maximum_fusion.q0), channel_id=1, source_target_pairs={{24,0},{97,1},{26,2},{99,3},{28,4},{101,5},{30,6},{103,7},{0,8},{1... | collective-permute-start | bytes 1572872 | tf_op jit(solution)/shard_map/ppermute | solution.py:223
  21.7 5.1 %collective-permute-start.7 = (f16[2,136,256]{2,1,0:T(8,128)(2,1)S(1)}, f16[2,136,256]{2,1,0:T(8,128)(2,1)S(1)}, u32[]{:S(2)}, u32[]{:S(2)}) collective-permute-start(f16[2,136,256]{2,1,0:T(8,128)(2,1)S(1)} %get-tuple-element.32), channel_id=1, source_target_pairs={{0,6},{1,7},{2,0},{3,1},{4,2},{5,3},{6,4},{7,5},{8,14},{9,15},{10,... | collective-permute-start | bytes 417800 | tf_op jit(solution)/shard_map/ppermute | solution.py:221
  24.7 5.6 %collective-permute-start.6 = (f16[2,136,256]{2,1,0:T(8,128)(2,1)S(1)}, f16[2,136,256]{2,1,0:T(8,128)(2,1)S(1)}, u32[]{:S(2)}, u32[]{:S(2)}) collective-permute-start(f16[2,136,256]{2,1,0:T(8,128)(2,1)S(1)} %select_convert_fusion.2), channel_id=1, source_target_pairs={{0,4},{1,5},{2,6},{3,7},{4,0},{5,1},{6,2},{7,3},{8,12},{9,13},{10,... | collective-permute-start | bytes 417800 | tf_op jit(solution)/shard_map/ppermute | solution.py:221
  25.1 7.2 %collective-permute-start.5 = (f16[2,136,256]{2,1,0:T(8,128)(2,1)S(1)}, f16[2,136,256]{2,1,0:T(8,128)(2,1)S(1)}, u32[]{:S(2)}, u32[]{:S(2)}) collective-permute-start(f16[2,136,256]{2,1,0:T(8,128)(2,1)S(1)} %get-tuple-element.31), channel_id=1, source_target_pairs={{0,2},{1,3},{2,4},{3,5},{4,6},{5,7},{6,0},{7,1},{8,10},{9,11},{10,... | collective-permute-start | bytes 417800 | tf_op jit(solution)/shard_map/ppermute | solution.py:221
  32.9 7.6 %collective-permute-start.12 = (f16[2,136,256]{2,1,0:T(8,128)(2,1)S(1)}, f16[2,136,256]{2,1,0:T(8,128)(2,1)S(1)}, u32[]{:S(2)}, u32[]{:S(2)}) collective-permute-start(f16[2,136,256]{2,1,0:T(8,128)(2,1)S(1)} %get-tuple-element.24), channel_id=1, source_target_pairs={{0,2},{1,3},{2,4},{3,5},{4,6},{5,7},{6,0},{7,1},{8,10},{9,11},{10,... | collective-permute-start | bytes 417800 | tf_op jit(solution)/shard_map/ppermute | solution.py:237
  32.9 7.6 %collective-permute-start.11 = (f16[2,136,256]{2,1,0:T(8,128)(2,1)S(1)}, f16[2,136,256]{2,1,0:T(8,128)(2,1)S(1)}, u32[]{:S(2)}, u32[]{:S(2)}) collective-permute-start(f16[2,136,256]{2,1,0:T(8,128)(2,1)S(1)} %get-tuple-element.24), channel_id=1, source_target_pairs={{0,4},{1,5},{2,6},{3,7},{4,0},{5,1},{6,2},{7,3},{8,12},{9,13},{10,... | collective-permute-start | bytes 417800 | tf_op jit(solution)/shard_map/ppermute | solution.py:237
  34.6 5.9 %collective-permute-start.10 = (f16[2,136,256]{2,1,0:T(8,128)(2,1)S(1)}, f16[2,136,256]{2,1,0:T(8,128)(2,1)S(1)}, u32[]{:S(2)}, u32[]{:S(2)}) collective-permute-start(f16[2,136,256]{2,1,0:T(8,128)(2,1)S(1)} %get-tuple-element.24), channel_id=1, source_target_pairs={{0,6},{1,7},{2,0},{3,1},{4,2},{5,3},{6,4},{7,5},{8,14},{9,15},{10,... | collective-permute-start | bytes 417800 | tf_op jit(solution)/shard_map/ppermute | solution.py:237
  35.8 7.8 %collective-permute-start.13 = (bf16[2,2,128,256]{3,2,1,0:T(8,128)(2,1)S(1)}, bf16[2,2,128,256]{3,2,1,0:T(8,128)(2,1)S(1)}, u32[]{:S(2)}, u32[]{:S(2)}) collective-permute-start(bf16[2,2,128,256]{3,2,1,0:T(8,128)(2,1)S(1)} %slice.180), channel_id=1, source_target_pairs={{8,0},{33,1},{10,2},{35,3},{12,4},{37,5},{14,6},{39,7},{16,8},{41,... | collective-permute-start | bytes 786440 | tf_op jit(solution)/shard_map/ppermute | solution.py:231
  40.2 6.7 %collective-permute-start.14 = (bf16[2,2,128,256]{3,2,1,0:T(8,128)(2,1)S(1)}, bf16[2,2,128,256]{3,2,1,0:T(8,128)(2,1)S(1)}, u32[]{:S(2)}, u32[]{:S(2)}) collective-permute-start(bf16[2,2,128,256]{3,2,1,0:T(8,128)(2,1)S(1)} %slice.181), channel_id=1, source_target_pairs={{24,0},{97,1},{26,2},{99,3},{28,4},{101,5},{30,6},{103,7},{0,8},{1... | collective-permute-start | bytes 786440 | tf_op jit(solution)/shard_map/ppermute | solution.py:232
  49.3 5.5 %collective-permute-start.15 = (f32[64,1024]{1,0:T(8,128)S(1)}, f32[64,1024]{1,0:T(8,128)S(1)}, u32[]{:S(2)}, u32[]{:S(2)}) collective-permute-start(f32[64,1024]{1,0:T(8,128)S(1)} %get-tuple-element.28), channel_id=1, source_target_pairs={{0,1},{1,0},{2,3},{3,2},{4,5},{5,4},{6,7},{7,6},{8,9},{9,8},{10,11... | collective-permute-start | bytes 786440 | tf_op jit(solution)/shard_map/ppermute | solution.py:240

commit v2 on v1

--- a/solution.py
+++ b/solution.py
@@ -10,6 +10,7 @@
 NT = (((1,), (1,)), ((), ()))
 PROJECT_VMEM = 61 * 2**20
 SCORE_VMEM = 24 * 2**20
+OWN_FLOPS = 12 * 10**9
 RING = 4
 WIDTH = 64
 QTOK = 256
@@ -127,43 +128,59 @@
     )(acts, grads, p_in, p_out)
 
 
-def score_kernel(scale, s0, s1, s2, s3, q0, q1, q2a, q2b, q3, keep, give):
-    t = lax.axis_index("tensor")
+def score_tokens(scale, sums, q0, q1, q2a, q2b, q3):
+    core = lax.axis_index("tensor") % 2
     chip = lax.axis_index("dp")
-    y, core = t // 2, t % 2
     x, z = chip // RING, chip % RING
-    sums = (s0, s1, s2, s3)
 
     def query(a, b, j):
         if a == 2:
             return (q2a if b < 2 else q2b)[b % 2, j]
         return (q0, q1, None, q3)[a][b, j]
 
-    for d in range(QUART):
-        acc = None
-        for j in range(2):
-            outs = sums[d][j, WIDTH : 2 * WIDTH, :]
-            for a in range(RING):
-                for b in range(RING):
-                    cx = lax.rem(x + jnp.where(core == 0, b, a), RING)
-                    cz = lax.rem(z + jnp.where(core == 0, a, b), RING)
-                    base = (cx * RING + cz) * 4
-                    feats = jnp.concatenate(
-                        [
-                            (sums[d][j, pl.ds(base + i, 1), :] * outs).astype(jnp.bfloat16)
-                            for i in range(4)
-                        ],
-                        0,
-                    )
-                    part = jnp.dot(query(a, b, j), feats, preferred_element_type=jnp.float32)
-                    acc = part if acc is None else acc + part
-        acc = acc * scale
+    acc = None
+    for j in range(2):
+        outs = sums[j, WIDTH : 2 * WIDTH, :]
+        for a in range(RING):
+            for b in range(RING):
+                cx = lax.rem(x + jnp.where(core == 0, b, a), RING)
+                cz = lax.rem(z + jnp.where(core == 0, a, b), RING)
+                base = (cx * RING + cz) * 4
+                feats = jnp.concatenate(
+                    [(sums[j, pl.ds(base + i, 1), :] * outs).astype(jnp.bfloat16) for i in range(4)], 0
+                )
+                part = jnp.dot(query(a, b, j), feats, preferred_element_type=jnp.float32)
+                acc = part if acc is None else acc + part
+    return acc * scale
+
+
+def own_score_kernel(scale, s0, q0, q1, q2a, q2b, q3, out):
+    out[...] = score_tokens(scale, s0, q0, q1, q2a, q2b, q3)
+
+
+def score_kernel(scale, own, s1, s2, s3, q0, q1, q2a, q2b, q3, keep, give):
+    y = lax.axis_index("tensor") // 2
+    for d, sums in enumerate((None, s1, s2, s3)):
+        acc = own[...] if d == 0 else score_tokens(scale, sums, q0, q1, q2a, q2b, q3)
         place = pl.ds(pl.multiple_of(lax.rem(y + d, QUART) * QTOK, QTOK), QTOK)
         keep[:, place] = acc[0:WIDTH]
         give[:, place] = acc[WIDTH : 2 * WIDTH]
 
 
-def score(sums, quers, scale):
+def own_score(total, quers, scale):
+    vm = pl.BlockSpec(memory_space=pltpu.VMEM)
+    return pl.pallas_call(
+        functools.partial(own_score_kernel, scale),
+        in_specs=[vm] * 6,
+        out_specs=vm,
+        out_shape=jax.ShapeDtypeStruct((2 * WIDTH, QTOK), jnp.float32),
+        compiler_params=pltpu.CompilerParams(vmem_limit_bytes=SCORE_VMEM),
+        cost_estimate=pl.CostEstimate(flops=OWN_FLOPS, bytes_accessed=4 * 2**20, transcendentals=0),
+        name="own_score",
+    )(total, *quers)
+
+
+def score(own, sums, quers, scale):
     vm = pl.BlockSpec(memory_space=pltpu.VMEM)
     shape = jax.ShapeDtypeStruct((WIDTH, QUART * QTOK), jnp.float32)
     return pl.pallas_call(
@@ -176,7 +193,11 @@
             flops=2 * 2 * 1024 * 4096 * 128, bytes_accessed=4 * 2**20, transcendentals=0
         ),
         name="score",
-    )(*sums, *quers)
+    )(own, *sums, *quers)
+
+
+def after(value, other):
+    return lax.optimization_barrier((value, other))[0]
 
 
 def row_index():
@@ -226,17 +247,16 @@
     for m in sent:
         top = jnp.maximum(top, powers(m))
     message = pack(total, top + 2.0)
-    message, plane1, plane3 = lax.optimization_barrier((message, plane1, plane3))
-    plane2 = (
-        lax.ppermute(plane1[:2], both, xz_perm(1, True)),
-        lax.ppermute(plane3[2:], both, xz_perm(3, True)),
-    )
+    plane1 = after(plane1, sent[2])
+    plane2 = lax.ppermute(plane1, both, xz_perm(1, True))
+    plane2 = (plane2[:2], plane2[2:])
     quers = [plane0, plane1, *plane2, plane3]
-    sums = [total[:, : 2 * WIDTH]]
+    own = own_score(total[:, : 2 * WIDTH], quers, scale)
+    sums = []
     for d in range(1, QUART):
-        sums.append(unpack(lax.ppermute(message, "tensor", y_perm(-d)))[:, : 2 * WIDTH])
-
-    keep_s, give_s = score(sums, quers, scale)
+        sums.append(unpack(after(lax.ppermute(message, "tensor", y_perm(-d)), own))[:, : 2 * WIDTH])
+
+    keep_s, give_s = score(own, sums, quers, scale)
     return (keep_s + lax.ppermute(give_s, "tensor", swap_perm())).T
 
 

time: 55.7 us -> 50.5 us (0.907)
  waiting for transfers between devices: 14 us -> 7.85 us
  starting transfers between devices: 24.5 us -> 25.3 us
    ppermute x2 -> x1, waiting for transfers between devices: 6.02 us -> 0.45 us  [local(): plane2 = lax.ppermute(plane1, both, xz_perm(1, True))]
    ppermute x3, waiting for transfers between devices: 6.46 us -> 1.6 us  [local(): lax.ppermute(packed[d - 1], 'tensor', y_perm(d))]
    ppermute x3, waiting for transfers between devices: 0.01 us -> 2.68 us  [local(): lax.ppermute(message, 'tensor', y_perm(-d))]
    ppermute x1, waiting for transfers between devices: 0.01 us -> 1.59 us  [local(): plane1 = lax.ppermute(plane0, both, xz_perm(1, True))]
    ppermute x1, starting transfers between devices: 4.31 us -> 5.89 us  [local(): return (keep_s + lax.ppermute(give_s, 'tensor', swap_perm())).T]
    ppermute x2 -> x1, starting transfers between devices: 4.72 us -> 3.3 us  [local(): plane2 = lax.ppermute(plane1, both, xz_perm(1, True))]
    pallas_call x0 -> x1, Pallas kernels: none -> 0.76 us  [own_score(): pl.pallas_call(functools.partial(own_score_kernel, scale), in_specs=[vm]...]
    ppermute x3, starting transfers between devices: 2.83 us -> 3.48 us  [local(): lax.ppermute(message, 'tensor', y_perm(-d))]
  transfers between devices with their start and end apart: 16 -> 15, of which waited for: 7 -> 7; matrix products, arithmetic and copies ran while one was open for 7% -> 7% of each run, Pallas kernels for 18% -> 21%
where the time goes in v2:
time: 50.5 us; the launch traced here: 50.4 us
  starting transfers between devices  25.3 us (50%)
  Pallas kernels  12.3 us (24%)
  waiting for transfers between devices  7.85 us (16%)
  local copies, waits for them, and re-layouts  2.39 us (5%)
  other arithmetic  2.11 us (4%)
    pallas_call x1, Pallas kernels, project(): pl.pallas_call(functools.partial(project_kernel, chunk, slots), in_specs=...  9.73 us
    ppermute x1, starting transfers between devices, local(): return (keep_s + lax.ppermute(give_s, 'tensor', swap_perm())).T  5.89 us
    ppermute x3, starting transfers between devices, local(): lax.ppermute(line0, both, xz_perm(d, False))  4.61 us
    ppermute x3, starting transfers between devices, local(): lax.ppermute(packed[d - 1], 'tensor', y_perm(d))  3.92 us
    ppermute x3, starting transfers between devices, local(): lax.ppermute(message, 'tensor', y_perm(-d))  3.48 us
    ppermute x1, starting transfers between devices, local(): plane2 = lax.ppermute(plane1, both, xz_perm(1, True))  3.3 us
    ppermute x3, waiting for transfers between devices, local(): lax.ppermute(message, 'tensor', y_perm(-d))  2.68 us
    ppermute x1, starting transfers between devices, local(): plane1 = lax.ppermute(plane0, both, xz_perm(1, True))  2.22 us
  transfers between devices with their start and end apart: 15, of which 7 were waited for; matrix products, arithmetic and copies ran while one was open for 7% of the time, Pallas kernels for 21%

profile of v2, /device:TPU:1, one launch (start us, length us, event | category | flops | bytes accessed | tf_op | source)
XLA Modules:
  0.0 50.4 jit_solution(5462363928394584890)
XLA Ops:
  0.0 1.4 %collective-permute-start = (bf16[4,64,256]{2,1,0:T(8,128)(2,1)}, bf16[4,64,256]{2,1,0:T(8,128)(2,1)S(1)}, u32[]{:S(2)}, u32[]{:S(2)}) collective-permute-start(bf16[4,64,256]{2,1,0:T(8,128)(2,1)} %param.9), channel_id=1, source_target_pairs={{0,1},{1,0},{2,3},{3,2},{4,5},{5,4},{6,7},{7,6},{8,9},{9,8},{10,11... | collective-permute-start | bytes 393224 | tf_op jit(solution)/shard_map/ppermute | solution.py:230
  1.4 0.8 %constant_dynamic-slice_fusion.1 = bf16[2,64,256]{2,1,0:T(8,128)(2,1)S(1)} fusion(bf16[4,64,256]{2,1,0:T(8,128)(2,1)} %param.9, s32[]{:T(128)S(6)} %select_n.71), kind=kLoop, calls=%fused_computation.84 | loop fusion | bytes 131076 | tf_op jit(solution)/shard_map/dynamic_slice | solution.py:231
  2.3 0.4 collective-permute-done
  2.6 3.9 %collective-permute-start.1 = (bf16[2,128,256]{2,1,0:T(8,128)(2,1)S(1)}, bf16[2,128,256]{2,1,0:T(8,128)(2,1)S(1)}, u32[]{:S(2)}, u32[]{:S(2)}) collective-permute-start(bf16[2,128,256]{2,1,0:T(8,128)(2,1)S(1)} %pad_maximum_fusion.1), channel_id=1, source_target_pairs={{32,0},{9,1},{34,2},{11,3},{36,4},{13,5},{38,6},{15,7},{40,8},{17,... | collective-permute-start | bytes 393224 | tf_op jit(solution)/shard_map/ppermute | solution.py:234
  6.6 0.7 %collective-permute-start.3 = (bf16[2,128,256]{2,1,0:T(8,128)(2,1)S(1)}, bf16[2,128,256]{2,1,0:T(8,128)(2,1)S(1)}, u32[]{:S(2)}, u32[]{:S(2)}) collective-permute-start(bf16[2,128,256]{2,1,0:T(8,128)(2,1)S(1)} %pad_maximum_fusion.1), channel_id=1, source_target_pairs={{96,0},{25,1},{98,2},{27,3},{100,4},{29,5},{102,6},{31,7},{104,8},... | collective-permute-start | bytes 393224 | tf_op jit(solution)/shard_map/ppermute | solution.py:234
  7.2 9.7 %project.1 = (f32[4,2,136,256]{3,2,1,0:T(8,128)}, f32[4,2,136,256]{3,2,1,0:T(8,128)}) custom-call(bf16[4,1024,512]{2,1,0:T(8,128)(2,1)} %acts.1, bf16[4,1024,1792]{2,1,0:T(8,128)(2,1)} %grads.1, bf16[4,64,512]{2,1,0:T(8,128)(2,1)} %p_in.1, bf16[4,64,1792]{2,1,0:T(8,128)(2,1)} %p_out.1), custom_call_target="tpu_custom_call" | custom-call | flops 1207959552 | bytes 18874368 | tf_op jit(solution)/shard_map/project/pallas_call | solution.py:107
  17.0 0.4 collective-permute-start.4
  17.4 1.3 %slice_bitcast_fusion.6 = (f32[2,136,256]{2,1,0:T(8,128)S(1)}, f32[2,136,256]{2,1,0:T(8,128)S(1)}, f32[2,136,256]{2,1,0:T(8,128)S(1)}, f32[2,136,256]{2,1,0:T(8,128)S(1)}) fusion(f32[4,2,136,256]{3,2,1,0:T(8,128)} %get-tuple-element.18), kind=kLoop, calls=%fused_computation.30 | loop fusion | bytes 2228224 | tf_op jit(solution)/shard_map/squeeze | solution.py:239
  18.9 0.1 pad_maximum_fusion.q0
  19.0 2.2 %collective-permute-start.8 = (bf16[4,2,128,256]{3,2,1,0:T(8,128)(2,1)S(1)}, bf16[4,2,128,256]{3,2,1,0:T(8,128)(2,1)S(1)}, u32[]{:S(2)}, u32[]{:S(2)}) collective-permute-start(bf16[4,2,128,256]{3,2,1,0:T(8,128)(2,1)S(1)} %pad_maximum_fusion.q0), channel_id=1, source_target_pairs={{8,0},{33,1},{10,2},{35,3},{12,4},{37,5},{14,6},{39,7},{16,8},{41,... | collective-permute-start | bytes 1572872 | tf_op jit(solution)/shard_map/ppermute | solution.py:243
  21.2 0.1 slice_bitcast_fusion.2
  21.4 0.3 select_convert_fusion.3
  21.7 2.8 %collective-permute-start.7 = (f16[2,136,256]{2,1,0:T(8,128)(2,1)S(1)}, f16[2,136,256]{2,1,0:T(8,128)(2,1)S(1)}, u32[]{:S(2)}, u32[]{:S(2)}) collective-permute-start(f16[2,136,256]{2,1,0:T(8,128)(2,1)S(1)} %get-tuple-element.34), channel_id=1, source_target_pairs={{0,6},{1,7},{2,0},{3,1},{4,2},{5,3},{6,4},{7,5},{8,14},{9,15},{10,... | collective-permute-start | bytes 417800 | tf_op jit(solution)/shard_map/ppermute | solution.py:242
  24.5 0.2 select_convert_fusion.2
  24.7 0.4 collective-permute-start.6
  25.1 0.7 %collective-permute-start.5 = (f16[2,136,256]{2,1,0:T(8,128)(2,1)S(1)}, f16[2,136,256]{2,1,0:T(8,128)(2,1)S(1)}, u32[]{:S(2)}, u32[]{:S(2)}) collective-permute-start(f16[2,136,256]{2,1,0:T(8,128)(2,1)S(1)} %get-tuple-element.33), channel_id=1, source_target_pairs={{0,2},{1,3},{2,4},{3,5},{4,6},{5,7},{6,0},{7,1},{8,10},{9,11},{10,... | collective-permute-start | bytes 417800 | tf_op jit(solution)/shard_map/ppermute | solution.py:242
  25.8 1.6 %collective-permute-done.8.q1 = bf16[4,2,128,256]{3,2,1,0:T(8,128)(2,1)S(1)} collective-permute-done((bf16[4,2,128,256]{3,2,1,0:T(8,128)(2,1)S(1)}, bf16[4,2,128,256]{3,2,1,0:T(8,128)(2,1)S(1)}, u32[]{:S(2)}, u32[]{:S(2)}) %collective-permute-start.8) | collective-permute-done | bytes 524320 | tf_op jit(solution)/shard_map/ppermute | solution.py:243
  27.4 3.3 %collective-permute-start.9 = (bf16[4,2,128,256]{3,2,1,0:T(8,128)(2,1)S(1)}, bf16[4,2,128,256]{3,2,1,0:T(8,128)(2,1)S(1)}, u32[]{:S(2)}, u32[]{:S(2)}) collective-permute-start(bf16[4,2,128,256]{3,2,1,0:T(8,128)(2,1)S(1)} %collective-permute-done.8.q1), channel_id=1, source_target_pairs={{8,0},{33,1},{10,2},{35,3},{12,4},{37,5},{14,6},{39,7},{16,8},{41,... | collective-permute-start | bytes 1572872 | tf_op jit(solution)/shard_map/ppermute | solution.py:251
  30.7 1.6 %collective-permute-done.5 = f16[2,136,256]{2,1,0:T(8,128)(2,1)S(1)} collective-permute-done((f16[2,136,256]{2,1,0:T(8,128)(2,1)S(1)}, f16[2,136,256]{2,1,0:T(8,128)(2,1)S(1)}, u32[]{:S(2)}, u32[]{:S(2)}) %collective-permute-start.5) | collective-permute-done | bytes 139296 | tf_op jit(solution)/shard_map/ppermute | solution.py:242
  32.4 0.5 select_convert_fusion
  32.9 0.1 collective-permute-start.13
  33.0 2.3 %collective-permute-start.12 = (f16[2,136,256]{2,1,0:T(8,128)(2,1)S(1)}, f16[2,136,256]{2,1,0:T(8,128)(2,1)S(1)}, u32[]{:S(2)}, u32[]{:S(2)}) collective-permute-start(f16[2,136,256]{2,1,0:T(8,128)(2,1)S(1)} %get-tuple-element.31), channel_id=1, source_target_pairs={{0,4},{1,5},{2,6},{3,7},{4,0},{5,1},{6,2},{7,3},{8,12},{9,13},{10,... | collective-permute-start | bytes 417800 | tf_op jit(solution)/shard_map/ppermute | solution.py:257
  35.3 1.1 %collective-permute-start.11 = (f16[2,136,256]{2,1,0:T(8,128)(2,1)S(1)}, f16[2,136,256]{2,1,0:T(8,128)(2,1)S(1)}, u32[]{:S(2)}, u32[]{:S(2)}) collective-permute-start(f16[2,136,256]{2,1,0:T(8,128)(2,1)S(1)} %get-tuple-element.31), channel_id=1, source_target_pairs={{0,6},{1,7},{2,0},{3,1},{4,2},{5,3},{6,4},{7,5},{8,14},{9,15},{10,... | collective-permute-start | bytes 417800 | tf_op jit(solution)/shard_map/ppermute | solution.py:257
  36.4 0.5 collective-permute-done.9
  36.9 0.8 %own_score.1.own = f32[128,256]{1,0:T(8,128)S(1)} custom-call(f32[2,128,256]{2,1,0:T(8,128)S(1)} %slice.204.s0, bf16[4,2,128,256]{3,2,1,0:T(8,128)(2,1)S(1)} %pad_maximum_fusion.q0, bf16[4,2,128,256]{3,2,1,0:T(8,128)(2,1)S(1)} %collective-permute-done.8.q1, bf16[2,2,128,256]{3,2,1,0:T(8,128)(2,1)S(1)} %get-tuple-element.44.q2a, ...), custom_call_target="tpu_custom_call" | custom-call | flops 12000000000 | bytes 4194304 | tf_op jit(solution)/shard_map/own_score/pallas_call | solution.py:172
  37.7 1.9 %collective-permute-done.13 = f16[2,136,256]{2,1,0:T(8,128)(2,1)S(1)} collective-permute-done((f16[2,136,256]{2,1,0:T(8,128)(2,1)S(1)}, f16[2,136,256]{2,1,0:T(8,128)(2,1)S(1)}, u32[]{:S(2)}, u32[]{:S(2)}) %collective-permute-start.13) | collective-permute-done | bytes 139296 | tf_op jit(solution)/shard_map/ppermute | solution.py:257
  39.6 0.8 %collective-permute-done.11 = f16[2,136,256]{2,1,0:T(8,128)(2,1)S(1)} collective-permute-done((f16[2,136,256]{2,1,0:T(8,128)(2,1)S(1)}, f16[2,136,256]{2,1,0:T(8,128)(2,1)S(1)}, u32[]{:S(2)}, u32[]{:S(2)}) %collective-permute-start.11) | collective-permute-done | bytes 139296 | tf_op jit(solution)/shard_map/ppermute | solution.py:257
  40.4 0.3 exponential_multiply_fusion
  40.7 1.9 %score.1 = (f32[64,1024]{1,0:T(8,128)S(1)}, f32[64,1024]{1,0:T(8,128)S(1)}) custom-call(f32[128,256]{1,0:T(8,128)S(1)} %own_score.1.own, f32[2,128,256]{2,1,0:T(8,128)S(1)} %get-tuple-element.75.s1, f32[2,128,256]{2,1,0:T(8,128)S(1)} %get-tuple-element.74.s2, f32[2,128,256]{2,1,0:T(8,128)S(1)} %get-tuple-element.73.s3, ...), custom_call_target="tpu_custom_call" | custom-call | flops 2147483648 | bytes 4194304 | tf_op jit(solution)/shard_map/score/pallas_call | solution.py:186
  42.6 5.9 %collective-permute-start.14 = (f32[64,1024]{1,0:T(8,128)S(1)}, f32[64,1024]{1,0:T(8,128)S(1)}, u32[]{:S(2)}, u32[]{:S(2)}) collective-permute-start(f32[64,1024]{1,0:T(8,128)S(1)} %get-tuple-element.30), channel_id=1, source_target_pairs={{0,1},{1,0},{2,3},{3,2},{4,5},{5,4},{6,7},{7,6},{8,9},{9,8},{10,11... | collective-permute-start | bytes 786440 | tf_op jit(solution)/shard_map/ppermute | solution.py:260
  48.5 1.2 %collective-permute-done.14 = f32[64,1024]{1,0:T(8,128)S(1)} collective-permute-done((f32[64,1024]{1,0:T(8,128)S(1)}, f32[64,1024]{1,0:T(8,128)S(1)}, u32[]{:S(2)}, u32[]{:S(2)}) %collective-permute-start.14) | collective-permute-done | bytes 262176 | tf_op jit(solution)/shard_map/ppermute | solution.py:260
  49.6 0.7 %add_bitcast_fusion = f32[1024,64]{0,1:T(8,128)} fusion(f32[64,1024]{1,0:T(8,128)S(1)} %get-tuple-element.29, f32[64,1024]{1,0:T(8,128)S(1)} %collective-permute-done.14), kind=kLoop, calls=%fused_computation.32 | loop fusion | flops 65536 | bytes 786432 | tf_op jit(solution)/shard_map/transpose | solution.py:260
  (55 shorter events, 0.2 us)
Async XLA Ops:
  0.0 2.6 %collective-permute-start = (bf16[4,64,256]{2,1,0:T(8,128)(2,1)}, bf16[4,64,256]{2,1,0:T(8,128)(2,1)S(1)}, u32[]{:S(2)}, u32[]{:S(2)}) collective-permute-start(bf16[4,64,256]{2,1,0:T(8,128)(2,1)} %param.9), channel_id=1, source_target_pairs={{0,1},{1,0},{2,3},{3,2},{4,5},{5,4},{6,7},{7,6},{8,9},{9,8},{10,11... | collective-permute-start | bytes 393224 | tf_op jit(solution)/shard_map/ppermute | solution.py:230
  2.6 14.3 %collective-permute-start.1 = (bf16[2,128,256]{2,1,0:T(8,128)(2,1)S(1)}, bf16[2,128,256]{2,1,0:T(8,128)(2,1)S(1)}, u32[]{:S(2)}, u32[]{:S(2)}) collective-permute-start(bf16[2,128,256]{2,1,0:T(8,128)(2,1)S(1)} %pad_maximum_fusion.1), channel_id=1, source_target_pairs={{32,0},{9,1},{34,2},{11,3},{36,4},{13,5},{38,6},{15,7},{40,8},{17,... | collective-permute-start | bytes 393224 | tf_op jit(solution)/shard_map/ppermute | solution.py:234
  6.5 10.4 %collective-permute-start.2 = (bf16[2,128,256]{2,1,0:T(8,128)(2,1)S(1)}, bf16[2,128,256]{2,1,0:T(8,128)(2,1)S(1)}, u32[]{:S(2)}, u32[]{:S(2)}) collective-permute-start(bf16[2,128,256]{2,1,0:T(8,128)(2,1)S(1)} %pad_maximum_fusion.1), channel_id=1, source_target_pairs={{64,0},{17,1},{66,2},{19,3},{68,4},{21,5},{70,6},{23,7},{72,8},{25... | collective-permute-start | bytes 393224 | tf_op jit(solution)/shard_map/ppermute | solution.py:234
  6.6 10.5 %collective-permute-start.3 = (bf16[2,128,256]{2,1,0:T(8,128)(2,1)S(1)}, bf16[2,128,256]{2,1,0:T(8,128)(2,1)S(1)}, u32[]{:S(2)}, u32[]{:S(2)}) collective-permute-start(bf16[2,128,256]{2,1,0:T(8,128)(2,1)S(1)} %pad_maximum_fusion.1), channel_id=1, source_target_pairs={{96,0},{25,1},{98,2},{27,3},{100,4},{29,5},{102,6},{31,7},{104,8},... | collective-permute-start | bytes 393224 | tf_op jit(solution)/shard_map/ppermute | solution.py:234
  17.0 4.2 %collective-permute-start.4 = (f32[4,2,136,256]{3,2,1,0:T(8,128)}, f32[4,2,136,256]{3,2,1,0:T(8,128)S(1)}, u32[]{:S(2)}, u32[]{:S(2)}) collective-permute-start(f32[4,2,136,256]{3,2,1,0:T(8,128)} %get-tuple-element.20), channel_id=1, source_target_pairs={{0,1},{1,0},{2,3},{3,2},{4,5},{5,4},{6,7},{7,6},{8,9},{9,8},{10,11... | collective-permute-start | bytes 3342344 | tf_op jit(solution)/shard_map/ppermute | solution.py:238
  18.9 2.4 %copy-start = (f32[4,2,136,256]{3,2,1,0:T(8,128)S(1)}, f32[4,2,136,256]{3,2,1,0:T(8,128)}, u32[]{:S(2)}) copy-start(f32[4,2,136,256]{3,2,1,0:T(8,128)} %get-tuple-element.18) | copy-start | bytes 3342340
  19.0 8.5 %collective-permute-start.8 = (bf16[4,2,128,256]{3,2,1,0:T(8,128)(2,1)S(1)}, bf16[4,2,128,256]{3,2,1,0:T(8,128)(2,1)S(1)}, u32[]{:S(2)}, u32[]{:S(2)}) collective-permute-start(bf16[4,2,128,256]{3,2,1,0:T(8,128)(2,1)S(1)} %pad_maximum_fusion.q0), channel_id=1, source_target_pairs={{8,0},{33,1},{10,2},{35,3},{12,4},{37,5},{14,6},{39,7},{16,8},{41,... | collective-permute-start | bytes 1572872 | tf_op jit(solution)/shard_map/ppermute | solution.py:243
  21.2 15.7 %collective-permute-start.10 = (bf16[4,2,128,256]{3,2,1,0:T(8,128)(2,1)S(1)}, bf16[4,2,128,256]{3,2,1,0:T(8,128)(2,1)S(1)}, u32[]{:S(2)}, u32[]{:S(2)}) collective-permute-start(bf16[4,2,128,256]{3,2,1,0:T(8,128)(2,1)S(1)} %pad_maximum_fusion.q0), channel_id=1, source_target_pairs={{24,0},{97,1},{26,2},{99,3},{28,4},{101,5},{30,6},{103,7},{0,8},{1... | collective-permute-start | bytes 1572872 | tf_op jit(solution)/shard_map/ppermute | solution.py:244
  21.7 5.7 %collective-permute-start.7 = (f16[2,136,256]{2,1,0:T(8,128)(2,1)S(1)}, f16[2,136,256]{2,1,0:T(8,128)(2,1)S(1)}, u32[]{:S(2)}, u32[]{:S(2)}) collective-permute-start(f16[2,136,256]{2,1,0:T(8,128)(2,1)S(1)} %get-tuple-element.34), channel_id=1, source_target_pairs={{0,6},{1,7},{2,0},{3,1},{4,2},{5,3},{6,4},{7,5},{8,14},{9,15},{10,... | collective-permute-start | bytes 417800 | tf_op jit(solution)/shard_map/ppermute | solution.py:242
  24.7 6.0 %collective-permute-start.6 = (f16[2,136,256]{2,1,0:T(8,128)(2,1)S(1)}, f16[2,136,256]{2,1,0:T(8,128)(2,1)S(1)}, u32[]{:S(2)}, u32[]{:S(2)}) collective-permute-start(f16[2,136,256]{2,1,0:T(8,128)(2,1)S(1)} %select_convert_fusion.2), channel_id=1, source_target_pairs={{0,4},{1,5},{2,6},{3,7},{4,0},{5,1},{6,2},{7,3},{8,12},{9,13},{10,... | collective-permute-start | bytes 417800 | tf_op jit(solution)/shard_map/ppermute | solution.py:242
  25.1 7.2 %collective-permute-start.5 = (f16[2,136,256]{2,1,0:T(8,128)(2,1)S(1)}, f16[2,136,256]{2,1,0:T(8,128)(2,1)S(1)}, u32[]{:S(2)}, u32[]{:S(2)}) collective-permute-start(f16[2,136,256]{2,1,0:T(8,128)(2,1)S(1)} %get-tuple-element.33), channel_id=1, source_target_pairs={{0,2},{1,3},{2,4},{3,5},{4,6},{5,7},{6,0},{7,1},{8,10},{9,11},{10,... | collective-permute-start | bytes 417800 | tf_op jit(solution)/shard_map/ppermute | solution.py:242
  27.4 9.4 %collective-permute-start.9 = (bf16[4,2,128,256]{3,2,1,0:T(8,128)(2,1)S(1)}, bf16[4,2,128,256]{3,2,1,0:T(8,128)(2,1)S(1)}, u32[]{:S(2)}, u32[]{:S(2)}) collective-permute-start(bf16[4,2,128,256]{3,2,1,0:T(8,128)(2,1)S(1)} %collective-permute-done.8.q1), channel_id=1, source_target_pairs={{8,0},{33,1},{10,2},{35,3},{12,4},{37,5},{14,6},{39,7},{16,8},{41,... | collective-permute-start | bytes 1572872 | tf_op jit(solution)/shard_map/ppermute | solution.py:251
  32.9 6.7 %collective-permute-start.13 = (f16[2,136,256]{2,1,0:T(8,128)(2,1)S(1)}, f16[2,136,256]{2,1,0:T(8,128)(2,1)S(1)}, u32[]{:S(2)}, u32[]{:S(2)}) collective-permute-start(f16[2,136,256]{2,1,0:T(8,128)(2,1)S(1)} %get-tuple-element.31), channel_id=1, source_target_pairs={{0,2},{1,3},{2,4},{3,5},{4,6},{5,7},{6,0},{7,1},{8,10},{9,11},{10,... | collective-permute-start | bytes 417800 | tf_op jit(solution)/shard_map/ppermute | solution.py:257
  33.0 6.6 %collective-permute-start.12 = (f16[2,136,256]{2,1,0:T(8,128)(2,1)S(1)}, f16[2,136,256]{2,1,0:T(8,128)(2,1)S(1)}, u32[]{:S(2)}, u32[]{:S(2)}) collective-permute-start(f16[2,136,256]{2,1,0:T(8,128)(2,1)S(1)} %get-tuple-element.31), channel_id=1, source_target_pairs={{0,4},{1,5},{2,6},{3,7},{4,0},{5,1},{6,2},{7,3},{8,12},{9,13},{10,... | collective-permute-start | bytes 417800 | tf_op jit(solution)/shard_map/ppermute | solution.py:257
  35.3 5.1 %collective-permute-start.11 = (f16[2,136,256]{2,1,0:T(8,128)(2,1)S(1)}, f16[2,136,256]{2,1,0:T(8,128)(2,1)S(1)}, u32[]{:S(2)}, u32[]{:S(2)}) collective-permute-start(f16[2,136,256]{2,1,0:T(8,128)(2,1)S(1)} %get-tuple-element.31), channel_id=1, source_target_pairs={{0,6},{1,7},{2,0},{3,1},{4,2},{5,3},{6,4},{7,5},{8,14},{9,15},{10,... | collective-permute-start | bytes 417800 | tf_op jit(solution)/shard_map/ppermute | solution.py:257
  42.6 7.1 %collective-permute-start.14 = (f32[64,1024]{1,0:T(8,128)S(1)}, f32[64,1024]{1,0:T(8,128)S(1)}, u32[]{:S(2)}, u32[]{:S(2)}) collective-permute-start(f32[64,1024]{1,0:T(8,128)S(1)} %get-tuple-element.30), channel_id=1, source_target_pairs={{0,1},{1,0},{2,3},{3,2},{4,5},{5,4},{6,7},{7,6},{8,9},{9,8},{10,11... | collective-permute-start | bytes 786440 | tf_op jit(solution)/shard_map/ppermute | solution.py:260

commit v3 on v2

--- a/solution.py
+++ b/solution.py
@@ -10,6 +10,7 @@
 NT = (((1,), (1,)), ((), ()))
 PROJECT_VMEM = 61 * 2**20
 SCORE_VMEM = 24 * 2**20
+ORDER = (1, 3, 2)
 OWN_FLOPS = 12 * 10**9
 RING = 4
 WIDTH = 64
@@ -20,21 +21,25 @@
 TOP = 15.0
 
 
+def flip(v, d):
+    return (v, v + 1 - 2 * (v % 2), (v + 2) % 4, 3 - v)[d]
+
+
 def swap_perm():
     return [(y * 2 + c, y * 2 + 1 - c) for y in range(RING) for c in range(2)]
 
 
 def y_perm(d):
-    return [(y * 2 + c, ((y + d) % RING) * 2 + c) for y in range(RING) for c in range(2)]
-
-
-def xz_perm(d, flip):
+    return [(y * 2 + c, flip(y, d) * 2 + c) for y in range(RING) for c in range(2)]
+
+
+def xz_perm(d, other):
     pairs = []
     for x in range(RING):
         for z in range(RING):
             for t in range(2 * RING):
-                along_x = (t % 2 == 0) != flip
-                sx, sz = ((x + d) % RING, z) if along_x else (x, (z + d) % RING)
+                along_x = (t % 2 == 0) != other
+                sx, sz = (flip(x, d), z) if along_x else (x, flip(z, d))
                 pairs.append(((sx * RING + sz) * 2 * RING + t, (x * RING + z) * 2 * RING + t))
     return pairs
 
@@ -65,7 +70,7 @@
             slot = len(steps) % slots
             group = []
             for k in range(per):
-                rows = pl.ds(pl.multiple_of(lax.rem(y + s * per + k, QUART) * QTOK, QTOK), QTOK)
+                rows = pl.ds(pl.multiple_of(flip(y, s * per + k) * QTOK, QTOK), QTOK)
                 place = pl.ds(k * QTOK, QTOK)
                 group.append(pltpu.make_async_copy(acts.at[layer, rows, :], av.at[slot, place, :], sem_a.at[slot, k]))
                 group.append(pltpu.make_async_copy(grads.at[layer, rows, :], gv.at[slot, place, :], sem_g.at[slot, k]))
@@ -143,8 +148,8 @@
         outs = sums[j, WIDTH : 2 * WIDTH, :]
         for a in range(RING):
             for b in range(RING):
-                cx = lax.rem(x + jnp.where(core == 0, b, a), RING)
-                cz = lax.rem(z + jnp.where(core == 0, a, b), RING)
+                cx = jnp.where(core == 0, flip(x, b), flip(x, a))
+                cz = jnp.where(core == 0, flip(z, a), flip(z, b))
                 base = (cx * RING + cz) * 4
                 feats = jnp.concatenate(
                     [(sums[j, pl.ds(base + i, 1), :] * outs).astype(jnp.bfloat16) for i in range(4)], 0
@@ -162,7 +167,7 @@
     y = lax.axis_index("tensor") // 2
     for d, sums in enumerate((None, s1, s2, s3)):
         acc = own[...] if d == 0 else score_tokens(scale, sums, q0, q1, q2a, q2b, q3)
-        place = pl.ds(pl.multiple_of(lax.rem(y + d, QUART) * QTOK, QTOK), QTOK)
+        place = pl.ds(pl.multiple_of(flip(y, d) * QTOK, QTOK), QTOK)
         keep[:, place] = acc[0:WIDTH]
         give[:, place] = acc[WIDTH : 2 * WIDTH]
 
@@ -239,7 +244,9 @@
     part = [keep[d] + taken[d] for d in range(QUART)]
     power = [jnp.maximum(powers(keep[d]), powers(taken[d])) + 1.0 for d in range(QUART)]
     packed = [pack(part[d], power[d]) for d in range(1, QUART)]
-    sent = [lax.ppermute(packed[d - 1], "tensor", y_perm(d)) for d in range(1, QUART)]
+    sent = [None] * 3
+    for d in ORDER:
+        sent[d - 1] = lax.ppermute(packed[d - 1], "tensor", y_perm(d))
     plane1 = lax.ppermute(plane0, both, xz_perm(1, True))
     plane3 = lax.ppermute(plane0, both, xz_perm(3, True))
     total = part[0] + sum(unpack(m) for m in sent)
@@ -247,14 +254,14 @@
     for m in sent:
         top = jnp.maximum(top, powers(m))
     message = pack(total, top + 2.0)
-    plane1 = after(plane1, sent[2])
-    plane2 = lax.ppermute(plane1, both, xz_perm(1, True))
+    plane3 = after(plane3, sent[1])
+    plane2 = lax.ppermute(plane3, both, xz_perm(1, True))
     plane2 = (plane2[:2], plane2[2:])
     quers = [plane0, plane1, *plane2, plane3]
     own = own_score(total[:, : 2 * WIDTH], quers, scale)
-    sums = []
-    for d in range(1, QUART):
-        sums.append(unpack(after(lax.ppermute(message, "tensor", y_perm(-d)), own))[:, : 2 * WIDTH])
+    sums = [None] * 3
+    for d in ORDER:
+        sums[d - 1] = unpack(after(lax.ppermute(message, "tensor", y_perm(d)), own))[:, : 2 * WIDTH]
 
     keep_s, give_s = score(own, sums, quers, scale)
     return (keep_s + lax.ppermute(give_s, "tensor", swap_perm())).T

time: 50.5 us -> 48.7 us (0.964)
  starting transfers between devices: 25.3 us -> 20.4 us
  waiting for transfers between devices: 7.85 us -> 10.9 us
    ppermute x7, starting transfers between devices: 10.7 us -> 7.19 us  [the longest x3 3.85 us: local(): sent[d - 1] = lax.ppermute(packed[d - 1], 'tensor', y_perm(d))]
    ppermute x1, waiting for transfers between devices: 0.01 us -> 3.13 us  [local(): plane3 = lax.ppermute(plane0, both, xz_perm(3, True))]
    ppermute x1, starting transfers between devices: 5.89 us -> 3.47 us  [local(): return (keep_s + lax.ppermute(give_s, 'tensor', swap_perm())).T]
    ppermute x1, starting transfers between devices: 0.01 us -> 1.82 us  [local(): plane3 = lax.ppermute(plane0, both, xz_perm(3, True))]
    ppermute x1, waiting for transfers between devices: 1.59 us -> 0.01 us  [local(): plane1 = lax.ppermute(plane0, both, xz_perm(1, True))]
    ppermute x7, waiting for transfers between devices: 4.73 us -> 6.22 us  [the longest x3 2.4 us: local(): sent[d - 1] = lax.ppermute(packed[d - 1], 'tensor', y_perm(d))]
    ppermute x1, starting transfers between devices: 2.22 us -> 1.27 us  [local(): plane1 = lax.ppermute(plane0, both, xz_perm(1, True))]
  transfers between devices with their start and end apart: 15 -> 15, of which waited for: 7 -> 8; matrix products, arithmetic and copies ran while one was open for 7% -> 7% of each run, Pallas kernels for 21% -> 22%
where the time goes in v3:
time: 48.7 us; the launch traced here: 48.5 us
  starting transfers between devices  20.4 us (42%)
  Pallas kernels  12.4 us (25%)
  waiting for transfers between devices  10.9 us (22%)
  local copies, waits for them, and re-layouts  2.39 us (5%)
  other arithmetic  2.1 us (4%)
    pallas_call x1, Pallas kernels, project(): pl.pallas_call(functools.partial(project_kernel, chunk, slots), in_specs=...  9.75 us
    ppermute x3, starting transfers between devices, local(): lax.ppermute(line0, both, xz_perm(d, False))  5.11 us
    ppermute x3, starting transfers between devices, local(): sent[d - 1] = lax.ppermute(packed[d - 1], 'tensor', y_perm(d))  3.85 us
    ppermute x1, starting transfers between devices, local(): return (keep_s + lax.ppermute(give_s, 'tensor', swap_perm())).T  3.47 us
    ppermute x3, starting transfers between devices, local(): lax.ppermute(message, 'tensor', y_perm(d))  3.33 us
    ppermute x1, waiting for transfers between devices, local(): plane3 = lax.ppermute(plane0, both, xz_perm(3, True))  3.13 us
    ppermute x3, waiting for transfers between devices, local(): sent[d - 1] = lax.ppermute(packed[d - 1], 'tensor', y_perm(d))  2.4 us
    ppermute x1, waiting for transfers between devices, local(): plane2 = lax.ppermute(plane3, both, xz_perm(1, True))  2.01 us
  transfers between devices with their start and end apart: 15, of which 8 were waited for; matrix products, arithmetic and copies ran while one was open for 7% of the time, Pallas kernels for 22%

profile of v3, /device:TPU:1, one launch (start us, length us, event | category | flops | bytes accessed | tf_op | source)
XLA Modules:
  0.0 48.5 jit_solution(15926918359382697559)
XLA Ops:
  0.0 1.4 %collective-permute-start = (bf16[4,64,256]{2,1,0:T(8,128)(2,1)}, bf16[4,64,256]{2,1,0:T(8,128)(2,1)S(1)}, u32[]{:S(2)}, u32[]{:S(2)}) collective-permute-start(bf16[4,64,256]{2,1,0:T(8,128)(2,1)} %param.9), channel_id=1, source_target_pairs={{0,1},{1,0},{2,3},{3,2},{4,5},{5,4},{6,7},{7,6},{8,9},{9,8},{10,11... | collective-permute-start | bytes 393224 | tf_op jit(solution)/shard_map/ppermute | solution.py:235
  1.4 0.8 %constant_dynamic-slice_fusion.1 = bf16[2,64,256]{2,1,0:T(8,128)(2,1)S(1)} fusion(bf16[4,64,256]{2,1,0:T(8,128)(2,1)} %param.9, s32[]{:T(128)S(6)} %select_n.71), kind=kLoop, calls=%fused_computation.84 | loop fusion | bytes 131076 | tf_op jit(solution)/shard_map/dynamic_slice | solution.py:236
  2.3 0.4 collective-permute-done
  2.6 1.8 %collective-permute-start.1 = (bf16[2,128,256]{2,1,0:T(8,128)(2,1)S(1)}, bf16[2,128,256]{2,1,0:T(8,128)(2,1)S(1)}, u32[]{:S(2)}, u32[]{:S(2)}) collective-permute-start(bf16[2,128,256]{2,1,0:T(8,128)(2,1)S(1)} %pad_maximum_fusion.1), channel_id=1, source_target_pairs={{32,0},{9,1},{34,2},{11,3},{36,4},{13,5},{38,6},{15,7},{40,8},{1,9... | collective-permute-start | bytes 393224 | tf_op jit(solution)/shard_map/ppermute | solution.py:239
  4.4 3.3 %collective-permute-start.2 = (bf16[2,128,256]{2,1,0:T(8,128)(2,1)S(1)}, bf16[2,128,256]{2,1,0:T(8,128)(2,1)S(1)}, u32[]{:S(2)}, u32[]{:S(2)}) collective-permute-start(bf16[2,128,256]{2,1,0:T(8,128)(2,1)S(1)} %pad_maximum_fusion.1), channel_id=1, source_target_pairs={{64,0},{17,1},{66,2},{19,3},{68,4},{21,5},{70,6},{23,7},{72,8},{25... | collective-permute-start | bytes 393224 | tf_op jit(solution)/shard_map/ppermute | solution.py:239
  7.7 9.8 %project.1 = (f32[4,2,136,256]{3,2,1,0:T(8,128)}, f32[4,2,136,256]{3,2,1,0:T(8,128)}) custom-call(bf16[4,1024,512]{2,1,0:T(8,128)(2,1)} %acts.1, bf16[4,1024,1792]{2,1,0:T(8,128)(2,1)} %grads.1, bf16[4,64,512]{2,1,0:T(8,128)(2,1)} %p_in.1, bf16[4,64,1792]{2,1,0:T(8,128)(2,1)} %p_out.1), custom_call_target="tpu_custom_call" | custom-call | flops 1207959552 | bytes 18874368 | tf_op jit(solution)/shard_map/project/pallas_call | solution.py:112
  17.5 0.1 collective-permute-start.4
  17.7 1.3 %slice_bitcast_fusion.6 = (f32[2,136,256]{2,1,0:T(8,128)S(1)}, f32[2,136,256]{2,1,0:T(8,128)S(1)}, f32[2,136,256]{2,1,0:T(8,128)S(1)}, f32[2,136,256]{2,1,0:T(8,128)S(1)}) fusion(f32[4,2,136,256]{3,2,1,0:T(8,128)} %get-tuple-element.18), kind=kLoop, calls=%fused_computation.30 | loop fusion | bytes 2228224 | tf_op jit(solution)/shard_map/squeeze | solution.py:244
  19.1 0.1 pad_maximum_fusion.q0
  19.2 1.3 %collective-permute-start.8 = (bf16[4,2,128,256]{3,2,1,0:T(8,128)(2,1)S(1)}, bf16[4,2,128,256]{3,2,1,0:T(8,128)(2,1)S(1)}, u32[]{:S(2)}, u32[]{:S(2)}) collective-permute-start(bf16[4,2,128,256]{3,2,1,0:T(8,128)(2,1)S(1)} %pad_maximum_fusion.q0), channel_id=1, source_target_pairs={{8,0},{33,1},{10,2},{35,3},{12,4},{37,5},{14,6},{39,7},{0,8},{41,9... | collective-permute-start | bytes 1572872 | tf_op jit(solution)/shard_map/ppermute | solution.py:250
  20.4 1.8 %collective-permute-start.9 = (bf16[4,2,128,256]{3,2,1,0:T(8,128)(2,1)S(1)}, bf16[4,2,128,256]{3,2,1,0:T(8,128)(2,1)S(1)}, u32[]{:S(2)}, u32[]{:S(2)}) collective-permute-start(bf16[4,2,128,256]{3,2,1,0:T(8,128)(2,1)S(1)} %pad_maximum_fusion.q0), channel_id=1, source_target_pairs={{24,0},{97,1},{26,2},{99,3},{28,4},{101,5},{30,6},{103,7},{16,8},{... | collective-permute-start | bytes 1572872 | tf_op jit(solution)/shard_map/ppermute | solution.py:251
  22.3 0.1 slice_bitcast_fusion.2
  22.5 0.2 select_convert_fusion.2
  22.7 3.0 %collective-permute-start.6 = (f16[2,136,256]{2,1,0:T(8,128)(2,1)S(1)}, f16[2,136,256]{2,1,0:T(8,128)(2,1)S(1)}, u32[]{:S(2)}, u32[]{:S(2)}) collective-permute-start(f16[2,136,256]{2,1,0:T(8,128)(2,1)S(1)} %select_convert_fusion.2), channel_id=1, source_target_pairs={{0,4},{1,5},{2,6},{3,7},{4,0},{5,1},{6,2},{7,3},{8,12},{9,13},{10,... | collective-permute-start | bytes 417800 | tf_op jit(solution)/shard_map/ppermute | solution.py:249
  25.7 0.3 select_convert_fusion.3
  26.0 0.9 %collective-permute-start.7 = (f16[2,136,256]{2,1,0:T(8,128)(2,1)S(1)}, f16[2,136,256]{2,1,0:T(8,128)(2,1)S(1)}, u32[]{:S(2)}, u32[]{:S(2)}) collective-permute-start(f16[2,136,256]{2,1,0:T(8,128)(2,1)S(1)} %get-tuple-element.34), channel_id=1, source_target_pairs={{0,6},{1,7},{2,4},{3,5},{4,2},{5,3},{6,0},{7,1},{8,14},{9,15},{10,... | collective-permute-start | bytes 417800 | tf_op jit(solution)/shard_map/ppermute | solution.py:249
  26.8 3.1 %collective-permute-done.9.q3 = bf16[4,2,128,256]{3,2,1,0:T(8,128)(2,1)S(1)} collective-permute-done((bf16[4,2,128,256]{3,2,1,0:T(8,128)(2,1)S(1)}, bf16[4,2,128,256]{3,2,1,0:T(8,128)(2,1)S(1)}, u32[]{:S(2)}, u32[]{:S(2)}) %collective-permute-start.9) | collective-permute-done | bytes 524320 | tf_op jit(solution)/shard_map/ppermute | solution.py:251
  30.0 1.7 %collective-permute-done.7 = f16[2,136,256]{2,1,0:T(8,128)(2,1)S(1)} collective-permute-done((f16[2,136,256]{2,1,0:T(8,128)(2,1)S(1)}, f16[2,136,256]{2,1,0:T(8,128)(2,1)S(1)}, u32[]{:S(2)}, u32[]{:S(2)}) %collective-permute-start.7) | collective-permute-done | bytes 139296 | tf_op jit(solution)/shard_map/ppermute | solution.py:249
  31.7 0.7 %collective-permute-done.5 = f16[2,136,256]{2,1,0:T(8,128)(2,1)S(1)} collective-permute-done((f16[2,136,256]{2,1,0:T(8,128)(2,1)S(1)}, f16[2,136,256]{2,1,0:T(8,128)(2,1)S(1)}, u32[]{:S(2)}, u32[]{:S(2)}) %collective-permute-start.5) | collective-permute-done | bytes 139296 | tf_op jit(solution)/shard_map/ppermute | solution.py:249
  32.5 0.5 select_convert_fusion
  32.9 2.3 %collective-permute-start.13 = (f16[2,136,256]{2,1,0:T(8,128)(2,1)S(1)}, f16[2,136,256]{2,1,0:T(8,128)(2,1)S(1)}, u32[]{:S(2)}, u32[]{:S(2)}) collective-permute-start(f16[2,136,256]{2,1,0:T(8,128)(2,1)S(1)} %get-tuple-element.31), channel_id=1, source_target_pairs={{0,6},{1,7},{2,4},{3,5},{4,2},{5,3},{6,0},{7,1},{8,14},{9,15},{10,... | collective-permute-start | bytes 417800 | tf_op jit(solution)/shard_map/ppermute | solution.py:264
  35.2 0.4 collective-permute-start.12
  35.7 0.6 %collective-permute-start.11 = (f16[2,136,256]{2,1,0:T(8,128)(2,1)S(1)}, f16[2,136,256]{2,1,0:T(8,128)(2,1)S(1)}, u32[]{:S(2)}, u32[]{:S(2)}) collective-permute-start(f16[2,136,256]{2,1,0:T(8,128)(2,1)S(1)} %get-tuple-element.31), channel_id=1, source_target_pairs={{0,2},{1,3},{2,0},{3,1},{4,6},{5,7},{6,4},{7,5},{8,10},{9,11},{10,... | collective-permute-start | bytes 417800 | tf_op jit(solution)/shard_map/ppermute | solution.py:264
  36.3 2.0 %collective-permute-done.10 = bf16[4,2,128,256]{3,2,1,0:T(8,128)(2,1)S(1)} collective-permute-done((bf16[4,2,128,256]{3,2,1,0:T(8,128)(2,1)S(1)}, bf16[4,2,128,256]{3,2,1,0:T(8,128)(2,1)S(1)}, u32[]{:S(2)}, u32[]{:S(2)}) %collective-permute-start.10) | collective-permute-done | bytes 524320 | tf_op jit(solution)/shard_map/ppermute | solution.py:258
  38.4 0.8 %own_score.1.own = f32[128,256]{1,0:T(8,128)S(1)} custom-call(f32[2,128,256]{2,1,0:T(8,128)S(1)} %slice.204.s0, bf16[4,2,128,256]{3,2,1,0:T(8,128)(2,1)S(1)} %pad_maximum_fusion.q0, bf16[4,2,128,256]{3,2,1,0:T(8,128)(2,1)S(1)} %collective-permute-done.8.q1, bf16[2,2,128,256]{3,2,1,0:T(8,128)(2,1)S(1)} %get-tuple-element.44.q2a, ...), custom_call_target="tpu_custom_call" | custom-call | flops 12000000000 | bytes 4194304 | tf_op jit(solution)/shard_map/own_score/pallas_call | solution.py:177
  39.2 1.6 %collective-permute-done.12 = f16[2,136,256]{2,1,0:T(8,128)(2,1)S(1)} collective-permute-done((f16[2,136,256]{2,1,0:T(8,128)(2,1)S(1)}, f16[2,136,256]{2,1,0:T(8,128)(2,1)S(1)}, u32[]{:S(2)}, u32[]{:S(2)}) %collective-permute-start.12) | collective-permute-done | bytes 139296 | tf_op jit(solution)/shard_map/ppermute | solution.py:264
  40.8 0.2 collective-permute-done.11
  41.0 0.3 exponential_multiply_fusion
  41.3 1.9 %score.1 = (f32[64,1024]{1,0:T(8,128)S(1)}, f32[64,1024]{1,0:T(8,128)S(1)}) custom-call(f32[128,256]{1,0:T(8,128)S(1)} %own_score.1.own, f32[2,128,256]{2,1,0:T(8,128)S(1)} %get-tuple-element.75.s1, f32[2,128,256]{2,1,0:T(8,128)S(1)} %get-tuple-element.74.s2, f32[2,128,256]{2,1,0:T(8,128)S(1)} %get-tuple-element.73.s3, ...), custom_call_target="tpu_custom_call" | custom-call | flops 2147483648 | bytes 4194304 | tf_op jit(solution)/shard_map/score/pallas_call | solution.py:191
  43.2 3.5 %collective-permute-start.14 = (f32[64,1024]{1,0:T(8,128)S(1)}, f32[64,1024]{1,0:T(8,128)S(1)}, u32[]{:S(2)}, u32[]{:S(2)}) collective-permute-start(f32[64,1024]{1,0:T(8,128)S(1)} %get-tuple-element.30), channel_id=1, source_target_pairs={{0,1},{1,0},{2,3},{3,2},{4,5},{5,4},{6,7},{7,6},{8,9},{9,8},{10,11... | collective-permute-start | bytes 786440 | tf_op jit(solution)/shard_map/ppermute | solution.py:267
  46.6 1.2 %collective-permute-done.14 = f32[64,1024]{1,0:T(8,128)S(1)} collective-permute-done((f32[64,1024]{1,0:T(8,128)S(1)}, f32[64,1024]{1,0:T(8,128)S(1)}, u32[]{:S(2)}, u32[]{:S(2)}) %collective-permute-start.14) | collective-permute-done | bytes 262176 | tf_op jit(solution)/shard_map/ppermute | solution.py:267
  47.8 0.7 %add_bitcast_fusion = f32[1024,64]{0,1:T(8,128)} fusion(f32[64,1024]{1,0:T(8,128)S(1)} %get-tuple-element.29, f32[64,1024]{1,0:T(8,128)S(1)} %collective-permute-done.14), kind=kLoop, calls=%fused_computation.32 | loop fusion | flops 65536 | bytes 786432 | tf_op jit(solution)/shard_map/transpose | solution.py:267
  (55 shorter events, 0.2 us)
Async XLA Ops:
  0.0 2.6 %collective-permute-start = (bf16[4,64,256]{2,1,0:T(8,128)(2,1)}, bf16[4,64,256]{2,1,0:T(8,128)(2,1)S(1)}, u32[]{:S(2)}, u32[]{:S(2)}) collective-permute-start(bf16[4,64,256]{2,1,0:T(8,128)(2,1)} %param.9), channel_id=1, source_target_pairs={{0,1},{1,0},{2,3},{3,2},{4,5},{5,4},{6,7},{7,6},{8,9},{9,8},{10,11... | collective-permute-start | bytes 393224 | tf_op jit(solution)/shard_map/ppermute | solution.py:235
  2.6 14.9 %collective-permute-start.1 = (bf16[2,128,256]{2,1,0:T(8,128)(2,1)S(1)}, bf16[2,128,256]{2,1,0:T(8,128)(2,1)S(1)}, u32[]{:S(2)}, u32[]{:S(2)}) collective-permute-start(bf16[2,128,256]{2,1,0:T(8,128)(2,1)S(1)} %pad_maximum_fusion.1), channel_id=1, source_target_pairs={{32,0},{9,1},{34,2},{11,3},{36,4},{13,5},{38,6},{15,7},{40,8},{1,9... | collective-permute-start | bytes 393224 | tf_op jit(solution)/shard_map/ppermute | solution.py:239
  4.4 13.1 %collective-permute-start.2 = (bf16[2,128,256]{2,1,0:T(8,128)(2,1)S(1)}, bf16[2,128,256]{2,1,0:T(8,128)(2,1)S(1)}, u32[]{:S(2)}, u32[]{:S(2)}) collective-permute-start(bf16[2,128,256]{2,1,0:T(8,128)(2,1)S(1)} %pad_maximum_fusion.1), channel_id=1, source_target_pairs={{64,0},{17,1},{66,2},{19,3},{68,4},{21,5},{70,6},{23,7},{72,8},{25... | collective-permute-start | bytes 393224 | tf_op jit(solution)/shard_map/ppermute | solution.py:239
  7.7 9.8 %collective-permute-start.3 = (bf16[2,128,256]{2,1,0:T(8,128)(2,1)S(1)}, bf16[2,128,256]{2,1,0:T(8,128)(2,1)S(1)}, u32[]{:S(2)}, u32[]{:S(2)}) collective-permute-start(bf16[2,128,256]{2,1,0:T(8,128)(2,1)S(1)} %pad_maximum_fusion.1), channel_id=1, source_target_pairs={{96,0},{25,1},{98,2},{27,3},{100,4},{29,5},{102,6},{31,7},{104,8},... | collective-permute-start | bytes 393224 | tf_op jit(solution)/shard_map/ppermute | solution.py:239
  17.5 4.7 %collective-permute-start.4 = (f32[4,2,136,256]{3,2,1,0:T(8,128)}, f32[4,2,136,256]{3,2,1,0:T(8,128)S(1)}, u32[]{:S(2)}, u32[]{:S(2)}) collective-permute-start(f32[4,2,136,256]{3,2,1,0:T(8,128)} %get-tuple-element.20), channel_id=1, source_target_pairs={{0,1},{1,0},{2,3},{3,2},{4,5},{5,4},{6,7},{7,6},{8,9},{9,8},{10,11... | collective-permute-start | bytes 3342344 | tf_op jit(solution)/shard_map/ppermute | solution.py:243
  19.2 3.3 %copy-start = (f32[4,2,136,256]{3,2,1,0:T(8,128)S(1)}, f32[4,2,136,256]{3,2,1,0:T(8,128)}, u32[]{:S(2)}) copy-start(f32[4,2,136,256]{3,2,1,0:T(8,128)} %get-tuple-element.18) | copy-start | bytes 3342340
  19.2 19.2 %collective-permute-start.8 = (bf16[4,2,128,256]{3,2,1,0:T(8,128)(2,1)S(1)}, bf16[4,2,128,256]{3,2,1,0:T(8,128)(2,1)S(1)}, u32[]{:S(2)}, u32[]{:S(2)}) collective-permute-start(bf16[4,2,128,256]{3,2,1,0:T(8,128)(2,1)S(1)} %pad_maximum_fusion.q0), channel_id=1, source_target_pairs={{8,0},{33,1},{10,2},{35,3},{12,4},{37,5},{14,6},{39,7},{0,8},{41,9... | collective-permute-start | bytes 1572872 | tf_op jit(solution)/shard_map/ppermute | solution.py:250
  20.4 9.5 %collective-permute-start.9 = (bf16[4,2,128,256]{3,2,1,0:T(8,128)(2,1)S(1)}, bf16[4,2,128,256]{3,2,1,0:T(8,128)(2,1)S(1)}, u32[]{:S(2)}, u32[]{:S(2)}) collective-permute-start(bf16[4,2,128,256]{3,2,1,0:T(8,128)(2,1)S(1)} %pad_maximum_fusion.q0), channel_id=1, source_target_pairs={{24,0},{97,1},{26,2},{99,3},{28,4},{101,5},{30,6},{103,7},{16,8},{... | collective-permute-start | bytes 1572872 | tf_op jit(solution)/shard_map/ppermute | solution.py:251
  22.7 7.3 %collective-permute-start.6 = (f16[2,136,256]{2,1,0:T(8,128)(2,1)S(1)}, f16[2,136,256]{2,1,0:T(8,128)(2,1)S(1)}, u32[]{:S(2)}, u32[]{:S(2)}) collective-permute-start(f16[2,136,256]{2,1,0:T(8,128)(2,1)S(1)} %select_convert_fusion.2), channel_id=1, source_target_pairs={{0,4},{1,5},{2,6},{3,7},{4,0},{5,1},{6,2},{7,3},{8,12},{9,13},{10,... | collective-permute-start | bytes 417800 | tf_op jit(solution)/shard_map/ppermute | solution.py:249
  26.0 5.7 %collective-permute-start.7 = (f16[2,136,256]{2,1,0:T(8,128)(2,1)S(1)}, f16[2,136,256]{2,1,0:T(8,128)(2,1)S(1)}, u32[]{:S(2)}, u32[]{:S(2)}) collective-permute-start(f16[2,136,256]{2,1,0:T(8,128)(2,1)S(1)} %get-tuple-element.34), channel_id=1, source_target_pairs={{0,6},{1,7},{2,4},{3,5},{4,2},{5,3},{6,0},{7,1},{8,14},{9,15},{10,... | collective-permute-start | bytes 417800 | tf_op jit(solution)/shard_map/ppermute | solution.py:249
  26.8 5.6 %collective-permute-start.5 = (f16[2,136,256]{2,1,0:T(8,128)(2,1)S(1)}, f16[2,136,256]{2,1,0:T(8,128)(2,1)S(1)}, u32[]{:S(2)}, u32[]{:S(2)}) collective-permute-start(f16[2,136,256]{2,1,0:T(8,128)(2,1)S(1)} %get-tuple-element.33), channel_id=1, source_target_pairs={{0,2},{1,3},{2,0},{3,1},{4,6},{5,7},{6,4},{7,5},{8,10},{9,11},{10,... | collective-permute-start | bytes 417800 | tf_op jit(solution)/shard_map/ppermute | solution.py:249
  30.0 8.3 %collective-permute-start.10 = (bf16[4,2,128,256]{3,2,1,0:T(8,128)(2,1)S(1)}, bf16[4,2,128,256]{3,2,1,0:T(8,128)(2,1)S(1)}, u32[]{:S(2)}, u32[]{:S(2)}) collective-permute-start(bf16[4,2,128,256]{3,2,1,0:T(8,128)(2,1)S(1)} %collective-permute-done.9.q3), channel_id=1, source_target_pairs={{8,0},{33,1},{10,2},{35,3},{12,4},{37,5},{14,6},{39,7},{0,8},{41,9... | collective-permute-start | bytes 1572872 | tf_op jit(solution)/shard_map/ppermute | solution.py:258
  32.9 6.2 %collective-permute-start.13 = (f16[2,136,256]{2,1,0:T(8,128)(2,1)S(1)}, f16[2,136,256]{2,1,0:T(8,128)(2,1)S(1)}, u32[]{:S(2)}, u32[]{:S(2)}) collective-permute-start(f16[2,136,256]{2,1,0:T(8,128)(2,1)S(1)} %get-tuple-element.31), channel_id=1, source_target_pairs={{0,6},{1,7},{2,4},{3,5},{4,2},{5,3},{6,0},{7,1},{8,14},{9,15},{10,... | collective-permute-start | bytes 417800 | tf_op jit(solution)/shard_map/ppermute | solution.py:264
  35.2 5.5 %collective-permute-start.12 = (f16[2,136,256]{2,1,0:T(8,128)(2,1)S(1)}, f16[2,136,256]{2,1,0:T(8,128)(2,1)S(1)}, u32[]{:S(2)}, u32[]{:S(2)}) collective-permute-start(f16[2,136,256]{2,1,0:T(8,128)(2,1)S(1)} %get-tuple-element.31), channel_id=1, source_target_pairs={{0,4},{1,5},{2,6},{3,7},{4,0},{5,1},{6,2},{7,3},{8,12},{9,13},{10,... | collective-permute-start | bytes 417800 | tf_op jit(solution)/shard_map/ppermute | solution.py:264
  35.7 5.3 %collective-permute-start.11 = (f16[2,136,256]{2,1,0:T(8,128)(2,1)S(1)}, f16[2,136,256]{2,1,0:T(8,128)(2,1)S(1)}, u32[]{:S(2)}, u32[]{:S(2)}) collective-permute-start(f16[2,136,256]{2,1,0:T(8,128)(2,1)S(1)} %get-tuple-element.31), channel_id=1, source_target_pairs={{0,2},{1,3},{2,0},{3,1},{4,6},{5,7},{6,4},{7,5},{8,10},{9,11},{10,... | collective-permute-start | bytes 417800 | tf_op jit(solution)/shard_map/ppermute | solution.py:264
  43.2 4.6 %collective-permute-start.14 = (f32[64,1024]{1,0:T(8,128)S(1)}, f32[64,1024]{1,0:T(8,128)S(1)}, u32[]{:S(2)}, u32[]{:S(2)}) collective-permute-start(f32[64,1024]{1,0:T(8,128)S(1)} %get-tuple-element.30), channel_id=1, source_target_pairs={{0,1},{1,0},{2,3},{3,2},{4,5},{5,4},{6,7},{7,6},{8,9},{9,8},{10,11... | collective-permute-start | bytes 786440 | tf_op jit(solution)/shard_map/ppermute | solution.py:267

commit v4 on v3

--- a/solution.py
+++ b/solution.py
@@ -133,15 +133,13 @@
     )(acts, grads, p_in, p_out)
 
 
-def score_tokens(scale, sums, q0, q1, q2a, q2b, q3):
+def score_tokens(scale, sums, q0, q1, q3, q2):
     core = lax.axis_index("tensor") % 2
     chip = lax.axis_index("dp")
     x, z = chip // RING, chip % RING
 
     def query(a, b, j):
-        if a == 2:
-            return (q2a if b < 2 else q2b)[b % 2, j]
-        return (q0, q1, None, q3)[a][b, j]
+        return (q0, q1, q2, q3)[a][b, j]
 
     acc = None
     for j in range(2):
@@ -159,14 +157,14 @@
     return acc * scale
 
 
-def own_score_kernel(scale, s0, q0, q1, q2a, q2b, q3, out):
-    out[...] = score_tokens(scale, s0, q0, q1, q2a, q2b, q3)
-
-
-def score_kernel(scale, own, s1, s2, s3, q0, q1, q2a, q2b, q3, keep, give):
+def own_score_kernel(scale, s0, q0, q1, q3, q2, out):
+    out[...] = score_tokens(scale, s0, q0, q1, q3, q2)
+
+
+def score_kernel(scale, own, s1, s2, s3, q0, q1, q3, q2, keep, give):
     y = lax.axis_index("tensor") // 2
     for d, sums in enumerate((None, s1, s2, s3)):
-        acc = own[...] if d == 0 else score_tokens(scale, sums, q0, q1, q2a, q2b, q3)
+        acc = own[...] if d == 0 else score_tokens(scale, sums, q0, q1, q3, q2)
         place = pl.ds(pl.multiple_of(flip(y, d) * QTOK, QTOK), QTOK)
         keep[:, place] = acc[0:WIDTH]
         give[:, place] = acc[WIDTH : 2 * WIDTH]
@@ -176,7 +174,7 @@
     vm = pl.BlockSpec(memory_space=pltpu.VMEM)
     return pl.pallas_call(
         functools.partial(own_score_kernel, scale),
-        in_specs=[vm] * 6,
+        in_specs=[vm] * 5,
         out_specs=vm,
         out_shape=jax.ShapeDtypeStruct((2 * WIDTH, QTOK), jnp.float32),
         compiler_params=pltpu.CompilerParams(vmem_limit_bytes=SCORE_VMEM),
@@ -190,7 +188,7 @@
     shape = jax.ShapeDtypeStruct((WIDTH, QUART * QTOK), jnp.float32)
     return pl.pallas_call(
         functools.partial(score_kernel, scale),
-        in_specs=[vm] * 9,
+        in_specs=[vm] * 8,
         out_specs=[vm] * 2,
         out_shape=[shape] * 2,
         compiler_params=pltpu.CompilerParams(vmem_limit_bytes=SCORE_VMEM),
@@ -248,16 +246,13 @@
     for d in ORDER:
         sent[d - 1] = lax.ppermute(packed[d - 1], "tensor", y_perm(d))
     plane1 = lax.ppermute(plane0, both, xz_perm(1, True))
-    plane3 = lax.ppermute(plane0, both, xz_perm(3, True))
     total = part[0] + sum(unpack(m) for m in sent)
     top = power[0]
     for m in sent:
         top = jnp.maximum(top, powers(m))
     message = pack(total, top + 2.0)
-    plane3 = after(plane3, sent[1])
-    plane2 = lax.ppermute(plane3, both, xz_perm(1, True))
-    plane2 = (plane2[:2], plane2[2:])
-    quers = [plane0, plane1, *plane2, plane3]
+    late = [lax.ppermute(p, both, xz_perm(3, True)) for p in (after(plane0, packed[2]), after(plane1, sent[1]))]
+    quers = [plane0, plane1, *late]
     own = own_score(total[:, : 2 * WIDTH], quers, scale)
     sums = [None] * 3
     for d in ORDER:

time: 48.7 us -> 47.5 us (0.975)
  waiting for transfers between devices: 10.9 us -> 7.4 us
  starting transfers between devices: 20.4 us -> 22.6 us
    ppermute x2, starting transfers between devices: 1.82 us -> 4.88 us  [local(): lax.ppermute(p, both, xz_perm(3, True))]
    ppermute x3, waiting for transfers between devices: 2.4 us -> 0.59 us  [local(): sent[d - 1] = lax.ppermute(packed[d - 1], 'tensor', y_perm(d))]
    ppermute x3, waiting for transfers between devices: 1.81 us -> 0.01 us  [local(): lax.ppermute(message, 'tensor', y_perm(d))]
    ppermute x1, starting transfers between devices: 3.47 us -> 2.58 us  [local(): return (keep_s + lax.ppermute(give_s, 'tensor', swap_perm())).T]
    ppermute x3, starting transfers between devices: 3.33 us -> 3.92 us  [local(): lax.ppermute(message, 'tensor', y_perm(d))]
    ppermute x3, starting transfers between devices: 5.11 us -> 4.59 us  [local(): lax.ppermute(line0, both, xz_perm(d, False))]
  transfers between devices with their start and end apart: 15 -> 15, of which waited for: 8 -> 5; matrix products, arithmetic and copies ran while one was open for 7% -> 7% of each run, Pallas kernels for 22% -> 22%
where the time goes in v4:
time: 47.5 us; the launch traced here: 47.3 us
  starting transfers between devices  22.6 us (48%)
  Pallas kernels  12.4 us (26%)
  waiting for transfers between devices  7.4 us (16%)
  local copies, waits for them, and re-layouts  2.36 us (5%)
  other arithmetic  2.09 us (4%)
    pallas_call x1, Pallas kernels, project(): pl.pallas_call(functools.partial(project_kernel, chunk, slots), in_specs=...  9.76 us
    ppermute x2, waiting for transfers between devices, local(): lax.ppermute(p, both, xz_perm(3, True))  5.15 us
    ppermute x2, starting transfers between devices, local(): lax.ppermute(p, both, xz_perm(3, True))  4.88 us
    ppermute x3, starting transfers between devices, local(): lax.ppermute(line0, both, xz_perm(d, False))  4.59 us
    ppermute x3, starting transfers between devices, local(): lax.ppermute(message, 'tensor', y_perm(d))  3.92 us
    ppermute x3, starting transfers between devices, local(): sent[d - 1] = lax.ppermute(packed[d - 1], 'tensor', y_perm(d))  3.85 us
    ppermute x1, starting transfers between devices, local(): return (keep_s + lax.ppermute(give_s, 'tensor', swap_perm())).T  2.58 us
    pallas_call x1, Pallas kernels, score(): pl.pallas_call(functools.partial(score_kernel, scale), in_specs=[vm] * 8,...  1.88 us
  transfers between devices with their start and end apart: 15, of which 5 were waited for; matrix products, arithmetic and copies ran while one was open for 7% of the time, Pallas kernels for 22%

profile of v4, /device:TPU:1, one launch (start us, length us, event | category | flops | bytes accessed | tf_op | source)
XLA Modules:
  0.0 47.3 jit_solution(453806656211884866)
XLA Ops:
  0.0 1.4 %collective-permute-start = (bf16[4,64,256]{2,1,0:T(8,128)(2,1)}, bf16[4,64,256]{2,1,0:T(8,128)(2,1)S(1)}, u32[]{:S(2)}, u32[]{:S(2)}) collective-permute-start(bf16[4,64,256]{2,1,0:T(8,128)(2,1)} %param.9), channel_id=1, source_target_pairs={{0,1},{1,0},{2,3},{3,2},{4,5},{5,4},{6,7},{7,6},{8,9},{9,8},{10,11... | collective-permute-start | bytes 393224 | tf_op jit(solution)/shard_map/ppermute | solution.py:233
  1.4 0.8 %constant_dynamic-slice_fusion.1 = bf16[2,64,256]{2,1,0:T(8,128)(2,1)S(1)} fusion(bf16[4,64,256]{2,1,0:T(8,128)(2,1)} %param.9, s32[]{:T(128)S(6)} %select_n.71), kind=kLoop, calls=%fused_computation.84 | loop fusion | bytes 131076 | tf_op jit(solution)/shard_map/dynamic_slice | solution.py:234
  2.3 0.4 collective-permute-done
  2.6 3.9 %collective-permute-start.3 = (bf16[2,128,256]{2,1,0:T(8,128)(2,1)S(1)}, bf16[2,128,256]{2,1,0:T(8,128)(2,1)S(1)}, u32[]{:S(2)}, u32[]{:S(2)}) collective-permute-start(bf16[2,128,256]{2,1,0:T(8,128)(2,1)S(1)} %pad_maximum_fusion.1), channel_id=1, source_target_pairs={{96,0},{25,1},{98,2},{27,3},{100,4},{29,5},{102,6},{31,7},{104,8},... | collective-permute-start | bytes 393224 | tf_op jit(solution)/shard_map/ppermute | solution.py:237
  6.6 0.7 %collective-permute-start.1 = (bf16[2,128,256]{2,1,0:T(8,128)(2,1)S(1)}, bf16[2,128,256]{2,1,0:T(8,128)(2,1)S(1)}, u32[]{:S(2)}, u32[]{:S(2)}) collective-permute-start(bf16[2,128,256]{2,1,0:T(8,128)(2,1)S(1)} %pad_maximum_fusion.1), channel_id=1, source_target_pairs={{32,0},{9,1},{34,2},{11,3},{36,4},{13,5},{38,6},{15,7},{40,8},{1,9... | collective-permute-start | bytes 393224 | tf_op jit(solution)/shard_map/ppermute | solution.py:237
  7.2 9.8 %project.1 = (f32[4,2,136,256]{3,2,1,0:T(8,128)}, f32[4,2,136,256]{3,2,1,0:T(8,128)}) custom-call(bf16[4,1024,512]{2,1,0:T(8,128)(2,1)} %acts.1, bf16[4,1024,1792]{2,1,0:T(8,128)(2,1)} %grads.1, bf16[4,64,512]{2,1,0:T(8,128)(2,1)} %p_in.1, bf16[4,64,1792]{2,1,0:T(8,128)(2,1)} %p_out.1), custom_call_target="tpu_custom_call" | custom-call | flops 1207959552 | bytes 18874368 | tf_op jit(solution)/shard_map/project/pallas_call | solution.py:112
  17.0 0.0 collective-permute-done.3
  17.0 0.0 collective-permute-done.2
  17.0 0.1 collective-permute-start.4
  17.1 1.3 %slice_bitcast_fusion.6 = (f32[2,136,256]{2,1,0:T(8,128)S(1)}, f32[2,136,256]{2,1,0:T(8,128)S(1)}, f32[2,136,256]{2,1,0:T(8,128)S(1)}, f32[2,136,256]{2,1,0:T(8,128)S(1)}) fusion(f32[4,2,136,256]{3,2,1,0:T(8,128)} %get-tuple-element.19), kind=kLoop, calls=%fused_computation.30 | loop fusion | bytes 2228224 | tf_op jit(solution)/shard_map/squeeze | solution.py:242
  18.6 0.1 pad_maximum_fusion.q0
  18.6 1.3 %collective-permute-start.8 = (bf16[4,2,128,256]{3,2,1,0:T(8,128)(2,1)S(1)}, bf16[4,2,128,256]{3,2,1,0:T(8,128)(2,1)S(1)}, u32[]{:S(2)}, u32[]{:S(2)}) collective-permute-start(bf16[4,2,128,256]{3,2,1,0:T(8,128)(2,1)S(1)} %pad_maximum_fusion.q0), channel_id=1, source_target_pairs={{8,0},{33,1},{10,2},{35,3},{12,4},{37,5},{14,6},{39,7},{0,8},{41,9... | collective-permute-start | bytes 1572872 | tf_op jit(solution)/shard_map/ppermute | solution.py:248
  19.9 0.1 collective-permute-done.4
  20.1 0.1 slice_bitcast_fusion.2
  20.3 0.2 select_convert_fusion.2
  20.5 3.0 %collective-permute-start.6 = (f16[2,136,256]{2,1,0:T(8,128)(2,1)S(1)}, f16[2,136,256]{2,1,0:T(8,128)(2,1)S(1)}, u32[]{:S(2)}, u32[]{:S(2)}) collective-permute-start(f16[2,136,256]{2,1,0:T(8,128)(2,1)S(1)} %select_convert_fusion.2), channel_id=1, source_target_pairs={{0,4},{1,5},{2,6},{3,7},{4,0},{5,1},{6,2},{7,3},{8,12},{9,13},{10,... | collective-permute-start | bytes 417800 | tf_op jit(solution)/shard_map/ppermute | solution.py:247
  23.5 0.3 select_convert_fusion.3
  23.8 0.9 %collective-permute-start.7 = (f16[2,136,256]{2,1,0:T(8,128)(2,1)S(1)}, f16[2,136,256]{2,1,0:T(8,128)(2,1)S(1)}, u32[]{:S(2)}, u32[]{:S(2)}) collective-permute-start(f16[2,136,256]{2,1,0:T(8,128)(2,1)S(1)} %get-tuple-element.36), channel_id=1, source_target_pairs={{0,6},{1,7},{2,4},{3,5},{4,2},{5,3},{6,0},{7,1},{8,14},{9,15},{10,... | collective-permute-start | bytes 417800 | tf_op jit(solution)/shard_map/ppermute | solution.py:247
  24.7 2.5 %collective-permute-start.9 = (bf16[4,2,128,256]{3,2,1,0:T(8,128)(2,1)S(1)}, bf16[4,2,128,256]{3,2,1,0:T(8,128)(2,1)S(1)}, u32[]{:S(2)}, u32[]{:S(2)}) collective-permute-start(bf16[4,2,128,256]{3,2,1,0:T(8,128)(2,1)S(1)} %pad_maximum_fusion.q0), channel_id=1, source_target_pairs={{24,0},{97,1},{26,2},{99,3},{28,4},{101,5},{30,6},{103,7},{16,8},{... | collective-permute-start | bytes 1572872 | tf_op jit(solution)/shard_map/ppermute | solution.py:254
  27.1 2.4 %collective-permute-start.10 = (bf16[4,2,128,256]{3,2,1,0:T(8,128)(2,1)S(1)}, bf16[4,2,128,256]{3,2,1,0:T(8,128)(2,1)S(1)}, u32[]{:S(2)}, u32[]{:S(2)}) collective-permute-start(bf16[4,2,128,256]{3,2,1,0:T(8,128)(2,1)S(1)} %collective-permute-done.8.q1), channel_id=1, source_target_pairs={{24,0},{97,1},{26,2},{99,3},{28,4},{101,5},{30,6},{103,7},{16,8},{... | collective-permute-start | bytes 1572872 | tf_op jit(solution)/shard_map/ppermute | solution.py:254
  29.5 0.6 %collective-permute-done.5 = f16[2,136,256]{2,1,0:T(8,128)(2,1)S(1)} collective-permute-done((f16[2,136,256]{2,1,0:T(8,128)(2,1)S(1)}, f16[2,136,256]{2,1,0:T(8,128)(2,1)S(1)}, u32[]{:S(2)}, u32[]{:S(2)}) %collective-permute-start.5) | collective-permute-done | bytes 139296 | tf_op jit(solution)/shard_map/ppermute | solution.py:247
  30.2 0.5 %select_convert_fusion = (f16[2,136,256]{2,1,0:T(8,128)(2,1)S(1)}, f32[2,136,256]{2,1,0:T(8,128)S(1)}) fusion(f32[2,256]{1,0:T(2,128)S(1)} %bitcast.137, f32[2,256]{1,0:T(2,128)S(1)} %bitcast.138, f32[2,256]{1,0:T(2,128)S(1)} %bitcast.129, f32[2,256]{1,0:T(2,128)S(1)} %bitcast.130, f32[2,256]{1,0:T(2,128)S(1)} %bitcast.152, f32[2,256]{1,0:T(2,128)S(1)} %bitcast.150, ...), kind=kLoop, calls=%fused_computation.24 | loop fusion | flops 2228224 | bytes 1413392 | tf_op jit(solution)/shard_map/convert_element_type | solution.py:219
  30.7 3.3 %collective-permute-start.13 = (f16[2,136,256]{2,1,0:T(8,128)(2,1)S(1)}, f16[2,136,256]{2,1,0:T(8,128)(2,1)S(1)}, u32[]{:S(2)}, u32[]{:S(2)}) collective-permute-start(f16[2,136,256]{2,1,0:T(8,128)(2,1)S(1)} %get-tuple-element.33), channel_id=1, source_target_pairs={{0,6},{1,7},{2,4},{3,5},{4,2},{5,3},{6,0},{7,1},{8,14},{9,15},{10,... | collective-permute-start | bytes 417800 | tf_op jit(solution)/shard_map/ppermute | solution.py:259
  34.0 0.4 collective-permute-start.12
  34.3 0.3 collective-permute-start.11
  34.7 5.1 %collective-permute-done.10.q2 = bf16[4,2,128,256]{3,2,1,0:T(8,128)(2,1)S(1)} collective-permute-done((bf16[4,2,128,256]{3,2,1,0:T(8,128)(2,1)S(1)}, bf16[4,2,128,256]{3,2,1,0:T(8,128)(2,1)S(1)}, u32[]{:S(2)}, u32[]{:S(2)}) %collective-permute-start.10) | collective-permute-done | bytes 524320 | tf_op jit(solution)/shard_map/ppermute | solution.py:254
  39.8 0.7 %own_score.1.own = f32[128,256]{1,0:T(8,128)S(1)} custom-call(f32[2,128,256]{2,1,0:T(8,128)S(1)} %slice.196.s0, bf16[4,2,128,256]{3,2,1,0:T(8,128)(2,1)S(1)} %pad_maximum_fusion.q0, bf16[4,2,128,256]{3,2,1,0:T(8,128)(2,1)S(1)} %collective-permute-done.8.q1, bf16[4,2,128,256]{3,2,1,0:T(8,128)(2,1)S(1)} %collective-permute-done.9.q3, ...), custom_call_target="tpu_custom_call" | custom-call | flops 12000000000 | bytes 4194304 | tf_op jit(solution)/shard_map/own_score/pallas_call | solution.py:175
  40.7 0.3 exponential_multiply_fusion
  41.0 1.9 %score.1 = (f32[64,1024]{1,0:T(8,128)S(1)}, f32[64,1024]{1,0:T(8,128)S(1)}) custom-call(f32[128,256]{1,0:T(8,128)S(1)} %own_score.1.own, f32[2,128,256]{2,1,0:T(8,128)S(1)} %get-tuple-element.75.s1, f32[2,128,256]{2,1,0:T(8,128)S(1)} %get-tuple-element.74.s2, f32[2,128,256]{2,1,0:T(8,128)S(1)} %get-tuple-element.73.s3, ...), custom_call_target="tpu_custom_call" | custom-call | flops 2147483648 | bytes 4194304 | tf_op jit(solution)/shard_map/score/pallas_call | solution.py:189
  42.8 2.6 %collective-permute-start.14 = (f32[64,1024]{1,0:T(8,128)S(1)}, f32[64,1024]{1,0:T(8,128)S(1)}, u32[]{:S(2)}, u32[]{:S(2)}) collective-permute-start(f32[64,1024]{1,0:T(8,128)S(1)} %get-tuple-element.32), channel_id=1, source_target_pairs={{0,1},{1,0},{2,3},{3,2},{4,5},{5,4},{6,7},{7,6},{8,9},{9,8},{10,11... | collective-permute-start | bytes 786440 | tf_op jit(solution)/shard_map/ppermute | solution.py:262
  45.4 1.2 %collective-permute-done.14 = f32[64,1024]{1,0:T(8,128)S(1)} collective-permute-done((f32[64,1024]{1,0:T(8,128)S(1)}, f32[64,1024]{1,0:T(8,128)S(1)}, u32[]{:S(2)}, u32[]{:S(2)}) %collective-permute-start.14) | collective-permute-done | bytes 262176 | tf_op jit(solution)/shard_map/ppermute | solution.py:262
  46.6 0.7 %add_bitcast_fusion = f32[1024,64]{0,1:T(8,128)} fusion(f32[64,1024]{1,0:T(8,128)S(1)} %get-tuple-element.31, f32[64,1024]{1,0:T(8,128)S(1)} %collective-permute-done.14), kind=kLoop, calls=%fused_computation.32 | loop fusion | flops 65536 | bytes 786432 | tf_op jit(solution)/shard_map/transpose | solution.py:262
  (54 shorter events, 0.2 us)
Async XLA Ops:
  0.0 2.6 %collective-permute-start = (bf16[4,64,256]{2,1,0:T(8,128)(2,1)}, bf16[4,64,256]{2,1,0:T(8,128)(2,1)S(1)}, u32[]{:S(2)}, u32[]{:S(2)}) collective-permute-start(bf16[4,64,256]{2,1,0:T(8,128)(2,1)} %param.9), channel_id=1, source_target_pairs={{0,1},{1,0},{2,3},{3,2},{4,5},{5,4},{6,7},{7,6},{8,9},{9,8},{10,11... | collective-permute-start | bytes 393224 | tf_op jit(solution)/shard_map/ppermute | solution.py:233
  2.6 14.4 %collective-permute-start.3 = (bf16[2,128,256]{2,1,0:T(8,128)(2,1)S(1)}, bf16[2,128,256]{2,1,0:T(8,128)(2,1)S(1)}, u32[]{:S(2)}, u32[]{:S(2)}) collective-permute-start(bf16[2,128,256]{2,1,0:T(8,128)(2,1)S(1)} %pad_maximum_fusion.1), channel_id=1, source_target_pairs={{96,0},{25,1},{98,2},{27,3},{100,4},{29,5},{102,6},{31,7},{104,8},... | collective-permute-start | bytes 393224 | tf_op jit(solution)/shard_map/ppermute | solution.py:237
  6.6 10.5 %collective-permute-start.2 = (bf16[2,128,256]{2,1,0:T(8,128)(2,1)S(1)}, bf16[2,128,256]{2,1,0:T(8,128)(2,1)S(1)}, u32[]{:S(2)}, u32[]{:S(2)}) collective-permute-start(bf16[2,128,256]{2,1,0:T(8,128)(2,1)S(1)} %pad_maximum_fusion.1), channel_id=1, source_target_pairs={{64,0},{17,1},{66,2},{19,3},{68,4},{21,5},{70,6},{23,7},{72,8},{25... | collective-permute-start | bytes 393224 | tf_op jit(solution)/shard_map/ppermute | solution.py:237
  6.6 10.5 %collective-permute-start.1 = (bf16[2,128,256]{2,1,0:T(8,128)(2,1)S(1)}, bf16[2,128,256]{2,1,0:T(8,128)(2,1)S(1)}, u32[]{:S(2)}, u32[]{:S(2)}) collective-permute-start(bf16[2,128,256]{2,1,0:T(8,128)(2,1)S(1)} %pad_maximum_fusion.1), channel_id=1, source_target_pairs={{32,0},{9,1},{34,2},{11,3},{36,4},{13,5},{38,6},{15,7},{40,8},{1,9... | collective-permute-start | bytes 393224 | tf_op jit(solution)/shard_map/ppermute | solution.py:237
  17.0 3.0 %collective-permute-start.4 = (f32[4,2,136,256]{3,2,1,0:T(8,128)}, f32[4,2,136,256]{3,2,1,0:T(8,128)S(1)}, u32[]{:S(2)}, u32[]{:S(2)}) collective-permute-start(f32[4,2,136,256]{3,2,1,0:T(8,128)} %get-tuple-element.21), channel_id=1, source_target_pairs={{0,1},{1,0},{2,3},{3,2},{4,5},{5,4},{6,7},{7,6},{8,9},{9,8},{10,11... | collective-permute-start | bytes 3342344 | tf_op jit(solution)/shard_map/ppermute | solution.py:241
  18.6 1.6 %copy-start = (f32[4,2,136,256]{3,2,1,0:T(8,128)S(1)}, f32[4,2,136,256]{3,2,1,0:T(8,128)}, u32[]{:S(2)}) copy-start(f32[4,2,136,256]{3,2,1,0:T(8,128)} %get-tuple-element.19) | copy-start | bytes 3342340
  18.6 8.5 %collective-permute-start.8 = (bf16[4,2,128,256]{3,2,1,0:T(8,128)(2,1)S(1)}, bf16[4,2,128,256]{3,2,1,0:T(8,128)(2,1)S(1)}, u32[]{:S(2)}, u32[]{:S(2)}) collective-permute-start(bf16[4,2,128,256]{3,2,1,0:T(8,128)(2,1)S(1)} %pad_maximum_fusion.q0), channel_id=1, source_target_pairs={{8,0},{33,1},{10,2},{35,3},{12,4},{37,5},{14,6},{39,7},{0,8},{41,9... | collective-permute-start | bytes 1572872 | tf_op jit(solution)/shard_map/ppermute | solution.py:248
  20.5 6.7 %collective-permute-start.6 = (f16[2,136,256]{2,1,0:T(8,128)(2,1)S(1)}, f16[2,136,256]{2,1,0:T(8,128)(2,1)S(1)}, u32[]{:S(2)}, u32[]{:S(2)}) collective-permute-start(f16[2,136,256]{2,1,0:T(8,128)(2,1)S(1)} %select_convert_fusion.2), channel_id=1, source_target_pairs={{0,4},{1,5},{2,6},{3,7},{4,0},{5,1},{6,2},{7,3},{8,12},{9,13},{10,... | collective-permute-start | bytes 417800 | tf_op jit(solution)/shard_map/ppermute | solution.py:247
  23.8 6.4 %collective-permute-start.7 = (f16[2,136,256]{2,1,0:T(8,128)(2,1)S(1)}, f16[2,136,256]{2,1,0:T(8,128)(2,1)S(1)}, u32[]{:S(2)}, u32[]{:S(2)}) collective-permute-start(f16[2,136,256]{2,1,0:T(8,128)(2,1)S(1)} %get-tuple-element.36), channel_id=1, source_target_pairs={{0,6},{1,7},{2,4},{3,5},{4,2},{5,3},{6,0},{7,1},{8,14},{9,15},{10,... | collective-permute-start | bytes 417800 | tf_op jit(solution)/shard_map/ppermute | solution.py:247
  24.6 5.5 %collective-permute-start.5 = (f16[2,136,256]{2,1,0:T(8,128)(2,1)S(1)}, f16[2,136,256]{2,1,0:T(8,128)(2,1)S(1)}, u32[]{:S(2)}, u32[]{:S(2)}) collective-permute-start(f16[2,136,256]{2,1,0:T(8,128)(2,1)S(1)} %get-tuple-element.35), channel_id=1, source_target_pairs={{0,2},{1,3},{2,0},{3,1},{4,6},{5,7},{6,4},{7,5},{8,10},{9,11},{10,... | collective-permute-start | bytes 417800 | tf_op jit(solution)/shard_map/ppermute | solution.py:247
  24.7 10.0 %collective-permute-start.9 = (bf16[4,2,128,256]{3,2,1,0:T(8,128)(2,1)S(1)}, bf16[4,2,128,256]{3,2,1,0:T(8,128)(2,1)S(1)}, u32[]{:S(2)}, u32[]{:S(2)}) collective-permute-start(bf16[4,2,128,256]{3,2,1,0:T(8,128)(2,1)S(1)} %pad_maximum_fusion.q0), channel_id=1, source_target_pairs={{24,0},{97,1},{26,2},{99,3},{28,4},{101,5},{30,6},{103,7},{16,8},{... | collective-permute-start | bytes 1572872 | tf_op jit(solution)/shard_map/ppermute | solution.py:254
  27.1 12.7 %collective-permute-start.10 = (bf16[4,2,128,256]{3,2,1,0:T(8,128)(2,1)S(1)}, bf16[4,2,128,256]{3,2,1,0:T(8,128)(2,1)S(1)}, u32[]{:S(2)}, u32[]{:S(2)}) collective-permute-start(bf16[4,2,128,256]{3,2,1,0:T(8,128)(2,1)S(1)} %collective-permute-done.8.q1), channel_id=1, source_target_pairs={{24,0},{97,1},{26,2},{99,3},{28,4},{101,5},{30,6},{103,7},{16,8},{... | collective-permute-start | bytes 1572872 | tf_op jit(solution)/shard_map/ppermute | solution.py:254
  30.7 9.8 %collective-permute-start.13 = (f16[2,136,256]{2,1,0:T(8,128)(2,1)S(1)}, f16[2,136,256]{2,1,0:T(8,128)(2,1)S(1)}, u32[]{:S(2)}, u32[]{:S(2)}) collective-permute-start(f16[2,136,256]{2,1,0:T(8,128)(2,1)S(1)} %get-tuple-element.33), channel_id=1, source_target_pairs={{0,6},{1,7},{2,4},{3,5},{4,2},{5,3},{6,0},{7,1},{8,14},{9,15},{10,... | collective-permute-start | bytes 417800 | tf_op jit(solution)/shard_map/ppermute | solution.py:259
  34.0 6.6 %collective-permute-start.12 = (f16[2,136,256]{2,1,0:T(8,128)(2,1)S(1)}, f16[2,136,256]{2,1,0:T(8,128)(2,1)S(1)}, u32[]{:S(2)}, u32[]{:S(2)}) collective-permute-start(f16[2,136,256]{2,1,0:T(8,128)(2,1)S(1)} %get-tuple-element.33), channel_id=1, source_target_pairs={{0,4},{1,5},{2,6},{3,7},{4,0},{5,1},{6,2},{7,3},{8,12},{9,13},{10,... | collective-permute-start | bytes 417800 | tf_op jit(solution)/shard_map/ppermute | solution.py:259
  34.3 6.3 %collective-permute-start.11 = (f16[2,136,256]{2,1,0:T(8,128)(2,1)S(1)}, f16[2,136,256]{2,1,0:T(8,128)(2,1)S(1)}, u32[]{:S(2)}, u32[]{:S(2)}) collective-permute-start(f16[2,136,256]{2,1,0:T(8,128)(2,1)S(1)} %get-tuple-element.33), channel_id=1, source_target_pairs={{0,2},{1,3},{2,0},{3,1},{4,6},{5,7},{6,4},{7,5},{8,10},{9,11},{10,... | collective-permute-start | bytes 417800 | tf_op jit(solution)/shard_map/ppermute | solution.py:259
  42.8 3.7 %collective-permute-start.14 = (f32[64,1024]{1,0:T(8,128)S(1)}, f32[64,1024]{1,0:T(8,128)S(1)}, u32[]{:S(2)}, u32[]{:S(2)}) collective-permute-start(f32[64,1024]{1,0:T(8,128)S(1)} %get-tuple-element.32), channel_id=1, source_target_pairs={{0,1},{1,0},{2,3},{3,2},{4,5},{5,4},{6,7},{7,6},{8,9},{9,8},{10,11... | collective-permute-start | bytes 786440 | tf_op jit(solution)/shard_map/ppermute | solution.py:262

commit v5 on v4

--- a/solution.py
+++ b/solution.py
@@ -8,7 +8,7 @@
 from jax.sharding import PartitionSpec as P
 
 NT = (((1,), (1,)), ((), ()))
-PROJECT_VMEM = 61 * 2**20
+PROJECT_VMEM = 50 * 2**20
 SCORE_VMEM = 24 * 2**20
 ORDER = (1, 3, 2)
 OWN_FLOPS = 12 * 10**9
@@ -52,20 +52,16 @@
             out[s * per + k, j, 2 * WIDTH + 4 * h : 2 * WIDTH + 4 * h + 4, :] = jnp.broadcast_to(power, (4, QTOK))
 
 
-def project_kernel(chunk, slots, acts, grads, p_in, p_out, keep, give, av, gv, piv, pov, sem_a, sem_g, sem_p):
+def project_kernel(chunk, slots, acts, grads, proj, keep, give, av, gv, pv, sem_a, sem_g, sem_p):
     t = lax.axis_index("tensor")
     y, core = t // 2, t % 2
     per = chunk // QTOK
+    d_in = acts.shape[2]
     weights, steps = [], []
     order = ((give, 2 * (1 - core), 0), (give, 2 * (1 - core), 1), (keep, 2 * core, 0), (keep, 2 * core, 1))
     for w, (out, first, j) in enumerate(order):
         layer = first + j
-        weights.append(
-            (
-                pltpu.make_async_copy(p_in.at[layer], piv.at[w], sem_p.at[2 * w]),
-                pltpu.make_async_copy(p_out.at[layer], pov.at[w], sem_p.at[2 * w + 1]),
-            )
-        )
+        weights.append(pltpu.make_async_copy(proj.at[layer], pv.at[w], sem_p.at[w]))
         for s in range(QUART // per):
             slot = len(steps) % slots
             group = []
@@ -77,23 +73,20 @@
             steps.append((out, j, s, w, slot, group))
     for n in range(slots):
         if n == 0:
-            for c in weights[0]:
-                c.start()
+            weights[0].start()
         for c in steps[n][5]:
             c.start()
         if n == 0:
-            for pair in weights[1:]:
-                for c in pair:
-                    c.start()
+            for c in weights[1:]:
+                c.start()
     for n, (out, j, s, w, slot, group) in enumerate(steps):
         if s == 0:
-            for c in weights[w]:
-                c.wait()
+            weights[w].wait()
         for c in group:
             c.wait()
         parts = (
-            lax.dot_general(piv[w], av[slot], NT, preferred_element_type=jnp.float32),
-            lax.dot_general(pov[w], gv[slot], NT, preferred_element_type=jnp.float32),
+            lax.dot_general(pv[w, :, :d_in], av[slot], NT, preferred_element_type=jnp.float32),
+            lax.dot_general(pv[w, :, d_in:], gv[slot], NT, preferred_element_type=jnp.float32),
         )
         if n > 0:
             add_powers(per, *steps[n - 1][:3])
@@ -106,22 +99,21 @@
     add_powers(per, *steps[-1][:3])
 
 
-def project(acts, grads, p_in, p_out, chunk, slots):
+def project(acts, grads, proj, chunk, slots):
     layers, tokens, d_in, d_out = acts.shape[0], acts.shape[1], acts.shape[2], grads.shape[2]
     in_any = pl.BlockSpec(memory_space=pl.ANY)
     return pl.pallas_call(
         functools.partial(project_kernel, chunk, slots),
-        in_specs=[in_any] * 4,
+        in_specs=[in_any] * 3,
         out_specs=[pl.BlockSpec(memory_space=pltpu.VMEM)] * 2,
         out_shape=[jax.ShapeDtypeStruct((QUART, 2, ROWS, QTOK), jnp.float32)] * 2,
         scratch_shapes=[
             pltpu.VMEM((slots, chunk, d_in), jnp.bfloat16),
             pltpu.VMEM((slots, chunk, d_out), jnp.bfloat16),
-            pltpu.VMEM((layers, WIDTH, d_in), jnp.bfloat16),
-            pltpu.VMEM((layers, WIDTH, d_out), jnp.bfloat16),
+            pltpu.VMEM((layers, WIDTH, d_in + d_out), jnp.bfloat16),
             pltpu.SemaphoreType.DMA((slots, chunk // QTOK)),
             pltpu.SemaphoreType.DMA((slots, chunk // QTOK)),
-            pltpu.SemaphoreType.DMA((2 * layers,)),
+            pltpu.SemaphoreType.DMA((layers,)),
         ],
         compiler_params=pltpu.CompilerParams(vmem_limit_bytes=PROJECT_VMEM),
         cost_estimate=pl.CostEstimate(
@@ -130,7 +122,7 @@
             transcendentals=0,
         ),
         name="project",
-    )(acts, grads, p_in, p_out)
+    )(acts, grads, proj)
 
 
 def score_tokens(scale, sums, q0, q1, q3, q2):
@@ -233,9 +225,10 @@
     theirs = lax.ppermute(query_feats, "tensor", swap_perm())
     mine = lax.dynamic_slice_in_dim(query_feats, 2 * core, 2, 0)
     got = lax.dynamic_slice_in_dim(theirs, 2 * core, 2, 0)
-    line0 = jnp.concatenate([mine, got], axis=1)
+    proj = jnp.concatenate([proj_input, proj_output], axis=2)
+    line0 = after(jnp.concatenate([mine, got], axis=1), proj)
     lines = [line0] + [lax.ppermute(line0, both, xz_perm(d, False)) for d in range(1, RING)]
-    keep, give = project(activations, out_grads, proj_input, proj_output, 512, 3)
+    keep, give = project(activations, out_grads, proj, 512, 3)
     give, lines = lax.optimization_barrier((give, lines))
     plane0 = jnp.stack(lines)
     taken = lax.ppermute(give, "tensor", swap_perm())

time: 47.5 us -> 47.1 us (level)
  Pallas kernels: 12.4 us -> 11.1 us
  waiting for transfers between devices: 7.4 us -> 8.37 us
    concatenate x0 -> x1, local copies, waits for them, and re-layouts: none -> 1.24 us  [local(): proj = jnp.concatenate([proj_input, proj_output], axis=2)]
    pallas_call x1, Pallas kernels: 9.76 us -> 8.53 us  [project(): pl.pallas_call(functools.partial(project_kernel, chunk, slots), in_specs=...]
    squeeze x2, local copies, waits for them, and re-layouts: 1.39 us -> 0.19 us  [local(): part = [keep[d] + taken[d] for d in range(QUART)]]
    ppermute x1, waiting for transfers between devices: 0.13 us -> 1.14 us  [local(): taken = lax.ppermute(give, 'tensor', swap_perm())]
    unnamed x30 -> x31, local copies, waits for them, and re-layouts: 0.07 us -> 1.04 us
    dynamic_slice x1, local copies, waits for them, and re-layouts: 0.84 us -> 0.01 us  [local(): mine = lax.dynamic_slice_in_dim(query_feats, 2 * core, 2, 0)]
  transfers between devices with their start and end apart: 15 -> 15, of which waited for: 5 -> 5; matrix products, arithmetic and copies ran while one was open for 7% -> 8% of each run, Pallas kernels for 22% -> 20%
where the time goes in v5:
time: 47.1 us; the launch traced here: 47 us
  starting transfers between devices  22.3 us (47%)
  Pallas kernels  11.1 us (24%)
  waiting for transfers between devices  8.37 us (18%)
  local copies, waits for them, and re-layouts  2.55 us (5%)
  other arithmetic  2.09 us (4%)
  between operations  0.49 us (1%)
    pallas_call x1, Pallas kernels, project(): pl.pallas_call(functools.partial(project_kernel, chunk, slots), in_specs=...  8.53 us
    ppermute x2, waiting for transfers between devices, local(): lax.ppermute(p, both, xz_perm(3, True))  5.14 us
    ppermute x2, starting transfers between devices, local(): lax.ppermute(p, both, xz_perm(3, True))  4.96 us
    ppermute x3, starting transfers between devices, local(): lax.ppermute(line0, both, xz_perm(d, False))  4.59 us
    ppermute x3, starting transfers between devices, local(): sent[d - 1] = lax.ppermute(packed[d - 1], 'tensor', y_perm(d))  3.85 us
    ppermute x3, starting transfers between devices, local(): lax.ppermute(message, 'tensor', y_perm(d))  3.55 us
    ppermute x1, starting transfers between devices, local(): return (keep_s + lax.ppermute(give_s, 'tensor', swap_perm())).T  2.59 us
    pallas_call x1, Pallas kernels, score(): pl.pallas_call(functools.partial(score_kernel, scale), in_specs=[vm] * 8,...  1.88 us
  transfers between devices with their start and end apart: 15, of which 5 were waited for; matrix products, arithmetic and copies ran while one was open for 8% of the time, Pallas kernels for 20%

profile of v5, /device:TPU:1, one launch (start us, length us, event | category | flops | bytes accessed | tf_op | source)
XLA Modules:
  0.0 47.0 jit_solution(13972513124368644688)
XLA Ops:
  0.0 1.4 %collective-permute-start = (bf16[4,64,256]{2,1,0:T(8,128)(2,1)}, bf16[4,64,256]{2,1,0:T(8,128)(2,1)S(1)}, u32[]{:S(2)}, u32[]{:S(2)}) collective-permute-start(bf16[4,64,256]{2,1,0:T(8,128)(2,1)} %param.9), channel_id=1, source_target_pairs={{0,1},{1,0},{2,3},{3,2},{4,5},{5,4},{6,7},{7,6},{8,9},{9,8},{10,11... | collective-permute-start | bytes 393224 | tf_op jit(solution)/shard_map/ppermute | solution.py:225
  1.4 1.0 %constant_dynamic-update-slice_fusion.1 = bf16[4,64,2304]{2,1,0:T(8,128)(2,1)S(1)} fusion(bf16[4,64,512]{2,1,0:T(8,128)(2,1)} %param.7), kind=kLoop, calls=%fused_computation.38 | loop fusion | bytes 524288
  2.4 1.2 %constant_dynamic-update-slice_fusion.proj = bf16[4,64,2304]{2,1,0:T(8,128)(2,1)S(1)} fusion(bf16[4,64,2304]{2,1,0:T(8,128)(2,1)S(1)} %constant_dynamic-update-slice_fusion.1, bf16[4,64,1792]{2,1,0:T(8,128)(2,1)} %param.8), kind=kLoop, calls=%fused_computation.37 | loop fusion | bytes 1835008 | tf_op jit(solution)/shard_map/concatenate | solution.py:228
  3.7 0.0 collective-permute-done
  3.7 3.9 %collective-permute-start.3 = (bf16[2,128,256]{2,1,0:T(8,128)(2,1)S(1)}, bf16[2,128,256]{2,1,0:T(8,128)(2,1)S(1)}, u32[]{:S(2)}, u32[]{:S(2)}) collective-permute-start(bf16[2,128,256]{2,1,0:T(8,128)(2,1)S(1)} %pad_maximum_fusion.1), channel_id=1, source_target_pairs={{96,0},{25,1},{98,2},{27,3},{100,4},{29,5},{102,6},{31,7},{104,8},... | collective-permute-start | bytes 393224 | tf_op jit(solution)/shard_map/ppermute | solution.py:230
  7.7 0.7 %collective-permute-start.1 = (bf16[2,128,256]{2,1,0:T(8,128)(2,1)S(1)}, bf16[2,128,256]{2,1,0:T(8,128)(2,1)S(1)}, u32[]{:S(2)}, u32[]{:S(2)}) collective-permute-start(bf16[2,128,256]{2,1,0:T(8,128)(2,1)S(1)} %pad_maximum_fusion.1), channel_id=1, source_target_pairs={{32,0},{9,1},{34,2},{11,3},{36,4},{13,5},{38,6},{15,7},{40,8},{1,9... | collective-permute-start | bytes 393224 | tf_op jit(solution)/shard_map/ppermute | solution.py:230
  8.3 8.5 %project.1 = (f32[4,2,136,256]{3,2,1,0:T(8,128)S(1)}, f32[4,2,136,256]{3,2,1,0:T(8,128)S(1)}) custom-call(bf16[4,1024,512]{2,1,0:T(8,128)(2,1)} %acts.1, bf16[4,1024,1792]{2,1,0:T(8,128)(2,1)} %grads.1, bf16[4,64,2304]{2,1,0:T(8,128)(2,1)S(1)} %constant_dynamic-update-slice_fusion.proj), custom_call_target="tpu_custom_call" | custom-call | flops 1207959552 | bytes 18874368 | tf_op jit(solution)/shard_map/project/pallas_call | solution.py:105
  16.9 0.1 collective-permute-start.4
  17.0 0.1 slice_bitcast_fusion.6
  17.2 0.1 pad_maximum_fusion.q0
  17.3 1.3 %collective-permute-start.8 = (bf16[4,2,128,256]{3,2,1,0:T(8,128)(2,1)S(1)}, bf16[4,2,128,256]{3,2,1,0:T(8,128)(2,1)S(1)}, u32[]{:S(2)}, u32[]{:S(2)}) collective-permute-start(bf16[4,2,128,256]{3,2,1,0:T(8,128)(2,1)S(1)} %pad_maximum_fusion.q0), channel_id=1, source_target_pairs={{8,0},{33,1},{10,2},{35,3},{12,4},{37,5},{14,6},{39,7},{0,8},{41,9... | collective-permute-start | bytes 1572872 | tf_op jit(solution)/shard_map/ppermute | solution.py:241
  18.6 1.1 %collective-permute-done.4 = f32[4,2,136,256]{3,2,1,0:T(8,128)S(1)} collective-permute-done((f32[4,2,136,256]{3,2,1,0:T(8,128)S(1)}, f32[4,2,136,256]{3,2,1,0:T(8,128)S(1)}, u32[]{:S(2)}, u32[]{:S(2)}) %collective-permute-start.4) | collective-permute-done | bytes 1114144 | tf_op jit(solution)/shard_map/ppermute | solution.py:234
  19.7 0.1 slice_bitcast_fusion.2
  19.9 0.2 select_convert_fusion.2
  20.1 3.0 %collective-permute-start.6 = (f16[2,136,256]{2,1,0:T(8,128)(2,1)S(1)}, f16[2,136,256]{2,1,0:T(8,128)(2,1)S(1)}, u32[]{:S(2)}, u32[]{:S(2)}) collective-permute-start(f16[2,136,256]{2,1,0:T(8,128)(2,1)S(1)} %select_convert_fusion.2), channel_id=1, source_target_pairs={{0,4},{1,5},{2,6},{3,7},{4,0},{5,1},{6,2},{7,3},{8,12},{9,13},{10,... | collective-permute-start | bytes 417800 | tf_op jit(solution)/shard_map/ppermute | solution.py:240
  23.1 0.3 select_convert_fusion.3
  23.4 0.9 %collective-permute-start.7 = (f16[2,136,256]{2,1,0:T(8,128)(2,1)S(1)}, f16[2,136,256]{2,1,0:T(8,128)(2,1)S(1)}, u32[]{:S(2)}, u32[]{:S(2)}) collective-permute-start(f16[2,136,256]{2,1,0:T(8,128)(2,1)S(1)} %get-tuple-element.38), channel_id=1, source_target_pairs={{0,6},{1,7},{2,4},{3,5},{4,2},{5,3},{6,0},{7,1},{8,14},{9,15},{10,... | collective-permute-start | bytes 417800 | tf_op jit(solution)/shard_map/ppermute | solution.py:240
  24.3 2.5 %collective-permute-start.9 = (bf16[4,2,128,256]{3,2,1,0:T(8,128)(2,1)S(1)}, bf16[4,2,128,256]{3,2,1,0:T(8,128)(2,1)S(1)}, u32[]{:S(2)}, u32[]{:S(2)}) collective-permute-start(bf16[4,2,128,256]{3,2,1,0:T(8,128)(2,1)S(1)} %pad_maximum_fusion.q0), channel_id=1, source_target_pairs={{24,0},{97,1},{26,2},{99,3},{28,4},{101,5},{30,6},{103,7},{16,8},{... | collective-permute-start | bytes 1572872 | tf_op jit(solution)/shard_map/ppermute | solution.py:247
  26.8 0.1 collective-permute-done.6
  26.9 2.5 %collective-permute-start.10 = (bf16[4,2,128,256]{3,2,1,0:T(8,128)(2,1)S(1)}, bf16[4,2,128,256]{3,2,1,0:T(8,128)(2,1)S(1)}, u32[]{:S(2)}, u32[]{:S(2)}) collective-permute-start(bf16[4,2,128,256]{3,2,1,0:T(8,128)(2,1)S(1)} %collective-permute-done.8.q1), channel_id=1, source_target_pairs={{24,0},{97,1},{26,2},{99,3},{28,4},{101,5},{30,6},{103,7},{16,8},{... | collective-permute-start | bytes 1572872 | tf_op jit(solution)/shard_map/ppermute | solution.py:247
  29.3 0.8 %collective-permute-done.5 = f16[2,136,256]{2,1,0:T(8,128)(2,1)S(1)} collective-permute-done((f16[2,136,256]{2,1,0:T(8,128)(2,1)S(1)}, f16[2,136,256]{2,1,0:T(8,128)(2,1)S(1)}, u32[]{:S(2)}, u32[]{:S(2)}) %collective-permute-start.5) | collective-permute-done | bytes 139296 | tf_op jit(solution)/shard_map/ppermute | solution.py:240
  30.3 0.5 %select_convert_fusion = (f16[2,136,256]{2,1,0:T(8,128)(2,1)S(1)}, f32[2,136,256]{2,1,0:T(8,128)S(1)}) fusion(f32[2,256]{1,0:T(2,128)S(1)} %bitcast.137, f32[2,256]{1,0:T(2,128)S(1)} %bitcast.138, f32[2,256]{1,0:T(2,128)S(1)} %bitcast.129, f32[2,256]{1,0:T(2,128)S(1)} %bitcast.130, f32[2,256]{1,0:T(2,128)S(1)} %bitcast.152, f32[2,256]{1,0:T(2,128)S(1)} %bitcast.150, ...), kind=kLoop, calls=%fused_computation.24 | loop fusion | flops 2228224 | bytes 1413392 | tf_op jit(solution)/shard_map/convert_element_type | solution.py:211
  30.7 2.9 %collective-permute-start.13 = (f16[2,136,256]{2,1,0:T(8,128)(2,1)S(1)}, f16[2,136,256]{2,1,0:T(8,128)(2,1)S(1)}, u32[]{:S(2)}, u32[]{:S(2)}) collective-permute-start(f16[2,136,256]{2,1,0:T(8,128)(2,1)S(1)} %get-tuple-element.35), channel_id=1, source_target_pairs={{0,6},{1,7},{2,4},{3,5},{4,2},{5,3},{6,0},{7,1},{8,14},{9,15},{10,... | collective-permute-start | bytes 417800 | tf_op jit(solution)/shard_map/ppermute | solution.py:252
  33.6 0.3 collective-permute-start.12
  34.0 0.3 collective-permute-start.11
  34.3 5.1 %collective-permute-done.10.q2 = bf16[4,2,128,256]{3,2,1,0:T(8,128)(2,1)S(1)} collective-permute-done((bf16[4,2,128,256]{3,2,1,0:T(8,128)(2,1)S(1)}, bf16[4,2,128,256]{3,2,1,0:T(8,128)(2,1)S(1)}, u32[]{:S(2)}, u32[]{:S(2)}) %collective-permute-start.10) | collective-permute-done | bytes 524320 | tf_op jit(solution)/shard_map/ppermute | solution.py:247
  39.5 0.7 %own_score.1.own = f32[128,256]{1,0:T(8,128)S(1)} custom-call(f32[2,128,256]{2,1,0:T(8,128)S(1)} %slice.196.s0, bf16[4,2,128,256]{3,2,1,0:T(8,128)(2,1)S(1)} %pad_maximum_fusion.q0, bf16[4,2,128,256]{3,2,1,0:T(8,128)(2,1)S(1)} %collective-permute-done.8.q1, bf16[4,2,128,256]{3,2,1,0:T(8,128)(2,1)S(1)} %collective-permute-done.9.q3, ...), custom_call_target="tpu_custom_call" | custom-call | flops 12000000000 | bytes 4194304 | tf_op jit(solution)/shard_map/own_score/pallas_call | solution.py:167
  40.3 0.3 exponential_multiply_fusion
  40.6 1.9 %score.1 = (f32[64,1024]{1,0:T(8,128)S(1)}, f32[64,1024]{1,0:T(8,128)S(1)}) custom-call(f32[128,256]{1,0:T(8,128)S(1)} %own_score.1.own, f32[2,128,256]{2,1,0:T(8,128)S(1)} %get-tuple-element.77.s1, f32[2,128,256]{2,1,0:T(8,128)S(1)} %get-tuple-element.76.s2, f32[2,128,256]{2,1,0:T(8,128)S(1)} %get-tuple-element.75.s3, ...), custom_call_target="tpu_custom_call" | custom-call | flops 2147483648 | bytes 4194304 | tf_op jit(solution)/shard_map/score/pallas_call | solution.py:181
  42.5 2.6 %collective-permute-start.14 = (f32[64,1024]{1,0:T(8,128)S(1)}, f32[64,1024]{1,0:T(8,128)S(1)}, u32[]{:S(2)}, u32[]{:S(2)}) collective-permute-start(f32[64,1024]{1,0:T(8,128)S(1)} %get-tuple-element.34), channel_id=1, source_target_pairs={{0,1},{1,0},{2,3},{3,2},{4,5},{5,4},{6,7},{7,6},{8,9},{9,8},{10,11... | collective-permute-start | bytes 786440 | tf_op jit(solution)/shard_map/ppermute | solution.py:255
  45.1 1.2 %collective-permute-done.14 = f32[64,1024]{1,0:T(8,128)S(1)} collective-permute-done((f32[64,1024]{1,0:T(8,128)S(1)}, f32[64,1024]{1,0:T(8,128)S(1)}, u32[]{:S(2)}, u32[]{:S(2)}) %collective-permute-start.14) | collective-permute-done | bytes 262176 | tf_op jit(solution)/shard_map/ppermute | solution.py:255
  46.2 0.7 %add_bitcast_fusion = f32[1024,64]{0,1:T(8,128)} fusion(f32[64,1024]{1,0:T(8,128)S(1)} %get-tuple-element.33, f32[64,1024]{1,0:T(8,128)S(1)} %collective-permute-done.14), kind=kLoop, calls=%fused_computation.32 | loop fusion | flops 65536 | bytes 786432 | tf_op jit(solution)/shard_map/transpose | solution.py:255
  (56 shorter events, 0.2 us)
Async XLA Ops:
  0.0 3.7 %copy-start = (bf16[4,64,256]{2,1,0:T(8,128)(2,1)S(1)}, bf16[4,64,256]{2,1,0:T(8,128)(2,1)}, u32[]{:S(2)}) copy-start(bf16[4,64,256]{2,1,0:T(8,128)(2,1)} %param.9) | copy-start | bytes 393220
  0.0 3.7 %collective-permute-start = (bf16[4,64,256]{2,1,0:T(8,128)(2,1)}, bf16[4,64,256]{2,1,0:T(8,128)(2,1)S(1)}, u32[]{:S(2)}, u32[]{:S(2)}) collective-permute-start(bf16[4,64,256]{2,1,0:T(8,128)(2,1)} %param.9), channel_id=1, source_target_pairs={{0,1},{1,0},{2,3},{3,2},{4,5},{5,4},{6,7},{7,6},{8,9},{9,8},{10,11... | collective-permute-start | bytes 393224 | tf_op jit(solution)/shard_map/ppermute | solution.py:225
  3.7 13.1 %collective-permute-start.3 = (bf16[2,128,256]{2,1,0:T(8,128)(2,1)S(1)}, bf16[2,128,256]{2,1,0:T(8,128)(2,1)S(1)}, u32[]{:S(2)}, u32[]{:S(2)}) collective-permute-start(bf16[2,128,256]{2,1,0:T(8,128)(2,1)S(1)} %pad_maximum_fusion.1), channel_id=1, source_target_pairs={{96,0},{25,1},{98,2},{27,3},{100,4},{29,5},{102,6},{31,7},{104,8},... | collective-permute-start | bytes 393224 | tf_op jit(solution)/shard_map/ppermute | solution.py:230
  7.7 9.2 %collective-permute-start.2 = (bf16[2,128,256]{2,1,0:T(8,128)(2,1)S(1)}, bf16[2,128,256]{2,1,0:T(8,128)(2,1)S(1)}, u32[]{:S(2)}, u32[]{:S(2)}) collective-permute-start(bf16[2,128,256]{2,1,0:T(8,128)(2,1)S(1)} %pad_maximum_fusion.1), channel_id=1, source_target_pairs={{64,0},{17,1},{66,2},{19,3},{68,4},{21,5},{70,6},{23,7},{72,8},{25... | collective-permute-start | bytes 393224 | tf_op jit(solution)/shard_map/ppermute | solution.py:230
  7.7 9.2 %collective-permute-start.1 = (bf16[2,128,256]{2,1,0:T(8,128)(2,1)S(1)}, bf16[2,128,256]{2,1,0:T(8,128)(2,1)S(1)}, u32[]{:S(2)}, u32[]{:S(2)}) collective-permute-start(bf16[2,128,256]{2,1,0:T(8,128)(2,1)S(1)} %pad_maximum_fusion.1), channel_id=1, source_target_pairs={{32,0},{9,1},{34,2},{11,3},{36,4},{13,5},{38,6},{15,7},{40,8},{1,9... | collective-permute-start | bytes 393224 | tf_op jit(solution)/shard_map/ppermute | solution.py:230
  16.9 2.8 %collective-permute-start.4 = (f32[4,2,136,256]{3,2,1,0:T(8,128)S(1)}, f32[4,2,136,256]{3,2,1,0:T(8,128)S(1)}, u32[]{:S(2)}, u32[]{:S(2)}) collective-permute-start(f32[4,2,136,256]{3,2,1,0:T(8,128)S(1)} %get-tuple-element.23), channel_id=1, source_target_pairs={{0,1},{1,0},{2,3},{3,2},{4,5},{5,4},{6,7},{7,6},{8,9},{9,8},{10,11... | collective-permute-start | bytes 3342344 | tf_op jit(solution)/shard_map/ppermute | solution.py:234
  17.3 9.5 %collective-permute-start.8 = (bf16[4,2,128,256]{3,2,1,0:T(8,128)(2,1)S(1)}, bf16[4,2,128,256]{3,2,1,0:T(8,128)(2,1)S(1)}, u32[]{:S(2)}, u32[]{:S(2)}) collective-permute-start(bf16[4,2,128,256]{3,2,1,0:T(8,128)(2,1)S(1)} %pad_maximum_fusion.q0), channel_id=1, source_target_pairs={{8,0},{33,1},{10,2},{35,3},{12,4},{37,5},{14,6},{39,7},{0,8},{41,9... | collective-permute-start | bytes 1572872 | tf_op jit(solution)/shard_map/ppermute | solution.py:241
  20.1 6.7 %collective-permute-start.6 = (f16[2,136,256]{2,1,0:T(8,128)(2,1)S(1)}, f16[2,136,256]{2,1,0:T(8,128)(2,1)S(1)}, u32[]{:S(2)}, u32[]{:S(2)}) collective-permute-start(f16[2,136,256]{2,1,0:T(8,128)(2,1)S(1)} %select_convert_fusion.2), channel_id=1, source_target_pairs={{0,4},{1,5},{2,6},{3,7},{4,0},{5,1},{6,2},{7,3},{8,12},{9,13},{10,... | collective-permute-start | bytes 417800 | tf_op jit(solution)/shard_map/ppermute | solution.py:240
  23.4 6.8 %collective-permute-start.7 = (f16[2,136,256]{2,1,0:T(8,128)(2,1)S(1)}, f16[2,136,256]{2,1,0:T(8,128)(2,1)S(1)}, u32[]{:S(2)}, u32[]{:S(2)}) collective-permute-start(f16[2,136,256]{2,1,0:T(8,128)(2,1)S(1)} %get-tuple-element.38), channel_id=1, source_target_pairs={{0,6},{1,7},{2,4},{3,5},{4,2},{5,3},{6,0},{7,1},{8,14},{9,15},{10,... | collective-permute-start | bytes 417800 | tf_op jit(solution)/shard_map/ppermute | solution.py:240
  24.3 5.9 %collective-permute-start.5 = (f16[2,136,256]{2,1,0:T(8,128)(2,1)S(1)}, f16[2,136,256]{2,1,0:T(8,128)(2,1)S(1)}, u32[]{:S(2)}, u32[]{:S(2)}) collective-permute-start(f16[2,136,256]{2,1,0:T(8,128)(2,1)S(1)} %get-tuple-element.37), channel_id=1, source_target_pairs={{0,2},{1,3},{2,0},{3,1},{4,6},{5,7},{6,4},{7,5},{8,10},{9,11},{10,... | collective-permute-start | bytes 417800 | tf_op jit(solution)/shard_map/ppermute | solution.py:240
  24.3 10.0 %collective-permute-start.9 = (bf16[4,2,128,256]{3,2,1,0:T(8,128)(2,1)S(1)}, bf16[4,2,128,256]{3,2,1,0:T(8,128)(2,1)S(1)}, u32[]{:S(2)}, u32[]{:S(2)}) collective-permute-start(bf16[4,2,128,256]{3,2,1,0:T(8,128)(2,1)S(1)} %pad_maximum_fusion.q0), channel_id=1, source_target_pairs={{24,0},{97,1},{26,2},{99,3},{28,4},{101,5},{30,6},{103,7},{16,8},{... | collective-permute-start | bytes 1572872 | tf_op jit(solution)/shard_map/ppermute | solution.py:247
  26.9 12.6 %collective-permute-start.10 = (bf16[4,2,128,256]{3,2,1,0:T(8,128)(2,1)S(1)}, bf16[4,2,128,256]{3,2,1,0:T(8,128)(2,1)S(1)}, u32[]{:S(2)}, u32[]{:S(2)}) collective-permute-start(bf16[4,2,128,256]{3,2,1,0:T(8,128)(2,1)S(1)} %collective-permute-done.8.q1), channel_id=1, source_target_pairs={{24,0},{97,1},{26,2},{99,3},{28,4},{101,5},{30,6},{103,7},{16,8},{... | collective-permute-start | bytes 1572872 | tf_op jit(solution)/shard_map/ppermute | solution.py:247
  30.7 9.5 %collective-permute-start.13 = (f16[2,136,256]{2,1,0:T(8,128)(2,1)S(1)}, f16[2,136,256]{2,1,0:T(8,128)(2,1)S(1)}, u32[]{:S(2)}, u32[]{:S(2)}) collective-permute-start(f16[2,136,256]{2,1,0:T(8,128)(2,1)S(1)} %get-tuple-element.35), channel_id=1, source_target_pairs={{0,6},{1,7},{2,4},{3,5},{4,2},{5,3},{6,0},{7,1},{8,14},{9,15},{10,... | collective-permute-start | bytes 417800 | tf_op jit(solution)/shard_map/ppermute | solution.py:252
  33.6 6.6 %collective-permute-start.12 = (f16[2,136,256]{2,1,0:T(8,128)(2,1)S(1)}, f16[2,136,256]{2,1,0:T(8,128)(2,1)S(1)}, u32[]{:S(2)}, u32[]{:S(2)}) collective-permute-start(f16[2,136,256]{2,1,0:T(8,128)(2,1)S(1)} %get-tuple-element.35), channel_id=1, source_target_pairs={{0,4},{1,5},{2,6},{3,7},{4,0},{5,1},{6,2},{7,3},{8,12},{9,13},{10,... | collective-permute-start | bytes 417800 | tf_op jit(solution)/shard_map/ppermute | solution.py:252
  34.0 6.3 %collective-permute-start.11 = (f16[2,136,256]{2,1,0:T(8,128)(2,1)S(1)}, f16[2,136,256]{2,1,0:T(8,128)(2,1)S(1)}, u32[]{:S(2)}, u32[]{:S(2)}) collective-permute-start(f16[2,136,256]{2,1,0:T(8,128)(2,1)S(1)} %get-tuple-element.35), channel_id=1, source_target_pairs={{0,2},{1,3},{2,0},{3,1},{4,6},{5,7},{6,4},{7,5},{8,10},{9,11},{10,... | collective-permute-start | bytes 417800 | tf_op jit(solution)/shard_map/ppermute | solution.py:252
  42.5 3.8 %collective-permute-start.14 = (f32[64,1024]{1,0:T(8,128)S(1)}, f32[64,1024]{1,0:T(8,128)S(1)}, u32[]{:S(2)}, u32[]{:S(2)}) collective-permute-start(f32[64,1024]{1,0:T(8,128)S(1)} %get-tuple-element.34), channel_id=1, source_target_pairs={{0,1},{1,0},{2,3},{3,2},{4,5},{5,4},{6,7},{7,6},{8,9},{9,8},{10,11... | collective-permute-start | bytes 786440 | tf_op jit(solution)/shard_map/ppermute | solution.py:255

commit v6 on v5

--- a/solution.py
+++ b/solution.py
@@ -231,7 +231,9 @@
     keep, give = project(activations, out_grads, proj, 512, 3)
     give, lines = lax.optimization_barrier((give, lines))
     plane0 = jnp.stack(lines)
-    taken = lax.ppermute(give, "tensor", swap_perm())
+    low = lax.ppermute(give[:2], "tensor", swap_perm())
+    high = lax.ppermute(give[2:], "tensor", swap_perm())
+    taken = [low[0], low[1], high[0], high[1]]
     part = [keep[d] + taken[d] for d in range(QUART)]
     power = [jnp.maximum(powers(keep[d]), powers(taken[d])) + 1.0 for d in range(QUART)]
     packed = [pack(part[d], power[d]) for d in range(1, QUART)]

time: 47.1 us -> 54.4 us (1.15)
  starting transfers between devices: 22.3 us -> 26.2 us
  waiting for transfers between devices: 8.37 us -> 11.7 us
    ppermute x3, waiting for transfers between devices: 0.01 us -> 5.07 us  [local(): lax.ppermute(line0, both, xz_perm(d, False))]
    ppermute x1, starting transfers between devices: 2.59 us -> 4.88 us  [local(): return (keep_s + lax.ppermute(give_s, 'tensor', swap_perm())).T]
    ppermute x2, waiting for transfers between devices: 5.14 us -> 3.55 us  [local(): lax.ppermute(p, both, xz_perm(3, True))]
    ppermute x1 -> x2, waiting for transfers between devices: 1.14 us -> 0.01 us  [the longest x1 0.01 us: local(): high = lax.ppermute(give[2:], 'tensor', swap_perm())]
    ppermute x3, waiting for transfers between devices: 0.91 us -> 1.7 us  [local(): sent[d - 1] = lax.ppermute(packed[d - 1], 'tensor', y_perm(d))]
    ppermute x2, starting transfers between devices: 4.96 us -> 5.75 us  [local(): lax.ppermute(p, both, xz_perm(3, True))]
    ppermute x1 -> x2, starting transfers between devices: 0.09 us -> 0.67 us  [the longest x1 0.38 us: local(): high = lax.ppermute(give[2:], 'tensor', swap_perm())]
  transfers between devices with their start and end apart: 15 -> 16, of which waited for: 5 -> 6; matrix products, arithmetic and copies ran while one was open for 8% -> 7% of each run, Pallas kernels for 20% -> 17%
where the time goes in v6:
time: 54.4 us; the launch traced here: 54.2 us
  starting transfers between devices  26.2 us (48%)
  waiting for transfers between devices  11.7 us (22%)
  Pallas kernels  11.2 us (21%)
  local copies, waits for them, and re-layouts  2.6 us (5%)
  other arithmetic  2.08 us (4%)
    pallas_call x1, Pallas kernels, project(): pl.pallas_call(functools.partial(project_kernel, chunk, slots), in_specs=...  8.56 us
    ppermute x2, starting transfers between devices, local(): lax.ppermute(p, both, xz_perm(3, True))  5.75 us
    ppermute x3, starting transfers between devices, local(): lax.ppermute(line0, both, xz_perm(d, False))  5.11 us
    ppermute x3, waiting for transfers between devices, local(): lax.ppermute(line0, both, xz_perm(d, False))  5.07 us
    ppermute x1, starting transfers between devices, local(): return (keep_s + lax.ppermute(give_s, 'tensor', swap_perm())).T  4.88 us
    ppermute x3, starting transfers between devices, local(): sent[d - 1] = lax.ppermute(packed[d - 1], 'tensor', y_perm(d))  3.72 us
    ppermute x2, waiting for transfers between devices, local(): lax.ppermute(p, both, xz_perm(3, True))  3.55 us
    ppermute x3, starting transfers between devices, local(): lax.ppermute(message, 'tensor', y_perm(d))  3.33 us
  transfers between devices with their start and end apart: 16, of which 6 were waited for; matrix products, arithmetic and copies ran while one was open for 7% of the time, Pallas kernels for 17%

profile of v6, /device:TPU:1, one launch (start us, length us, event | category | flops | bytes accessed | tf_op | source)
XLA Modules:
  0.0 54.2 jit_solution(3867634133278042869)
XLA Ops:
  0.0 1.4 %collective-permute-start = (bf16[4,64,256]{2,1,0:T(8,128)(2,1)}, bf16[4,64,256]{2,1,0:T(8,128)(2,1)S(1)}, u32[]{:S(2)}, u32[]{:S(2)}) collective-permute-start(bf16[4,64,256]{2,1,0:T(8,128)(2,1)} %param.9), channel_id=1, source_target_pairs={{0,1},{1,0},{2,3},{3,2},{4,5},{5,4},{6,7},{7,6},{8,9},{9,8},{10,11... | collective-permute-start | bytes 393224 | tf_op jit(solution)/shard_map/ppermute | solution.py:225
  1.4 1.0 %constant_dynamic-update-slice_fusion.1 = bf16[4,64,2304]{2,1,0:T(8,128)(2,1)S(1)} fusion(bf16[4,64,512]{2,1,0:T(8,128)(2,1)} %param.7), kind=kLoop, calls=%fused_computation.38 | loop fusion | bytes 524288
  2.4 1.2 %constant_dynamic-update-slice_fusion.proj = bf16[4,64,2304]{2,1,0:T(8,128)(2,1)S(1)} fusion(bf16[4,64,2304]{2,1,0:T(8,128)(2,1)S(1)} %constant_dynamic-update-slice_fusion.1, bf16[4,64,1792]{2,1,0:T(8,128)(2,1)} %param.8), kind=kLoop, calls=%fused_computation.37 | loop fusion | bytes 1835008 | tf_op jit(solution)/shard_map/concatenate | solution.py:228
  3.6 8.6 %project.1 = (f32[4,2,136,256]{3,2,1,0:T(8,128)S(1)}, f32[4,2,136,256]{3,2,1,0:T(8,128)S(1)}) custom-call(bf16[4,1024,512]{2,1,0:T(8,128)(2,1)} %acts.1, bf16[4,1024,1792]{2,1,0:T(8,128)(2,1)} %grads.1, bf16[4,64,2304]{2,1,0:T(8,128)(2,1)S(1)} %constant_dynamic-update-slice_fusion.proj), custom_call_target="tpu_custom_call" | custom-call | flops 1207959552 | bytes 18874368 | tf_op jit(solution)/shard_map/project/pallas_call | solution.py:105
  12.3 1.8 %collective-permute-start.1 = (bf16[2,128,256]{2,1,0:T(8,128)(2,1)S(1)}, bf16[2,128,256]{2,1,0:T(8,128)(2,1)S(1)}, u32[]{:S(2)}, u32[]{:S(2)}) collective-permute-start(bf16[2,128,256]{2,1,0:T(8,128)(2,1)S(1)} %pad_maximum_fusion.1), channel_id=1, source_target_pairs={{32,0},{9,1},{34,2},{11,3},{36,4},{13,5},{38,6},{15,7},{40,8},{1,9... | collective-permute-start | bytes 393224 | tf_op jit(solution)/shard_map/ppermute | solution.py:230
  14.1 3.3 %collective-permute-start.2 = (bf16[2,128,256]{2,1,0:T(8,128)(2,1)S(1)}, bf16[2,128,256]{2,1,0:T(8,128)(2,1)S(1)}, u32[]{:S(2)}, u32[]{:S(2)}) collective-permute-start(bf16[2,128,256]{2,1,0:T(8,128)(2,1)S(1)} %pad_maximum_fusion.1), channel_id=1, source_target_pairs={{64,0},{17,1},{66,2},{19,3},{68,4},{21,5},{70,6},{23,7},{72,8},{25... | collective-permute-start | bytes 393224 | tf_op jit(solution)/shard_map/ppermute | solution.py:230
  17.5 3.7 %collective-permute-done.2 = bf16[2,128,256]{2,1,0:T(8,128)(2,1)S(1)} collective-permute-done((bf16[2,128,256]{2,1,0:T(8,128)(2,1)S(1)}, bf16[2,128,256]{2,1,0:T(8,128)(2,1)S(1)}, u32[]{:S(2)}, u32[]{:S(2)}) %collective-permute-start.2) | collective-permute-done | bytes 131104 | tf_op jit(solution)/shard_map/ppermute | solution.py:230
  21.2 1.4 %collective-permute-done.3 = bf16[2,128,256]{2,1,0:T(8,128)(2,1)S(1)} collective-permute-done((bf16[2,128,256]{2,1,0:T(8,128)(2,1)S(1)}, bf16[2,128,256]{2,1,0:T(8,128)(2,1)S(1)}, u32[]{:S(2)}, u32[]{:S(2)}) %collective-permute-start.3) | collective-permute-done | bytes 131104 | tf_op jit(solution)/shard_map/ppermute | solution.py:230
  22.6 0.1 fusion.16
  22.7 0.4 collective-permute-start.6
  23.2 0.3 collective-permute-start.4
  23.5 1.3 %collective-permute-start.9 = (bf16[4,2,128,256]{3,2,1,0:T(8,128)(2,1)S(1)}, bf16[4,2,128,256]{3,2,1,0:T(8,128)(2,1)S(1)}, u32[]{:S(2)}, u32[]{:S(2)}) collective-permute-start(bf16[4,2,128,256]{3,2,1,0:T(8,128)(2,1)S(1)} %pad_maximum_fusion.q0), channel_id=1, source_target_pairs={{8,0},{33,1},{10,2},{35,3},{12,4},{37,5},{14,6},{39,7},{0,8},{41,9... | collective-permute-start | bytes 1572872 | tf_op jit(solution)/shard_map/ppermute | solution.py:243
  24.9 0.3 select_convert_fusion.2
  25.3 2.8 %collective-permute-start.8 = (f16[2,136,256]{2,1,0:T(8,128)(2,1)S(1)}, f16[2,136,256]{2,1,0:T(8,128)(2,1)S(1)}, u32[]{:S(2)}, u32[]{:S(2)}) collective-permute-start(f16[2,136,256]{2,1,0:T(8,128)(2,1)S(1)} %get-tuple-element.38), channel_id=1, source_target_pairs={{0,6},{1,7},{2,4},{3,5},{4,2},{5,3},{6,0},{7,1},{8,14},{9,15},{10,... | collective-permute-start | bytes 417800 | tf_op jit(solution)/shard_map/ppermute | solution.py:242
  28.2 0.4 collective-permute-start.7
  28.6 0.2 select_convert_fusion.3
  28.8 0.5 collective-permute-start.5
  29.3 2.5 %collective-permute-start.10 = (bf16[4,2,128,256]{3,2,1,0:T(8,128)(2,1)S(1)}, bf16[4,2,128,256]{3,2,1,0:T(8,128)(2,1)S(1)}, u32[]{:S(2)}, u32[]{:S(2)}) collective-permute-start(bf16[4,2,128,256]{3,2,1,0:T(8,128)(2,1)S(1)} %pad_maximum_fusion.q0), channel_id=1, source_target_pairs={{24,0},{97,1},{26,2},{99,3},{28,4},{101,5},{30,6},{103,7},{16,8},{... | collective-permute-start | bytes 1572872 | tf_op jit(solution)/shard_map/ppermute | solution.py:249
  31.7 0.2 collective-permute-done.9.q1
  31.9 1.7 %collective-permute-done.7 = f16[2,136,256]{2,1,0:T(8,128)(2,1)S(1)} collective-permute-done((f16[2,136,256]{2,1,0:T(8,128)(2,1)S(1)}, f16[2,136,256]{2,1,0:T(8,128)(2,1)S(1)}, u32[]{:S(2)}, u32[]{:S(2)}) %collective-permute-start.7) | collective-permute-done | bytes 139296 | tf_op jit(solution)/shard_map/ppermute | solution.py:242
  33.6 3.3 %collective-permute-start.11 = (bf16[4,2,128,256]{3,2,1,0:T(8,128)(2,1)S(1)}, bf16[4,2,128,256]{3,2,1,0:T(8,128)(2,1)S(1)}, u32[]{:S(2)}, u32[]{:S(2)}) collective-permute-start(bf16[4,2,128,256]{3,2,1,0:T(8,128)(2,1)S(1)} %collective-permute-done.9.q1), channel_id=1, source_target_pairs={{24,0},{97,1},{26,2},{99,3},{28,4},{101,5},{30,6},{103,7},{16,8},{... | collective-permute-start | bytes 1572872 | tf_op jit(solution)/shard_map/ppermute | solution.py:249
  37.0 0.5 select_convert_fusion
  37.5 0.7 %collective-permute-start.14 = (f16[2,136,256]{2,1,0:T(8,128)(2,1)S(1)}, f16[2,136,256]{2,1,0:T(8,128)(2,1)S(1)}, u32[]{:S(2)}, u32[]{:S(2)}) collective-permute-start(f16[2,136,256]{2,1,0:T(8,128)(2,1)S(1)} %get-tuple-element.35), channel_id=1, source_target_pairs={{0,6},{1,7},{2,4},{3,5},{4,2},{5,3},{6,0},{7,1},{8,14},{9,15},{10,... | collective-permute-start | bytes 417800 | tf_op jit(solution)/shard_map/ppermute | solution.py:254
  38.2 1.0 %collective-permute-start.13 = (f16[2,136,256]{2,1,0:T(8,128)(2,1)S(1)}, f16[2,136,256]{2,1,0:T(8,128)(2,1)S(1)}, u32[]{:S(2)}, u32[]{:S(2)}) collective-permute-start(f16[2,136,256]{2,1,0:T(8,128)(2,1)S(1)} %get-tuple-element.35), channel_id=1, source_target_pairs={{0,4},{1,5},{2,6},{3,7},{4,0},{5,1},{6,2},{7,3},{8,12},{9,13},{10,... | collective-permute-start | bytes 417800 | tf_op jit(solution)/shard_map/ppermute | solution.py:254
  39.2 1.6 %collective-permute-start.12 = (f16[2,136,256]{2,1,0:T(8,128)(2,1)S(1)}, f16[2,136,256]{2,1,0:T(8,128)(2,1)S(1)}, u32[]{:S(2)}, u32[]{:S(2)}) collective-permute-start(f16[2,136,256]{2,1,0:T(8,128)(2,1)S(1)} %get-tuple-element.35), channel_id=1, source_target_pairs={{0,2},{1,3},{2,0},{3,1},{4,6},{5,7},{6,4},{7,5},{8,10},{9,11},{10,... | collective-permute-start | bytes 417800 | tf_op jit(solution)/shard_map/ppermute | solution.py:254
  40.9 3.6 %collective-permute-done.11.q2 = bf16[4,2,128,256]{3,2,1,0:T(8,128)(2,1)S(1)} collective-permute-done((bf16[4,2,128,256]{3,2,1,0:T(8,128)(2,1)S(1)}, bf16[4,2,128,256]{3,2,1,0:T(8,128)(2,1)S(1)}, u32[]{:S(2)}, u32[]{:S(2)}) %collective-permute-start.11) | collective-permute-done | bytes 524320 | tf_op jit(solution)/shard_map/ppermute | solution.py:249
  44.4 0.7 %own_score.1.own = f32[128,256]{1,0:T(8,128)S(1)} custom-call(f32[2,128,256]{2,1,0:T(8,128)S(1)} %slice.200.s0, bf16[4,2,128,256]{3,2,1,0:T(8,128)(2,1)S(1)} %pad_maximum_fusion.q0, bf16[4,2,128,256]{3,2,1,0:T(8,128)(2,1)S(1)} %collective-permute-done.9.q1, bf16[4,2,128,256]{3,2,1,0:T(8,128)(2,1)S(1)} %collective-permute-done.10.q3, ...), custom_call_target="tpu_custom_call" | custom-call | flops 12000000000 | bytes 4194304 | tf_op jit(solution)/shard_map/own_score/pallas_call | solution.py:167
  45.3 0.3 exponential_multiply_fusion
  45.6 1.9 %score.1 = (f32[64,1024]{1,0:T(8,128)S(1)}, f32[64,1024]{1,0:T(8,128)S(1)}) custom-call(f32[128,256]{1,0:T(8,128)S(1)} %own_score.1.own, f32[2,128,256]{2,1,0:T(8,128)S(1)} %get-tuple-element.79.s1, f32[2,128,256]{2,1,0:T(8,128)S(1)} %get-tuple-element.78.s2, f32[2,128,256]{2,1,0:T(8,128)S(1)} %get-tuple-element.77.s3, ...), custom_call_target="tpu_custom_call" | custom-call | flops 2147483648 | bytes 4194304 | tf_op jit(solution)/shard_map/score/pallas_call | solution.py:181
  47.5 4.9 %collective-permute-start.15 = (f32[64,1024]{1,0:T(8,128)S(1)}, f32[64,1024]{1,0:T(8,128)S(1)}, u32[]{:S(2)}, u32[]{:S(2)}) collective-permute-start(f32[64,1024]{1,0:T(8,128)S(1)} %get-tuple-element.34), channel_id=1, source_target_pairs={{0,1},{1,0},{2,3},{3,2},{4,5},{5,4},{6,7},{7,6},{8,9},{9,8},{10,11... | collective-permute-start | bytes 786440 | tf_op jit(solution)/shard_map/ppermute | solution.py:257
  52.3 1.2 %collective-permute-done.15 = f32[64,1024]{1,0:T(8,128)S(1)} collective-permute-done((f32[64,1024]{1,0:T(8,128)S(1)}, f32[64,1024]{1,0:T(8,128)S(1)}, u32[]{:S(2)}, u32[]{:S(2)}) %collective-permute-start.15) | collective-permute-done | bytes 262176 | tf_op jit(solution)/shard_map/ppermute | solution.py:257
  53.5 0.7 %add_bitcast_fusion = f32[1024,64]{0,1:T(8,128)} fusion(f32[64,1024]{1,0:T(8,128)S(1)} %get-tuple-element.33, f32[64,1024]{1,0:T(8,128)S(1)} %collective-permute-done.15), kind=kLoop, calls=%fused_computation.32 | loop fusion | flops 65536 | bytes 786432 | tf_op jit(solution)/shard_map/transpose | solution.py:257
  (60 shorter events, 0.5 us)
Async XLA Ops:
  0.0 12.3 %collective-permute-start = (bf16[4,64,256]{2,1,0:T(8,128)(2,1)}, bf16[4,64,256]{2,1,0:T(8,128)(2,1)S(1)}, u32[]{:S(2)}, u32[]{:S(2)}) collective-permute-start(bf16[4,64,256]{2,1,0:T(8,128)(2,1)} %param.9), channel_id=1, source_target_pairs={{0,1},{1,0},{2,3},{3,2},{4,5},{5,4},{6,7},{7,6},{8,9},{9,8},{10,11... | collective-permute-start | bytes 393224 | tf_op jit(solution)/shard_map/ppermute | solution.py:225
  3.6 8.6 %copy-start = (bf16[4,64,256]{2,1,0:T(8,128)(2,1)S(1)}, bf16[4,64,256]{2,1,0:T(8,128)(2,1)}, u32[]{:S(2)}) copy-start(bf16[4,64,256]{2,1,0:T(8,128)(2,1)} %param.9) | copy-start | bytes 393220
  12.3 5.2 %collective-permute-start.1 = (bf16[2,128,256]{2,1,0:T(8,128)(2,1)S(1)}, bf16[2,128,256]{2,1,0:T(8,128)(2,1)S(1)}, u32[]{:S(2)}, u32[]{:S(2)}) collective-permute-start(bf16[2,128,256]{2,1,0:T(8,128)(2,1)S(1)} %pad_maximum_fusion.1), channel_id=1, source_target_pairs={{32,0},{9,1},{34,2},{11,3},{36,4},{13,5},{38,6},{15,7},{40,8},{1,9... | collective-permute-start | bytes 393224 | tf_op jit(solution)/shard_map/ppermute | solution.py:230
  14.1 7.1 %collective-permute-start.2 = (bf16[2,128,256]{2,1,0:T(8,128)(2,1)S(1)}, bf16[2,128,256]{2,1,0:T(8,128)(2,1)S(1)}, u32[]{:S(2)}, u32[]{:S(2)}) collective-permute-start(bf16[2,128,256]{2,1,0:T(8,128)(2,1)S(1)} %pad_maximum_fusion.1), channel_id=1, source_target_pairs={{64,0},{17,1},{66,2},{19,3},{68,4},{21,5},{70,6},{23,7},{72,8},{25... | collective-permute-start | bytes 393224 | tf_op jit(solution)/shard_map/ppermute | solution.py:230
  17.4 5.2 %collective-permute-start.3 = (bf16[2,128,256]{2,1,0:T(8,128)(2,1)S(1)}, bf16[2,128,256]{2,1,0:T(8,128)(2,1)S(1)}, u32[]{:S(2)}, u32[]{:S(2)}) collective-permute-start(bf16[2,128,256]{2,1,0:T(8,128)(2,1)S(1)} %pad_maximum_fusion.1), channel_id=1, source_target_pairs={{96,0},{25,1},{98,2},{27,3},{100,4},{29,5},{102,6},{31,7},{104,8},... | collective-permute-start | bytes 393224 | tf_op jit(solution)/shard_map/ppermute | solution.py:230
  22.7 2.1 %collective-permute-start.6 = (f32[2,2,136,256]{3,2,1,0:T(8,128)S(1)}, f32[2,2,136,256]{3,2,1,0:T(8,128)S(1)}, u32[]{:S(2)}, u32[]{:S(2)}) collective-permute-start(f32[2,2,136,256]{3,2,1,0:T(8,128)S(1)} %get-tuple-element.43), channel_id=1, source_target_pairs={{0,1},{1,0},{2,3},{3,2},{4,5},{5,4},{6,7},{7,6},{8,9},{9,8},{10,11... | collective-permute-start | bytes 1671176 | tf_op jit(solution)/shard_map/ppermute | solution.py:235
  23.2 4.9 %collective-permute-start.4 = (f32[2,2,136,256]{3,2,1,0:T(8,128)S(1)}, f32[2,2,136,256]{3,2,1,0:T(8,128)S(1)}, u32[]{:S(2)}, u32[]{:S(2)}) collective-permute-start(f32[2,2,136,256]{3,2,1,0:T(8,128)S(1)} %get-tuple-element.44), channel_id=1, source_target_pairs={{0,1},{1,0},{2,3},{3,2},{4,5},{5,4},{6,7},{7,6},{8,9},{9,8},{10,11... | collective-permute-start | bytes 1671176 | tf_op jit(solution)/shard_map/ppermute | solution.py:234
  23.5 8.4 %collective-permute-start.9 = (bf16[4,2,128,256]{3,2,1,0:T(8,128)(2,1)S(1)}, bf16[4,2,128,256]{3,2,1,0:T(8,128)(2,1)S(1)}, u32[]{:S(2)}, u32[]{:S(2)}) collective-permute-start(bf16[4,2,128,256]{3,2,1,0:T(8,128)(2,1)S(1)} %pad_maximum_fusion.q0), channel_id=1, source_target_pairs={{8,0},{33,1},{10,2},{35,3},{12,4},{37,5},{14,6},{39,7},{0,8},{41,9... | collective-permute-start | bytes 1572872 | tf_op jit(solution)/shard_map/ppermute | solution.py:243
  25.3 11.7 %collective-permute-start.8 = (f16[2,136,256]{2,1,0:T(8,128)(2,1)S(1)}, f16[2,136,256]{2,1,0:T(8,128)(2,1)S(1)}, u32[]{:S(2)}, u32[]{:S(2)}) collective-permute-start(f16[2,136,256]{2,1,0:T(8,128)(2,1)S(1)} %get-tuple-element.38), channel_id=1, source_target_pairs={{0,6},{1,7},{2,4},{3,5},{4,2},{5,3},{6,0},{7,1},{8,14},{9,15},{10,... | collective-permute-start | bytes 417800 | tf_op jit(solution)/shard_map/ppermute | solution.py:242
  28.2 5.5 %collective-permute-start.7 = (f16[2,136,256]{2,1,0:T(8,128)(2,1)S(1)}, f16[2,136,256]{2,1,0:T(8,128)(2,1)S(1)}, u32[]{:S(2)}, u32[]{:S(2)}) collective-permute-start(f16[2,136,256]{2,1,0:T(8,128)(2,1)S(1)} %get-tuple-element.37), channel_id=1, source_target_pairs={{0,4},{1,5},{2,6},{3,7},{4,0},{5,1},{6,2},{7,3},{8,12},{9,13},{10,... | collective-permute-start | bytes 417800 | tf_op jit(solution)/shard_map/ppermute | solution.py:242
  28.8 8.2 %collective-permute-start.5 = (f16[2,136,256]{2,1,0:T(8,128)(2,1)S(1)}, f16[2,136,256]{2,1,0:T(8,128)(2,1)S(1)}, u32[]{:S(2)}, u32[]{:S(2)}) collective-permute-start(f16[2,136,256]{2,1,0:T(8,128)(2,1)S(1)} %select_convert_fusion.3), channel_id=1, source_target_pairs={{0,2},{1,3},{2,0},{3,1},{4,6},{5,7},{6,4},{7,5},{8,10},{9,11},{10,... | collective-permute-start | bytes 417800 | tf_op jit(solution)/shard_map/ppermute | solution.py:242
  29.3 11.6 %collective-permute-start.10 = (bf16[4,2,128,256]{3,2,1,0:T(8,128)(2,1)S(1)}, bf16[4,2,128,256]{3,2,1,0:T(8,128)(2,1)S(1)}, u32[]{:S(2)}, u32[]{:S(2)}) collective-permute-start(bf16[4,2,128,256]{3,2,1,0:T(8,128)(2,1)S(1)} %pad_maximum_fusion.q0), channel_id=1, source_target_pairs={{24,0},{97,1},{26,2},{99,3},{28,4},{101,5},{30,6},{103,7},{16,8},{... | collective-permute-start | bytes 1572872 | tf_op jit(solution)/shard_map/ppermute | solution.py:249
  33.6 10.8 %collective-permute-start.11 = (bf16[4,2,128,256]{3,2,1,0:T(8,128)(2,1)S(1)}, bf16[4,2,128,256]{3,2,1,0:T(8,128)(2,1)S(1)}, u32[]{:S(2)}, u32[]{:S(2)}) collective-permute-start(bf16[4,2,128,256]{3,2,1,0:T(8,128)(2,1)S(1)} %collective-permute-done.9.q1), channel_id=1, source_target_pairs={{24,0},{97,1},{26,2},{99,3},{28,4},{101,5},{30,6},{103,7},{16,8},{... | collective-permute-start | bytes 1572872 | tf_op jit(solution)/shard_map/ppermute | solution.py:249
  37.5 7.7 %collective-permute-start.14 = (f16[2,136,256]{2,1,0:T(8,128)(2,1)S(1)}, f16[2,136,256]{2,1,0:T(8,128)(2,1)S(1)}, u32[]{:S(2)}, u32[]{:S(2)}) collective-permute-start(f16[2,136,256]{2,1,0:T(8,128)(2,1)S(1)} %get-tuple-element.35), channel_id=1, source_target_pairs={{0,6},{1,7},{2,4},{3,5},{4,2},{5,3},{6,0},{7,1},{8,14},{9,15},{10,... | collective-permute-start | bytes 417800 | tf_op jit(solution)/shard_map/ppermute | solution.py:254
  38.2 7.0 %collective-permute-start.13 = (f16[2,136,256]{2,1,0:T(8,128)(2,1)S(1)}, f16[2,136,256]{2,1,0:T(8,128)(2,1)S(1)}, u32[]{:S(2)}, u32[]{:S(2)}) collective-permute-start(f16[2,136,256]{2,1,0:T(8,128)(2,1)S(1)} %get-tuple-element.35), channel_id=1, source_target_pairs={{0,4},{1,5},{2,6},{3,7},{4,0},{5,1},{6,2},{7,3},{8,12},{9,13},{10,... | collective-permute-start | bytes 417800 | tf_op jit(solution)/shard_map/ppermute | solution.py:254
  39.2 6.0 %collective-permute-start.12 = (f16[2,136,256]{2,1,0:T(8,128)(2,1)S(1)}, f16[2,136,256]{2,1,0:T(8,128)(2,1)S(1)}, u32[]{:S(2)}, u32[]{:S(2)}) collective-permute-start(f16[2,136,256]{2,1,0:T(8,128)(2,1)S(1)} %get-tuple-element.35), channel_id=1, source_target_pairs={{0,2},{1,3},{2,0},{3,1},{4,6},{5,7},{6,4},{7,5},{8,10},{9,11},{10,... | collective-permute-start | bytes 417800 | tf_op jit(solution)/shard_map/ppermute | solution.py:254
  47.5 6.0 %collective-permute-start.15 = (f32[64,1024]{1,0:T(8,128)S(1)}, f32[64,1024]{1,0:T(8,128)S(1)}, u32[]{:S(2)}, u32[]{:S(2)}) collective-permute-start(f32[64,1024]{1,0:T(8,128)S(1)} %get-tuple-element.34), channel_id=1, source_target_pairs={{0,1},{1,0},{2,3},{3,2},{4,5},{5,4},{6,7},{7,6},{8,9},{9,8},{10,11... | collective-permute-start | bytes 786440 | tf_op jit(solution)/shard_map/ppermute | solution.py:257
